TPU v7x, 32 devices: a whole 2x2x4 slice. The times are simulated.
32 devices in a mesh: gx: 4 (over y, x), gy: 4 (over z), mem: 2 (over core).
Axes of the slice: x: 2, y: 2, z: 4, core: 2. Of those that a mesh axis runs over, the one named last changes fastest.
Arguments:
- src_hist: bfloat16 [4, 128, 512, 128], P('mem', 'gx', 'gy'), may hold values from -6 to 6
- rec_p: float32 [128, 512, 128], P('gx', 'gy'), may hold values from -6 to 6
- rec_q: float32 [128, 512, 128], P('gx', 'gy'), may hold values from -6 to 6
- prev_p: float32 [128, 512, 128], P('gx', 'gy'), may hold values from -6 to 6
- prev_q: float32 [128, 512, 128], P('gx', 'gy'), may hold values from -6 to 6
- horiz: float32 [128, 512, 128], P('gx', 'gy'), may hold values from 0.04 to 0.12
- vert: float32 [128, 512, 128], P('gx', 'gy'), may hold values from 0.04 to 0.12
- ratio: float32 [128, 512, 128], P('gx', 'gy'), may hold values from 0.6 to 1
- tilt: float32 [128, 512, 128], P('gx', 'gy'), may hold values from -0.4 to 0.4
- rec_pos: int32 [1024], replicated, may hold values from 0 to 8388607
- rec_data: float32 [4, 1024], replicated, may hold values from -6 to 6
- lag_offs: int32 [2, 2], P('mem'), may hold values from -8 to 8, as said below
Outputs:
- image: float32 [2, 128, 512, 128], P('mem', 'gx', 'gy')
- out_p: float32 [128, 512, 128], P('gx', 'gy')
- out_q: float32 [128, 512, 128], P('gx', 'gy')
Inputs may be any that keep to these rules, and one draw needn't show every extreme that they name: `lag_offs`: each offset lies within -8 .. 8; the offset pair (8, -8) occurs in every draw.
All inputs are finite; a program needn't handle non-finite values.
Results may differ from a plain program's by a relative error of at most 0.0003.
Values may be sent and summed in bfloat16 or wider, within the bound.
No kernel may reach another device: no remote copies, remote signals or barrier semaphores. Data moves between devices by JAX's collectives and lax.ppermute only.
A program may use at most 128 MiB of HBM per device.

v0:
```python
import jax
import jax.numpy as jnp
from jax import lax
from jax.sharding import PartitionSpec as P

NT = 4
HMAX = 8


def with_halo(cells, sides, width):
    for axis, dim in sides:
        count = lax.axis_size(axis)
        ends = count - 1
        head = lax.slice_in_dim(cells, 0, width, axis=dim)
        tail = lax.slice_in_dim(cells, cells.shape[dim] - width, cells.shape[dim], axis=dim)
        cells = jnp.concatenate(
            [
                lax.ppermute(tail, axis, [(i, (i + 1) % count) for i in range(ends)]),
                cells,
                lax.ppermute(head, axis, [((i + 1) % count, i) for i in range(ends)]),
            ],
            axis=dim,
        )
    return cells


def advance(p, q, old_p, old_q, wide_p, wide_q, horiz, vert, ratio, tilt):
    lateral = wide_p[2:, 1:-1] + wide_p[:-2, 1:-1] + wide_p[1:-1, 2:] + wide_p[1:-1, :-2] - 4.0 * p
    deep = jnp.pad(wide_q[:, 1:-1], ((0, 0), (0, 0), (1, 1)))
    center = deep[1:-1]
    second = center[:, :, 2:] + center[:, :, :-2] - 2.0 * q
    mixed = 0.25 * (deep[2:, :, 2:] - deep[2:, :, :-2] - deep[:-2, :, 2:] + deep[:-2, :, :-2])
    horizontal = horiz * lateral
    upright = vert * (second + tilt * mixed)
    new_p = 2.0 * p - old_p + horizontal + upright
    new_q = 2.0 * q - old_q + ratio * horizontal + upright
    return (new_p, new_q)


def body(
    src_hist, rec_p, rec_q, prev_p, prev_q, horiz, vert, ratio, tilt, rec_pos, rec_data, lag_offs
):
    shape = rec_p.shape
    width_x, width_y, depth = shape
    cells = width_x * width_y * depth
    start_x = lax.axis_index("gx") * width_x
    start_y = lax.axis_index("gy") * width_y
    plane = width_y * lax.axis_size("gy") * depth
    glob_x = rec_pos // plane
    rest = rec_pos % plane
    glob_y = rest // depth
    glob_z = rest % depth
    local_x = glob_x - start_x
    local_y = glob_y - start_y
    inside = (local_x >= 0) & (local_x < width_x) & (local_y >= 0) & (local_y < width_y)
    target = jnp.where(inside, local_x * (width_y * depth) + local_y * depth + glob_z, cells)
    history = lax.all_gather(src_hist, "mem", axis=0, tiled=True)

    def snapshot_at(t):
        snap = lax.dynamic_index_in_dim(history, t, 0, keepdims=False)
        return with_halo(snap, (("gx", 0), ("gy", 1)), HMAX)

    fields = jnp.stack([rec_p, rec_q])
    older = jnp.stack([prev_p, prev_q])
    image = jnp.zeros((lag_offs.shape[0],) + shape, jnp.float32)

    def advance_step(k, carry):
        fields, older, image = carry
        t = NT - 1 - k
        wide_s = snapshot_at(t)
        current = fields[0]

        def one_lag(offset):
            piece = lax.dynamic_slice(
                wide_s, (HMAX - offset[0], HMAX - offset[1], jnp.int32(0)), shape
            )
            return piece.astype(jnp.float32) * current

        image = image + jax.vmap(one_lag)(lag_offs)
        wide = with_halo(fields, (("gx", 1), ("gy", 2)), 1)
        new_p, new_q = advance(
            fields[0], fields[1], older[0], older[1], wide[0], wide[1], horiz, vert, ratio, tilt
        )
        amount = lax.dynamic_index_in_dim(rec_data, t, 0, keepdims=False)
        new_p = new_p.reshape(-1).at[target].add(amount, mode="drop").reshape(shape)
        new_q = new_q.reshape(-1).at[target].add(amount, mode="drop").reshape(shape)
        return (jnp.stack([new_p, new_q]), fields, image)

    fields, older, image = lax.fori_loop(0, NT, advance_step, (fields, older, image))
    return (image, fields[0], fields[1])


def solution(mesh):
    placed = (
        P("mem", "gx", "gy", None),
        P("gx", "gy", None),
        P("gx", "gy", None),
        P("gx", "gy", None),
        P("gx", "gy", None),
        P("gx", "gy", None),
        P("gx", "gy", None),
        P("gx", "gy", None),
        P("gx", "gy", None),
        P(),
        P(),
        P("mem", None),
    )
    return jax.shard_map(
        body,
        mesh=mesh,
        in_specs=placed,
        out_specs=(P("mem", "gx", "gy", None), P("gx", "gy", None), P("gx", "gy", None)),
        check_vma=False,
    )
```

profile of v0, /device:TPU:0, one launch (start us, length us, event | category | flops | bytes accessed | tf_op | source)
XLA Modules:
  0.0 360.7 jit_solution(14253578611384786499)
XLA Ops:
  11.3 7.1 %pad_maximum_fusion.5 = (f32[2,32,128,128]{3,2,1,0:T(8,128)}, f32[2,32,128,128]{3,2,1,0:T(8,128)}) fusion(f32[1,32,128,128]{3,2,1,0:T(8,128)S(1)} %bitcast.91, f32[1,32,128,128]{3,2,1,0:T(8,128)} %bitcast.92, f32[1,32,128,128]{3,2,1,0:T(8,128)} %bitcast.93, f32[1,32,128,128]{3,2,1,0:T(8,128)} %bitcast.94), kind=kLoop, calls=%fused_computation.55 | loop fusion | flops 2097152 | bytes 16777216 | tf_op jit(solution)/shard_map/stack | solution.py:63
  18.4 7.6 %all-gather.2.cloned.1.call-done = bf16[4,32,128,128]{3,2,1,0:T(8,128)(2,1)} async-done(((bf16[2,32,128,128]{3,2,1,0:T(8,128)(2,1)}), bf16[4,32,128,128]{3,2,1,0:T(8,128)(2,1)}) %all-gather.2.cloned.1.call-update) | async-done | bytes 4194320 | tf_op jit(solution)/shard_map/all_gather | solution.py:57
  26.0 323.1 %while.21 = (s32[]{:T(128)}, f32[2,32,128,128]{3,2,1,0:T(8,128)}, f32[2,32,128,128]{3,2,1,0:T(8,128)}, f32[1,32,128,128]{3,2,1,0:T(8,128)}, f32[32,128,128]{2,1,...) while((s32[]{:T(128)}, f32[2,32,128,128]{3,2,1,0:T(8,128)}, ...), condition=%wide.region_3.4_spmd.clone, body=%wide.region_0.3_spmd.clone.sunk | while | flops 24353800 | bytes 151216752 | solution.py:89
  35.1 5.9 %collective-permute-start.5 = (bf16[8,128,128]{2,1,0:T(8,128)(2,1)}, bf16[8,128,128]{2,1,0:T(8,128)(2,1)}, u32[]{:S(2)}, u32[]{:S(2)}) collective-permute-start(bf16[8,128,128]{2,1,0:T(8,128)(2,1)} %get-tuple-element.500), channel_id=1, source_target_pairs={{0,8},{8,16},{16,24},{1,9},{9,17},{17,25},{2,10},{10,18},{18,26},{... | collective-permute-start | bytes 786440 | tf_op jit(solution)/shard_map/while/body/eval_jaxpr/ppermute | solution.py:18
  48.9 4.5 %collective-permute-start.3 = (f32[2,34,1,128]{3,2,1,0:T(1,128)S(1)}, f32[2,34,1,128]{3,2,1,0:T(1,128)S(1)}, u32[]{:S(2)}, u32[]{:S(2)}) collective-permute-start(f32[2,34,1,128]{3,2,1,0:T(1,128)S(1)} %get-tuple-element.491), channel_id=1, source_target_pairs={{0,2},{2,4},{4,6},{1,3},{3,5},{5,7},{8,10},{10,12},{12,14},{9,11},... | collective-permute-start | bytes 104456 | tf_op jit(solution)/shard_map/while/body/eval_jaxpr/ppermute | solution.py:18
  60.3 7.0 %fusion.40 = (f32[32,128,128]{2,1,0:T(8,128)S(1)}, f32[32,128,128]{2,1,0:T(8,128)S(1)}, f32[32,128,128]{2,1,0:T(8,128)}) fusion(f32[2,32,128,128]{3,2,1,0:T(8,128)} %get-tuple-element.522, f32[2,32,128,128]{3,2,1,0:T(8,128)S(1)} %copy-done, f32[32,128,128]{2,1,0:T(8,128)} %get-tuple-element.541, f32[34,130,128]{2,1,0:T(8,128)S(1)} %get-tuple-element.492, ...), kind=kLoop, calls=%fused_computation.32.clone.1 | loop fusion | flops 10485760 | bytes 29491200 | tf_op jit(solution)/shard_map/while/body/eval_jaxpr/add | solution.py:35
  74.2 5.3 %fusion.41 = f32[32,128,128]{2,1,0:T(8,128)} fusion(f32[32,128,128]{2,1,0:T(8,128)} %get-tuple-element.494, f32[32,128,128]{2,1,0:T(8,128)} %get-tuple-element.546, f32[32,128,128]{2,1,0:T(8,128)S(1)} %get-tuple-element.495, f32[2,32,128,128]{3,2,1,0:T(8,128)} %get-tuple-element.522, f32[2,32,128,128]{3,2,1,0:T(8,128)S(1)} %copy-done), kind=kLoop, calls=%fused_computation.30.clone.1 | loop fusion | flops 2621440 | bytes 12582912 | tf_op jit(solution)/shard_map/while/body/eval_jaxpr/add | solution.py:36
  81.5 8.3 %scatter_fusion = f32[524288]{0:T(1024)} fusion(f32[524288]{0:T(1024)} %bitcast.89, s32[1024]{0:T(1024)S(1)} %bitcast.95, f32[1024]{0:T(1024)S(1)} %bitcast.97), kind=kCustom, calls=%fused_computation.1.clone.clone.1 | custom fusion | flops 1024 | bytes 16384 | tf_op jit(solution)/shard_map/while/body/eval_jaxpr/scatter-add | solution.py:86
  89.8 6.8 %scatter_fusion.1 = f32[524288]{0:T(1024)S(1)} fusion(f32[524288]{0:T(1024)S(1)} %bitcast.87, s32[1024]{0:T(1024)S(1)} %bitcast.96, f32[1024]{0:T(1024)S(1)} %bitcast.98), kind=kCustom, calls=%fused_computation.clone.clone.1 | custom fusion | flops 1024 | bytes 16384 | tf_op jit(solution)/shard_map/while/body/eval_jaxpr/scatter-add | solution.py:85
  96.7 6.5 %fusion.43 = f32[1,32,128,128]{3,2,1,0:T(8,128)} fusion(f32[1,32,128,128]{3,2,1,0:T(8,128)} %get-tuple-element.523, f32[2,32,128,128]{3,2,1,0:T(8,128)} %get-tuple-element.521, s32[]{:T(128)} %bitcast.85, s32[]{:T(128)} %bitcast.86, bf16[48,8,128]{2,1,0:T(8,128)(2,1)S(1)} %collective-permute-done.6, bf16[8,128,128]{2,1,0:T(8,128)(2,1)} %collective-permute-done.5, ...), kind=kLoop, calls=%fused_computation.27.clone.1 | loop fusion | flops 7340032 | bytes 8060937 | tf_op jit(solution)/shard_map/while/body/eval_jaxpr/add | solution.py:79
  115.0 5.9 %collective-permute-start.5 = (bf16[8,128,128]{2,1,0:T(8,128)(2,1)}, bf16[8,128,128]{2,1,0:T(8,128)(2,1)}, u32[]{:S(2)}, u32[]{:S(2)}) collective-permute-start(bf16[8,128,128]{2,1,0:T(8,128)(2,1)} %get-tuple-element.500), channel_id=1, source_target_pairs={{0,8},{8,16},{16,24},{1,9},{9,17},{17,25},{2,10},{10,18},{18,26},{... | collective-permute-start | bytes 786440 | tf_op jit(solution)/shard_map/while/body/eval_jaxpr/ppermute | solution.py:18
  128.8 5.2 %collective-permute-start.3 = (f32[2,34,1,128]{3,2,1,0:T(1,128)S(1)}, f32[2,34,1,128]{3,2,1,0:T(1,128)S(1)}, u32[]{:S(2)}, u32[]{:S(2)}) collective-permute-start(f32[2,34,1,128]{3,2,1,0:T(1,128)S(1)} %get-tuple-element.491), channel_id=1, source_target_pairs={{0,2},{2,4},{4,6},{1,3},{3,5},{5,7},{8,10},{10,12},{12,14},{9,11},... | collective-permute-start | bytes 104456 | tf_op jit(solution)/shard_map/while/body/eval_jaxpr/ppermute | solution.py:18
  140.9 7.0 %fusion.40 = (f32[32,128,128]{2,1,0:T(8,128)S(1)}, f32[32,128,128]{2,1,0:T(8,128)S(1)}, f32[32,128,128]{2,1,0:T(8,128)}) fusion(f32[2,32,128,128]{3,2,1,0:T(8,128)} %get-tuple-element.522, f32[2,32,128,128]{3,2,1,0:T(8,128)S(1)} %copy-done, f32[32,128,128]{2,1,0:T(8,128)} %get-tuple-element.541, f32[34,130,128]{2,1,0:T(8,128)S(1)} %get-tuple-element.492, ...), kind=kLoop, calls=%fused_computation.32.clone.1 | loop fusion | flops 10485760 | bytes 29491200 | tf_op jit(solution)/shard_map/while/body/eval_jaxpr/add | solution.py:35
  154.8 5.3 %fusion.41 = f32[32,128,128]{2,1,0:T(8,128)} fusion(f32[32,128,128]{2,1,0:T(8,128)} %get-tuple-element.494, f32[32,128,128]{2,1,0:T(8,128)} %get-tuple-element.546, f32[32,128,128]{2,1,0:T(8,128)S(1)} %get-tuple-element.495, f32[2,32,128,128]{3,2,1,0:T(8,128)} %get-tuple-element.522, f32[2,32,128,128]{3,2,1,0:T(8,128)S(1)} %copy-done), kind=kLoop, calls=%fused_computation.30.clone.1 | loop fusion | flops 2621440 | bytes 12582912 | tf_op jit(solution)/shard_map/while/body/eval_jaxpr/add | solution.py:36
  162.1 8.3 %scatter_fusion = f32[524288]{0:T(1024)} fusion(f32[524288]{0:T(1024)} %bitcast.89, s32[1024]{0:T(1024)S(1)} %bitcast.95, f32[1024]{0:T(1024)S(1)} %bitcast.97), kind=kCustom, calls=%fused_computation.1.clone.clone.1 | custom fusion | flops 1024 | bytes 16384 | tf_op jit(solution)/shard_map/while/body/eval_jaxpr/scatter-add | solution.py:86
  170.4 6.8 %scatter_fusion.1 = f32[524288]{0:T(1024)S(1)} fusion(f32[524288]{0:T(1024)S(1)} %bitcast.87, s32[1024]{0:T(1024)S(1)} %bitcast.96, f32[1024]{0:T(1024)S(1)} %bitcast.98), kind=kCustom, calls=%fused_computation.clone.clone.1 | custom fusion | flops 1024 | bytes 16384 | tf_op jit(solution)/shard_map/while/body/eval_jaxpr/scatter-add | solution.py:85
  177.3 7.1 %fusion.43 = f32[1,32,128,128]{3,2,1,0:T(8,128)} fusion(f32[1,32,128,128]{3,2,1,0:T(8,128)} %get-tuple-element.523, f32[2,32,128,128]{3,2,1,0:T(8,128)} %get-tuple-element.521, s32[]{:T(128)} %bitcast.85, s32[]{:T(128)} %bitcast.86, bf16[48,8,128]{2,1,0:T(8,128)(2,1)S(1)} %collective-permute-done.6, bf16[8,128,128]{2,1,0:T(8,128)(2,1)} %collective-permute-done.5, ...), kind=kLoop, calls=%fused_computation.27.clone.1 | loop fusion | flops 7340032 | bytes 8060937 | tf_op jit(solution)/shard_map/while/body/eval_jaxpr/add | solution.py:79
  196.3 5.9 %collective-permute-start.5 = (bf16[8,128,128]{2,1,0:T(8,128)(2,1)}, bf16[8,128,128]{2,1,0:T(8,128)(2,1)}, u32[]{:S(2)}, u32[]{:S(2)}) collective-permute-start(bf16[8,128,128]{2,1,0:T(8,128)(2,1)} %get-tuple-element.500), channel_id=1, source_target_pairs={{0,8},{8,16},{16,24},{1,9},{9,17},{17,25},{2,10},{10,18},{18,26},{... | collective-permute-start | bytes 786440 | tf_op jit(solution)/shard_map/while/body/eval_jaxpr/ppermute | solution.py:18
  210.1 5.2 %collective-permute-start.3 = (f32[2,34,1,128]{3,2,1,0:T(1,128)S(1)}, f32[2,34,1,128]{3,2,1,0:T(1,128)S(1)}, u32[]{:S(2)}, u32[]{:S(2)}) collective-permute-start(f32[2,34,1,128]{3,2,1,0:T(1,128)S(1)} %get-tuple-element.491), channel_id=1, source_target_pairs={{0,2},{2,4},{4,6},{1,3},{3,5},{5,7},{8,10},{10,12},{12,14},{9,11},... | collective-permute-start | bytes 104456 | tf_op jit(solution)/shard_map/while/body/eval_jaxpr/ppermute | solution.py:18
  222.1 7.0 %fusion.40 = (f32[32,128,128]{2,1,0:T(8,128)S(1)}, f32[32,128,128]{2,1,0:T(8,128)S(1)}, f32[32,128,128]{2,1,0:T(8,128)}) fusion(f32[2,32,128,128]{3,2,1,0:T(8,128)} %get-tuple-element.522, f32[2,32,128,128]{3,2,1,0:T(8,128)S(1)} %copy-done, f32[32,128,128]{2,1,0:T(8,128)} %get-tuple-element.541, f32[34,130,128]{2,1,0:T(8,128)S(1)} %get-tuple-element.492, ...), kind=kLoop, calls=%fused_computation.32.clone.1 | loop fusion | flops 10485760 | bytes 29491200 | tf_op jit(solution)/shard_map/while/body/eval_jaxpr/add | solution.py:35
  236.1 5.3 %fusion.41 = f32[32,128,128]{2,1,0:T(8,128)} fusion(f32[32,128,128]{2,1,0:T(8,128)} %get-tuple-element.494, f32[32,128,128]{2,1,0:T(8,128)} %get-tuple-element.546, f32[32,128,128]{2,1,0:T(8,128)S(1)} %get-tuple-element.495, f32[2,32,128,128]{3,2,1,0:T(8,128)} %get-tuple-element.522, f32[2,32,128,128]{3,2,1,0:T(8,128)S(1)} %copy-done), kind=kLoop, calls=%fused_computation.30.clone.1 | loop fusion | flops 2621440 | bytes 12582912 | tf_op jit(solution)/shard_map/while/body/eval_jaxpr/add | solution.py:36
  243.3 8.3 %scatter_fusion = f32[524288]{0:T(1024)} fusion(f32[524288]{0:T(1024)} %bitcast.89, s32[1024]{0:T(1024)S(1)} %bitcast.95, f32[1024]{0:T(1024)S(1)} %bitcast.97), kind=kCustom, calls=%fused_computation.1.clone.clone.1 | custom fusion | flops 1024 | bytes 16384 | tf_op jit(solution)/shard_map/while/body/eval_jaxpr/scatter-add | solution.py:86
  251.6 6.8 %scatter_fusion.1 = f32[524288]{0:T(1024)S(1)} fusion(f32[524288]{0:T(1024)S(1)} %bitcast.87, s32[1024]{0:T(1024)S(1)} %bitcast.96, f32[1024]{0:T(1024)S(1)} %bitcast.98), kind=kCustom, calls=%fused_computation.clone.clone.1 | custom fusion | flops 1024 | bytes 16384 | tf_op jit(solution)/shard_map/while/body/eval_jaxpr/scatter-add | solution.py:85
  258.5 7.1 %fusion.43 = f32[1,32,128,128]{3,2,1,0:T(8,128)} fusion(f32[1,32,128,128]{3,2,1,0:T(8,128)} %get-tuple-element.523, f32[2,32,128,128]{3,2,1,0:T(8,128)} %get-tuple-element.521, s32[]{:T(128)} %bitcast.85, s32[]{:T(128)} %bitcast.86, bf16[48,8,128]{2,1,0:T(8,128)(2,1)S(1)} %collective-permute-done.6, bf16[8,128,128]{2,1,0:T(8,128)(2,1)} %collective-permute-done.5, ...), kind=kLoop, calls=%fused_computation.27.clone.1 | loop fusion | flops 7340032 | bytes 8060937 | tf_op jit(solution)/shard_map/while/body/eval_jaxpr/add | solution.py:79
  277.5 5.9 %collective-permute-start.5 = (bf16[8,128,128]{2,1,0:T(8,128)(2,1)}, bf16[8,128,128]{2,1,0:T(8,128)(2,1)}, u32[]{:S(2)}, u32[]{:S(2)}) collective-permute-start(bf16[8,128,128]{2,1,0:T(8,128)(2,1)} %get-tuple-element.500), channel_id=1, source_target_pairs={{0,8},{8,16},{16,24},{1,9},{9,17},{17,25},{2,10},{10,18},{18,26},{... | collective-permute-start | bytes 786440 | tf_op jit(solution)/shard_map/while/body/eval_jaxpr/ppermute | solution.py:18
  291.3 5.2 %collective-permute-start.3 = (f32[2,34,1,128]{3,2,1,0:T(1,128)S(1)}, f32[2,34,1,128]{3,2,1,0:T(1,128)S(1)}, u32[]{:S(2)}, u32[]{:S(2)}) collective-permute-start(f32[2,34,1,128]{3,2,1,0:T(1,128)S(1)} %get-tuple-element.491), channel_id=1, source_target_pairs={{0,2},{2,4},{4,6},{1,3},{3,5},{5,7},{8,10},{10,12},{12,14},{9,11},... | collective-permute-start | bytes 104456 | tf_op jit(solution)/shard_map/while/body/eval_jaxpr/ppermute | solution.py:18
  303.3 7.0 %fusion.40 = (f32[32,128,128]{2,1,0:T(8,128)S(1)}, f32[32,128,128]{2,1,0:T(8,128)S(1)}, f32[32,128,128]{2,1,0:T(8,128)}) fusion(f32[2,32,128,128]{3,2,1,0:T(8,128)} %get-tuple-element.522, f32[2,32,128,128]{3,2,1,0:T(8,128)S(1)} %copy-done, f32[32,128,128]{2,1,0:T(8,128)} %get-tuple-element.541, f32[34,130,128]{2,1,0:T(8,128)S(1)} %get-tuple-element.492, ...), kind=kLoop, calls=%fused_computation.32.clone.1 | loop fusion | flops 10485760 | bytes 29491200 | tf_op jit(solution)/shard_map/while/body/eval_jaxpr/add | solution.py:35
  317.3 5.3 %fusion.41 = f32[32,128,128]{2,1,0:T(8,128)} fusion(f32[32,128,128]{2,1,0:T(8,128)} %get-tuple-element.494, f32[32,128,128]{2,1,0:T(8,128)} %get-tuple-element.546, f32[32,128,128]{2,1,0:T(8,128)S(1)} %get-tuple-element.495, f32[2,32,128,128]{3,2,1,0:T(8,128)} %get-tuple-element.522, f32[2,32,128,128]{3,2,1,0:T(8,128)S(1)} %copy-done), kind=kLoop, calls=%fused_computation.30.clone.1 | loop fusion | flops 2621440 | bytes 12582912 | tf_op jit(solution)/shard_map/while/body/eval_jaxpr/add | solution.py:36
  324.5 8.3 %scatter_fusion = f32[524288]{0:T(1024)} fusion(f32[524288]{0:T(1024)} %bitcast.89, s32[1024]{0:T(1024)S(1)} %bitcast.95, f32[1024]{0:T(1024)S(1)} %bitcast.97), kind=kCustom, calls=%fused_computation.1.clone.clone.1 | custom fusion | flops 1024 | bytes 16384 | tf_op jit(solution)/shard_map/while/body/eval_jaxpr/scatter-add | solution.py:86
  332.9 6.8 %scatter_fusion.1 = f32[524288]{0:T(1024)S(1)} fusion(f32[524288]{0:T(1024)S(1)} %bitcast.87, s32[1024]{0:T(1024)S(1)} %bitcast.96, f32[1024]{0:T(1024)S(1)} %bitcast.98), kind=kCustom, calls=%fused_computation.clone.clone.1 | custom fusion | flops 1024 | bytes 16384 | tf_op jit(solution)/shard_map/while/body/eval_jaxpr/scatter-add | solution.py:85
  339.7 7.1 %fusion.43 = f32[1,32,128,128]{3,2,1,0:T(8,128)} fusion(f32[1,32,128,128]{3,2,1,0:T(8,128)} %get-tuple-element.523, f32[2,32,128,128]{3,2,1,0:T(8,128)} %get-tuple-element.521, s32[]{:T(128)} %bitcast.85, s32[]{:T(128)} %bitcast.86, bf16[48,8,128]{2,1,0:T(8,128)(2,1)S(1)} %collective-permute-done.6, bf16[8,128,128]{2,1,0:T(8,128)(2,1)} %collective-permute-done.5, ...), kind=kLoop, calls=%fused_computation.27.clone.1 | loop fusion | flops 7340032 | bytes 8060937 | tf_op jit(solution)/shard_map/while/body/eval_jaxpr/add | solution.py:79
  349.1 4.7 %slice_bitcast_fusion.2 = (f32[32,128,128]{2,1,0:T(8,128)}, f32[32,128,128]{2,1,0:T(8,128)}) fusion(f32[2,32,128,128]{3,2,1,0:T(8,128)} %get-tuple-element.304), kind=kLoop, calls=%fused_computation.57 | loop fusion | bytes 8388608 | tf_op jit(solution)/shard_map/squeeze | solution.py:90
  (156 shorter events, 142.4 us)
Async XLA Ops:
  7.2 18.8 %all-gather.2.cloned.1.call-start = ((), (), s32[]{:S(2)}) async-start(), calls=%async_computation | async-start | bytes 6291456 | tf_op jit(solution)/shard_map/all_gather | solution.py:57
  27.0 16.0 %collective-permute-start = (f32[2,1,128,128]{3,2,1,0:T(8,128)S(1)}, f32[2,1,128,128]{3,2,1,0:T(8,128)S(1)}, u32[]{:S(2)}, u32[]{:S(2)}) collective-permute-start(f32[2,1,128,128]{3,2,1,0:T(8,128)S(1)} %get-tuple-element.488), channel_id=1, source_target_pairs={{0,8},{8,16},{16,24},{1,9},{9,17},{17,25},{2,10},{10,18},{18,26},{... | collective-permute-start | bytes 393224 | tf_op jit(solution)/shard_map/while/body/eval_jaxpr/ppermute | solution.py:18
  30.6 14.8 %collective-permute-start.1 = (f32[2,1,128,128]{3,2,1,0:T(8,128)S(1)}, f32[2,1,128,128]{3,2,1,0:T(8,128)S(1)}, u32[]{:S(2)}, u32[]{:S(2)}) collective-permute-start(f32[2,1,128,128]{3,2,1,0:T(8,128)S(1)} %get-tuple-element.489), channel_id=1, source_target_pairs={{8,0},{16,8},{24,16},{9,1},{17,9},{25,17},{10,2},{18,10},{26,18},{... | collective-permute-start | bytes 393224 | tf_op jit(solution)/shard_map/while/body/eval_jaxpr/ppermute | solution.py:20
  33.8 33.5 %collective-permute-start.4 = (bf16[8,128,128]{2,1,0:T(8,128)(2,1)}, bf16[8,128,128]{2,1,0:T(8,128)(2,1)S(1)}, u32[]{:S(2)}, u32[]{:S(2)}) collective-permute-start(bf16[8,128,128]{2,1,0:T(8,128)(2,1)} %get-tuple-element.499), channel_id=1, source_target_pairs={{8,0},{16,8},{24,16},{9,1},{17,9},{25,17},{10,2},{18,10},{26,18},{... | collective-permute-start | bytes 786440 | tf_op jit(solution)/shard_map/while/body/eval_jaxpr/ppermute | solution.py:20
  35.1 32.2 %collective-permute-start.5 = (bf16[8,128,128]{2,1,0:T(8,128)(2,1)}, bf16[8,128,128]{2,1,0:T(8,128)(2,1)}, u32[]{:S(2)}, u32[]{:S(2)}) collective-permute-start(bf16[8,128,128]{2,1,0:T(8,128)(2,1)} %get-tuple-element.500), channel_id=1, source_target_pairs={{0,8},{8,16},{16,24},{1,9},{9,17},{17,25},{2,10},{10,18},{18,26},{... | collective-permute-start | bytes 786440 | tf_op jit(solution)/shard_map/while/body/eval_jaxpr/ppermute | solution.py:18
  47.6 6.6 %collective-permute-start.2 = (f32[2,34,1,128]{3,2,1,0:T(1,128)S(1)}, f32[2,34,1,128]{3,2,1,0:T(1,128)S(1)}, u32[]{:S(2)}, u32[]{:S(2)}) collective-permute-start(f32[2,34,1,128]{3,2,1,0:T(1,128)S(1)} %get-tuple-element.490), channel_id=1, source_target_pairs={{2,0},{4,2},{6,4},{3,1},{5,3},{7,5},{10,8},{12,10},{14,12},{11,9},... | collective-permute-start | bytes 104456 | tf_op jit(solution)/shard_map/while/body/eval_jaxpr/ppermute | solution.py:20
  68.7 27.9 %collective-permute-start.6 = (bf16[48,8,128]{2,1,0:T(8,128)(2,1)}, bf16[48,8,128]{2,1,0:T(8,128)(2,1)S(1)}, u32[]{:S(2)}, u32[]{:S(2)}) collective-permute-start(bf16[48,8,128]{2,1,0:T(8,128)(2,1)} %get-tuple-element.501), channel_id=1, source_target_pairs={{0,2},{2,4},{4,6},{1,3},{3,5},{5,7},{8,10},{10,12},{12,14},{9,11},... | collective-permute-start | bytes 294920 | tf_op jit(solution)/shard_map/while/body/eval_jaxpr/ppermute | solution.py:18
  72.9 23.7 %collective-permute-start.7 = (bf16[48,8,128]{2,1,0:T(8,128)(2,1)}, bf16[48,8,128]{2,1,0:T(8,128)(2,1)}, u32[]{:S(2)}, u32[]{:S(2)}) collective-permute-start(bf16[48,8,128]{2,1,0:T(8,128)(2,1)} %get-tuple-element.502), channel_id=1, source_target_pairs={{2,0},{4,2},{6,4},{3,1},{5,3},{7,5},{10,8},{12,10},{14,12},{11,9},... | collective-permute-start | bytes 294920 | tf_op jit(solution)/shard_map/while/body/eval_jaxpr/ppermute | solution.py:20
  106.4 16.5 %collective-permute-start = (f32[2,1,128,128]{3,2,1,0:T(8,128)S(1)}, f32[2,1,128,128]{3,2,1,0:T(8,128)S(1)}, u32[]{:S(2)}, u32[]{:S(2)}) collective-permute-start(f32[2,1,128,128]{3,2,1,0:T(8,128)S(1)} %get-tuple-element.488), channel_id=1, source_target_pairs={{0,8},{8,16},{16,24},{1,9},{9,17},{17,25},{2,10},{10,18},{18,26},{... | collective-permute-start | bytes 393224 | tf_op jit(solution)/shard_map/while/body/eval_jaxpr/ppermute | solution.py:18
  110.6 14.8 %collective-permute-start.1 = (f32[2,1,128,128]{3,2,1,0:T(8,128)S(1)}, f32[2,1,128,128]{3,2,1,0:T(8,128)S(1)}, u32[]{:S(2)}, u32[]{:S(2)}) collective-permute-start(f32[2,1,128,128]{3,2,1,0:T(8,128)S(1)} %get-tuple-element.489), channel_id=1, source_target_pairs={{8,0},{16,8},{24,16},{9,1},{17,9},{25,17},{10,2},{18,10},{26,18},{... | collective-permute-start | bytes 393224 | tf_op jit(solution)/shard_map/while/body/eval_jaxpr/ppermute | solution.py:20
  113.8 34.1 %collective-permute-start.4 = (bf16[8,128,128]{2,1,0:T(8,128)(2,1)}, bf16[8,128,128]{2,1,0:T(8,128)(2,1)S(1)}, u32[]{:S(2)}, u32[]{:S(2)}) collective-permute-start(bf16[8,128,128]{2,1,0:T(8,128)(2,1)} %get-tuple-element.499), channel_id=1, source_target_pairs={{8,0},{16,8},{24,16},{9,1},{17,9},{25,17},{10,2},{18,10},{26,18},{... | collective-permute-start | bytes 786440 | tf_op jit(solution)/shard_map/while/body/eval_jaxpr/ppermute | solution.py:20
  115.0 32.8 %collective-permute-start.5 = (bf16[8,128,128]{2,1,0:T(8,128)(2,1)}, bf16[8,128,128]{2,1,0:T(8,128)(2,1)}, u32[]{:S(2)}, u32[]{:S(2)}) collective-permute-start(bf16[8,128,128]{2,1,0:T(8,128)(2,1)} %get-tuple-element.500), channel_id=1, source_target_pairs={{0,8},{8,16},{16,24},{1,9},{9,17},{17,25},{2,10},{10,18},{18,26},{... | collective-permute-start | bytes 786440 | tf_op jit(solution)/shard_map/while/body/eval_jaxpr/ppermute | solution.py:18
  127.5 7.2 %collective-permute-start.2 = (f32[2,34,1,128]{3,2,1,0:T(1,128)S(1)}, f32[2,34,1,128]{3,2,1,0:T(1,128)S(1)}, u32[]{:S(2)}, u32[]{:S(2)}) collective-permute-start(f32[2,34,1,128]{3,2,1,0:T(1,128)S(1)} %get-tuple-element.490), channel_id=1, source_target_pairs={{2,0},{4,2},{6,4},{3,1},{5,3},{7,5},{10,8},{12,10},{14,12},{11,9},... | collective-permute-start | bytes 104456 | tf_op jit(solution)/shard_map/while/body/eval_jaxpr/ppermute | solution.py:20
  128.8 6.8 %collective-permute-start.3 = (f32[2,34,1,128]{3,2,1,0:T(1,128)S(1)}, f32[2,34,1,128]{3,2,1,0:T(1,128)S(1)}, u32[]{:S(2)}, u32[]{:S(2)}) collective-permute-start(f32[2,34,1,128]{3,2,1,0:T(1,128)S(1)} %get-tuple-element.491), channel_id=1, source_target_pairs={{0,2},{2,4},{4,6},{1,3},{3,5},{5,7},{8,10},{10,12},{12,14},{9,11},... | collective-permute-start | bytes 104456 | tf_op jit(solution)/shard_map/while/body/eval_jaxpr/ppermute | solution.py:18
  149.3 27.9 %collective-permute-start.6 = (bf16[48,8,128]{2,1,0:T(8,128)(2,1)}, bf16[48,8,128]{2,1,0:T(8,128)(2,1)S(1)}, u32[]{:S(2)}, u32[]{:S(2)}) collective-permute-start(bf16[48,8,128]{2,1,0:T(8,128)(2,1)} %get-tuple-element.501), channel_id=1, source_target_pairs={{0,2},{2,4},{4,6},{1,3},{3,5},{5,7},{8,10},{10,12},{12,14},{9,11},... | collective-permute-start | bytes 294920 | tf_op jit(solution)/shard_map/while/body/eval_jaxpr/ppermute | solution.py:18
  153.5 23.7 %collective-permute-start.7 = (bf16[48,8,128]{2,1,0:T(8,128)(2,1)}, bf16[48,8,128]{2,1,0:T(8,128)(2,1)}, u32[]{:S(2)}, u32[]{:S(2)}) collective-permute-start(bf16[48,8,128]{2,1,0:T(8,128)(2,1)} %get-tuple-element.502), channel_id=1, source_target_pairs={{2,0},{4,2},{6,4},{3,1},{5,3},{7,5},{10,8},{12,10},{14,12},{11,9},... | collective-permute-start | bytes 294920 | tf_op jit(solution)/shard_map/while/body/eval_jaxpr/ppermute | solution.py:20
  187.7 16.5 %collective-permute-start = (f32[2,1,128,128]{3,2,1,0:T(8,128)S(1)}, f32[2,1,128,128]{3,2,1,0:T(8,128)S(1)}, u32[]{:S(2)}, u32[]{:S(2)}) collective-permute-start(f32[2,1,128,128]{3,2,1,0:T(8,128)S(1)} %get-tuple-element.488), channel_id=1, source_target_pairs={{0,8},{8,16},{16,24},{1,9},{9,17},{17,25},{2,10},{10,18},{18,26},{... | collective-permute-start | bytes 393224 | tf_op jit(solution)/shard_map/while/body/eval_jaxpr/ppermute | solution.py:18
  191.8 14.8 %collective-permute-start.1 = (f32[2,1,128,128]{3,2,1,0:T(8,128)S(1)}, f32[2,1,128,128]{3,2,1,0:T(8,128)S(1)}, u32[]{:S(2)}, u32[]{:S(2)}) collective-permute-start(f32[2,1,128,128]{3,2,1,0:T(8,128)S(1)} %get-tuple-element.489), channel_id=1, source_target_pairs={{8,0},{16,8},{24,16},{9,1},{17,9},{25,17},{10,2},{18,10},{26,18},{... | collective-permute-start | bytes 393224 | tf_op jit(solution)/shard_map/while/body/eval_jaxpr/ppermute | solution.py:20
  195.0 34.1 %collective-permute-start.4 = (bf16[8,128,128]{2,1,0:T(8,128)(2,1)}, bf16[8,128,128]{2,1,0:T(8,128)(2,1)S(1)}, u32[]{:S(2)}, u32[]{:S(2)}) collective-permute-start(bf16[8,128,128]{2,1,0:T(8,128)(2,1)} %get-tuple-element.499), channel_id=1, source_target_pairs={{8,0},{16,8},{24,16},{9,1},{17,9},{25,17},{10,2},{18,10},{26,18},{... | collective-permute-start | bytes 786440 | tf_op jit(solution)/shard_map/while/body/eval_jaxpr/ppermute | solution.py:20
  196.3 32.8 %collective-permute-start.5 = (bf16[8,128,128]{2,1,0:T(8,128)(2,1)}, bf16[8,128,128]{2,1,0:T(8,128)(2,1)}, u32[]{:S(2)}, u32[]{:S(2)}) collective-permute-start(bf16[8,128,128]{2,1,0:T(8,128)(2,1)} %get-tuple-element.500), channel_id=1, source_target_pairs={{0,8},{8,16},{16,24},{1,9},{9,17},{17,25},{2,10},{10,18},{18,26},{... | collective-permute-start | bytes 786440 | tf_op jit(solution)/shard_map/while/body/eval_jaxpr/ppermute | solution.py:18
  208.8 7.2 %collective-permute-start.2 = (f32[2,34,1,128]{3,2,1,0:T(1,128)S(1)}, f32[2,34,1,128]{3,2,1,0:T(1,128)S(1)}, u32[]{:S(2)}, u32[]{:S(2)}) collective-permute-start(f32[2,34,1,128]{3,2,1,0:T(1,128)S(1)} %get-tuple-element.490), channel_id=1, source_target_pairs={{2,0},{4,2},{6,4},{3,1},{5,3},{7,5},{10,8},{12,10},{14,12},{11,9},... | collective-permute-start | bytes 104456 | tf_op jit(solution)/shard_map/while/body/eval_jaxpr/ppermute | solution.py:20
  210.1 6.8 %collective-permute-start.3 = (f32[2,34,1,128]{3,2,1,0:T(1,128)S(1)}, f32[2,34,1,128]{3,2,1,0:T(1,128)S(1)}, u32[]{:S(2)}, u32[]{:S(2)}) collective-permute-start(f32[2,34,1,128]{3,2,1,0:T(1,128)S(1)} %get-tuple-element.491), channel_id=1, source_target_pairs={{0,2},{2,4},{4,6},{1,3},{3,5},{5,7},{8,10},{10,12},{12,14},{9,11},... | collective-permute-start | bytes 104456 | tf_op jit(solution)/shard_map/while/body/eval_jaxpr/ppermute | solution.py:18
  230.5 27.9 %collective-permute-start.6 = (bf16[48,8,128]{2,1,0:T(8,128)(2,1)}, bf16[48,8,128]{2,1,0:T(8,128)(2,1)S(1)}, u32[]{:S(2)}, u32[]{:S(2)}) collective-permute-start(bf16[48,8,128]{2,1,0:T(8,128)(2,1)} %get-tuple-element.501), channel_id=1, source_target_pairs={{0,2},{2,4},{4,6},{1,3},{3,5},{5,7},{8,10},{10,12},{12,14},{9,11},... | collective-permute-start | bytes 294920 | tf_op jit(solution)/shard_map/while/body/eval_jaxpr/ppermute | solution.py:18
  234.8 23.7 %collective-permute-start.7 = (bf16[48,8,128]{2,1,0:T(8,128)(2,1)}, bf16[48,8,128]{2,1,0:T(8,128)(2,1)}, u32[]{:S(2)}, u32[]{:S(2)}) collective-permute-start(bf16[48,8,128]{2,1,0:T(8,128)(2,1)} %get-tuple-element.502), channel_id=1, source_target_pairs={{2,0},{4,2},{6,4},{3,1},{5,3},{7,5},{10,8},{12,10},{14,12},{11,9},... | collective-permute-start | bytes 294920 | tf_op jit(solution)/shard_map/while/body/eval_jaxpr/ppermute | solution.py:20
  268.9 16.5 %collective-permute-start = (f32[2,1,128,128]{3,2,1,0:T(8,128)S(1)}, f32[2,1,128,128]{3,2,1,0:T(8,128)S(1)}, u32[]{:S(2)}, u32[]{:S(2)}) collective-permute-start(f32[2,1,128,128]{3,2,1,0:T(8,128)S(1)} %get-tuple-element.488), channel_id=1, source_target_pairs={{0,8},{8,16},{16,24},{1,9},{9,17},{17,25},{2,10},{10,18},{18,26},{... | collective-permute-start | bytes 393224 | tf_op jit(solution)/shard_map/while/body/eval_jaxpr/ppermute | solution.py:18
  273.0 14.8 %collective-permute-start.1 = (f32[2,1,128,128]{3,2,1,0:T(8,128)S(1)}, f32[2,1,128,128]{3,2,1,0:T(8,128)S(1)}, u32[]{:S(2)}, u32[]{:S(2)}) collective-permute-start(f32[2,1,128,128]{3,2,1,0:T(8,128)S(1)} %get-tuple-element.489), channel_id=1, source_target_pairs={{8,0},{16,8},{24,16},{9,1},{17,9},{25,17},{10,2},{18,10},{26,18},{... | collective-permute-start | bytes 393224 | tf_op jit(solution)/shard_map/while/body/eval_jaxpr/ppermute | solution.py:20
  276.2 34.1 %collective-permute-start.4 = (bf16[8,128,128]{2,1,0:T(8,128)(2,1)}, bf16[8,128,128]{2,1,0:T(8,128)(2,1)S(1)}, u32[]{:S(2)}, u32[]{:S(2)}) collective-permute-start(bf16[8,128,128]{2,1,0:T(8,128)(2,1)} %get-tuple-element.499), channel_id=1, source_target_pairs={{8,0},{16,8},{24,16},{9,1},{17,9},{25,17},{10,2},{18,10},{26,18},{... | collective-permute-start | bytes 786440 | tf_op jit(solution)/shard_map/while/body/eval_jaxpr/ppermute | solution.py:20
  277.5 32.8 %collective-permute-start.5 = (bf16[8,128,128]{2,1,0:T(8,128)(2,1)}, bf16[8,128,128]{2,1,0:T(8,128)(2,1)}, u32[]{:S(2)}, u32[]{:S(2)}) collective-permute-start(bf16[8,128,128]{2,1,0:T(8,128)(2,1)} %get-tuple-element.500), channel_id=1, source_target_pairs={{0,8},{8,16},{16,24},{1,9},{9,17},{17,25},{2,10},{10,18},{18,26},{... | collective-permute-start | bytes 786440 | tf_op jit(solution)/shard_map/while/body/eval_jaxpr/ppermute | solution.py:18
  290.0 7.2 %collective-permute-start.2 = (f32[2,34,1,128]{3,2,1,0:T(1,128)S(1)}, f32[2,34,1,128]{3,2,1,0:T(1,128)S(1)}, u32[]{:S(2)}, u32[]{:S(2)}) collective-permute-start(f32[2,34,1,128]{3,2,1,0:T(1,128)S(1)} %get-tuple-element.490), channel_id=1, source_target_pairs={{2,0},{4,2},{6,4},{3,1},{5,3},{7,5},{10,8},{12,10},{14,12},{11,9},... | collective-permute-start | bytes 104456 | tf_op jit(solution)/shard_map/while/body/eval_jaxpr/ppermute | solution.py:20
  291.3 6.8 %collective-permute-start.3 = (f32[2,34,1,128]{3,2,1,0:T(1,128)S(1)}, f32[2,34,1,128]{3,2,1,0:T(1,128)S(1)}, u32[]{:S(2)}, u32[]{:S(2)}) collective-permute-start(f32[2,34,1,128]{3,2,1,0:T(1,128)S(1)} %get-tuple-element.491), channel_id=1, source_target_pairs={{0,2},{2,4},{4,6},{1,3},{3,5},{5,7},{8,10},{10,12},{12,14},{9,11},... | collective-permute-start | bytes 104456 | tf_op jit(solution)/shard_map/while/body/eval_jaxpr/ppermute | solution.py:18
  311.8 27.9 %collective-permute-start.6 = (bf16[48,8,128]{2,1,0:T(8,128)(2,1)}, bf16[48,8,128]{2,1,0:T(8,128)(2,1)S(1)}, u32[]{:S(2)}, u32[]{:S(2)}) collective-permute-start(bf16[48,8,128]{2,1,0:T(8,128)(2,1)} %get-tuple-element.501), channel_id=1, source_target_pairs={{0,2},{2,4},{4,6},{1,3},{3,5},{5,7},{8,10},{10,12},{12,14},{9,11},... | collective-permute-start | bytes 294920 | tf_op jit(solution)/shard_map/while/body/eval_jaxpr/ppermute | solution.py:18
  316.0 23.7 %collective-permute-start.7 = (bf16[48,8,128]{2,1,0:T(8,128)(2,1)}, bf16[48,8,128]{2,1,0:T(8,128)(2,1)}, u32[]{:S(2)}, u32[]{:S(2)}) collective-permute-start(bf16[48,8,128]{2,1,0:T(8,128)(2,1)} %get-tuple-element.502), channel_id=1, source_target_pairs={{2,0},{4,2},{6,4},{3,1},{5,3},{7,5},{10,8},{12,10},{14,12},{11,9},... | collective-permute-start | bytes 294920 | tf_op jit(solution)/shard_map/while/body/eval_jaxpr/ppermute | solution.py:20
  (16 other events, 60.0 us)
Sparse Core Ops, SparseCore 0:
  9.6 16.3 all-gather.1
where the time goes:
time: 365 us; the launch traced here: 361 us
  other arithmetic  171 us (47%)
  starting transfers between devices  97.2 us (27%)
  local copies, waits for them, and re-layouts  63.5 us (17%)
  between operations  16.7 us (5%)
  waiting for transfers between devices  11.8 us (3%)
    ppermute x16, starting transfers between devices, with_halo(): lax.ppermute(tail, axis, [(i, (i + 1) % count) for i in range(ends)])  76.5 us
    while x36, local copies, waits for them, and re-layouts  33.4 us
    scatter-add x4, other arithmetic, advance_step(): new_q = new_q.reshape(-1).at[target].add(amount, mode='drop').reshape(shape)  33.3 us
    add x4, other arithmetic, advance(): new_p = 2.0 * p - old_p + horizontal + upright  28 us
    add x4, other arithmetic, advance_step(): image = image + jax.vmap(one_lag)(lag_offs)  27.9 us
    scatter-add x4, other arithmetic, advance_step(): new_p = new_p.reshape(-1).at[target].add(amount, mode='drop').reshape(shape)  27.3 us
    add x4, other arithmetic, advance(): new_q = 2.0 * q - old_q + ratio * horizontal + upright  21.3 us
    ppermute x16, starting transfers between devices, with_halo(): lax.ppermute(head, axis, [((i + 1) % count, i) for i in range(ends)])  20.6 us
  transfers between devices with their start and end apart: 33, of which 5 were waited for; matrix products, arithmetic and copies ran while one was open for 46% of the time, Pallas kernels for 0%

commit v1 on v0

v1 whole, which is shorter than its diff:
```python
import functools

import jax
import jax.numpy as jnp
from jax import lax
from jax.experimental import pallas as pl
from jax.experimental.pallas import tpu as pltpu
from jax.sharding import PartitionSpec as P

NT = 4
HMAX = 8
DEEP = NT
ROW0 = 16
F32 = jnp.float32
BF16 = jnp.bfloat16
ANY = pl.BlockSpec(memory_space=pl.ANY)
SMEM = pl.BlockSpec(memory_space=pltpu.SMEM)
VMEM = pl.BlockSpec(memory_space=pltpu.VMEM)
DEPTHS = (DEEP, DEEP) + (DEEP - 1,) * 6
STARTS = tuple(sum(DEPTHS[:i]) for i in range(8))
LAYERS = sum(DEPTHS)


def params(mib):
    return pltpu.CompilerParams(vmem_limit_bytes=mib * 2**20)


def copy_all(pairs, sems):
    copies = [pltpu.make_async_copy(a, b, sems.at[i]) for i, (a, b) in enumerate(pairs)]
    for c in copies:
        c.start()
    return copies


def wait_all(copies):
    for c in copies:
        c.wait()


def pack_x_kernel(scal, *refs):
    fields, out, stage, sems = refs[:8], refs[8], refs[9], refs[10]
    core = scal[0]
    width = fields[0].shape[0]
    pairs = []
    for f, s, d in zip(fields, STARTS, DEPTHS):
        begin = jnp.where(core == 0, width - d, 0)
        pairs.append((f.at[pl.ds(begin, d)], stage.at[pl.ds(s, d)]))
    copies = copy_all(pairs, sems)
    for c, s, d in zip(copies, STARTS, DEPTHS):
        c.wait()
        out[s : s + d] = stage[s : s + d].astype(BF16)


def pack_x(scal, fields):
    shape = (LAYERS,) + fields[0].shape[1:]
    return pl.pallas_call(
        pack_x_kernel,
        out_shape=jax.ShapeDtypeStruct(shape, BF16),
        in_specs=[SMEM] + [ANY] * 8,
        out_specs=VMEM,
        scratch_shapes=[pltpu.VMEM(shape, F32), pltpu.SemaphoreType.DMA((8,))],
        compiler_params=params(16),
        name="pack_x",
    )(scal, *fields)


def pack_y_kernel(scal, *refs):
    fields, own, other, out, stage, snaps, mixed, sems = refs[:8], *refs[8:]
    core = scal[0]
    rows = fields[0].shape[1]
    start = pl.multiple_of(jnp.where(core == 0, rows - 8, 0), 8)
    wide = pl.multiple_of(jnp.where(core == 0, rows - 16, 0), 16)
    pairs = [(f.at[:, pl.ds(start, 8)], stage.at[i]) for i, f in enumerate(fields)]
    pairs.append((own.at[:, :, pl.ds(wide, 16)], snaps.at[core]))
    pairs.append((other.at[:, :, pl.ds(wide, 16)], snaps.at[1 - core]))
    copies = copy_all(pairs, sems)
    skip = jnp.where(core == 0, 4, 0)
    for slab in range(2):
        for i in range(4):
            f = 4 * slab + i
            copies[f].wait()
            mixed[:, 4 * i : 4 * i + 4, :] = stage[f, :, pl.ds(skip, 4), :]
        out[slab] = mixed[...].astype(BF16)
    wait_all(copies[8:])
    for pair in range(2):
        for i in range(2):
            both = snaps[pair, i].astype(F32)
            mixed[:, 8 * i : 8 * i + 8, :] = jnp.where(core == 0, both[:, 8:], both[:, :8])
        out[2 + pair] = mixed[...].astype(BF16)


def pack_y(scal, fields, own, other):
    width, _, depth = fields[0].shape
    return pl.pallas_call(
        pack_y_kernel,
        out_shape=jax.ShapeDtypeStruct((4, width, 16, depth), BF16),
        in_specs=[SMEM] + [ANY] * 10,
        out_specs=VMEM,
        scratch_shapes=[
            pltpu.VMEM((8, width, 8, depth), F32),
            pltpu.VMEM((2, 2, width, 16, depth), BF16),
            pltpu.VMEM((width, 16, depth), F32),
            pltpu.SemaphoreType.DMA((10,)),
        ],
        compiler_params=params(16),
        name="pack_y",
    )(scal, *fields, own, other)


def pack_corner_kernel(scal, y_own, y_other, own, other, xc, xs, sems):
    core = scal[0]
    width = own.shape[1]
    near = jnp.where(core == 0, width - DEEP, 0)
    far = jnp.where(core == 0, width - HMAX, 0)
    pairs = []
    for ref, side in ((y_own, core), (y_other, 1 - core)):
        pairs.append((ref.at[pl.ds(0, 2), pl.ds(near, DEEP)], xc.at[side]))
        for pair in range(2):
            for layer in range(HMAX):
                pairs.append(
                    (
                        ref.at[2 + pair, far + layer],
                        xs.at[NT * HMAX + 2 * side + pair, pl.ds(16 * layer, 16)],
                    )
                )
    for ref, half in ((own, core), (other, 1 - core)):
        for i in range(2):
            pairs.append(
                (ref.at[i, pl.ds(far, HMAX)], xs.at[pl.ds((2 * half + i) * HMAX, HMAX)])
            )
    wait_all(copy_all(pairs, sems))


def pack_corner(scal, y_own, y_other, own, other):
    _, width, rows, depth = own.shape
    return pl.pallas_call(
        pack_corner_kernel,
        out_shape=(
            jax.ShapeDtypeStruct((2, 2, DEEP, 16, depth), BF16),
            jax.ShapeDtypeStruct((NT * HMAX + 4, rows, depth), BF16),
        ),
        in_specs=[SMEM] + [ANY] * 4,
        out_specs=(ANY, ANY),
        scratch_shapes=[pltpu.SemaphoreType.DMA((2 + 4 * HMAX + 4,))],
        compiler_params=params(16),
        name="pack_corner",
    )(scal, y_own, y_other, own, other)


def pick_kernel(target, count, chosen, places):
    def one(r, n):
        place = target[r]
        chosen[n] = r
        places[n] = place
        return n + jnp.where(place >= 0, 1, 0)

    total = target.shape[0]
    count[0] = lax.fori_loop(0, total, one, jnp.int32(0), unroll=8)


def pick(target):
    n = target.shape[0]
    return pl.pallas_call(
        pick_kernel,
        out_shape=(
            jax.ShapeDtypeStruct((1,), jnp.int32),
            jax.ShapeDtypeStruct((n + 1,), jnp.int32),
            jax.ShapeDtypeStruct((n + 1,), jnp.int32),
        ),
        in_specs=[SMEM],
        out_specs=(SMEM, SMEM, SMEM),
        name="pick_receivers",
    )(target)


def wave_kernel(scal, count, chosen, places, data, *refs):
    fields = refs[:8]
    xw_own, xw_other, y_own, y_other, xc_own, xc_other = refs[8:14]
    p_outs, q_out = refs[14:18], refs[18]
    bufs = refs[19:27]
    s_xw, s_y, s_xc, stage, sem_in, sem_halo, sem_out = refs[27:]
    core = scal[0]
    width, rows, depth = fields[0].shape
    mid = (pl.ds(DEEP, width), pl.ds(ROW0, rows))
    mains = copy_all([(f, b.at[mid]) for f, b in zip(fields, bufs)], sem_in)
    halos = copy_all(
        [
            (xw_own, s_xw.at[core]),
            (xw_other, s_xw.at[1 - core]),
            (y_own.at[pl.ds(0, 2)], s_y.at[core]),
            (y_other.at[pl.ds(0, 2)], s_y.at[1 - core]),
            (xc_own, s_xc.at[core]),
            (xc_other, s_xc.at[1 - core]),
        ],
        sem_halo,
    )
    wait_all(halos)
    for side in range(2):
        for f in range(8):
            d = DEPTHS[f]
            to = DEEP - d if side == 0 else DEEP + width
            part = s_xw[side, STARTS[f] : STARTS[f] + d]
            bufs[f][to : to + d, ROW0 : ROW0 + rows, :] = part.astype(F32)
    for yside in range(2):
        to = ROW0 - DEEP if yside == 0 else ROW0 + rows
        for slab in range(2):
            stage[DEEP : DEEP + width] = s_y[yside, slab].astype(F32)
            for xside in range(2):
                at = 0 if xside == 0 else DEEP + width
                stage[at : at + DEEP] = s_xc[xside, yside, slab].astype(F32)
            for i in range(4):
                bufs[4 * slab + i][:, to : to + DEEP, :] = stage[:, 4 * i : 4 * i + 4, :]
    wait_all(mains)

    horiz, vert, ratio, tilt = bufs[4:]
    lane = lax.broadcasted_iota(jnp.int32, (16, depth), 1)
    first, last = lane == 0, lane == depth - 1
    thin = lax.broadcasted_iota(jnp.int32, (1, depth), 1)

    def up_z(v):
        return jnp.where(last, 0.0, pltpu.roll(v, depth - 1, 1))

    def down_z(v):
        return jnp.where(first, 0.0, pltpu.roll(v, 1, 1))

    def step(k, p, q, old_p, old_q):
        low, high = 1 + k, width + 2 * DEEP - 1 - k
        if k < NT - 1:
            begins = range(ROW0 - 8, ROW0 + rows + 8, 16)
        else:
            begins = range(ROW0, ROW0 + rows, 16)
        for r in begins:
            at = pl.ds(r, 16)

            def cell(x, carry, r=r, at=at):
                p_m, p_c, q_m, q_c = carry
                p_n, q_n = p[x + 1, at, :], q[x + 1, at, :]
                lateral = (p_m + p_n) + (p[x, pl.ds(r - 1, 16), :] + p[x, pl.ds(r + 1, 16), :]) - 4.0 * p_c
                slope = q_n - q_m
                second = (up_z(q_c) + down_z(q_c)) - 2.0 * q_c
                mixed = up_z(slope) - down_z(slope)
                horizontal = horiz[x, at, :] * lateral
                upright = vert[x, at, :] * (second + (0.25 * tilt[x, at, :]) * mixed)
                old_p[x, at, :] = (2.0 * p_c - old_p[x, at, :]) + (horizontal + upright)
                old_q[x, at, :] = (2.0 * q_c - old_q[x, at, :]) + (ratio[x, at, :] * horizontal + upright)
                return p_c, p_n, q_c, q_n

            init = (p[low - 1, at, :], p[low, at, :], q[low - 1, at, :], q[low, at, :])
            lax.fori_loop(low, high, cell, init, unroll=2)

        def inject(j, _):
            place = places[j]
            amount = data[NT - 1 - k, chosen[j]]
            x, y, z = place >> 16, (place >> 8) & 255, place & 255
            add = jnp.where(thin == z, amount, 0.0)
            old_p[x, pl.ds(y, 1), :] = old_p[x, pl.ds(y, 1), :] + add
            old_q[x, pl.ds(y, 1), :] = old_q[x, pl.ds(y, 1), :] + add
            return 0

        lax.fori_loop(0, count[0], inject, 0)

    p_now, q_now, p_old, q_old = bufs[:4]
    outs = []
    for k in range(NT):
        if k >= 2:
            outs[k - 2].wait()
        step(k, p_now, q_now, p_old, q_old)
        p_now, p_old, q_now, q_old = p_old, p_now, q_old, q_now
        outs.append(pltpu.make_async_copy(p_now.at[mid], p_outs[k], sem_out.at[k]))
        outs[-1].start()
    tail = pltpu.make_async_copy(q_now.at[mid], q_out, sem_out.at[NT])
    tail.start()
    wait_all(outs[NT - 2 :] + [tail])


def wave(scal, receivers, data, fields, halos):
    shape = fields[0].shape
    width, rows, depth = shape
    big = (width + 2 * DEEP, rows + 2 * ROW0, depth)
    return pl.pallas_call(
        wave_kernel,
        out_shape=(jax.ShapeDtypeStruct(shape, F32),) * 5,
        in_specs=[SMEM] * 5 + [ANY] * 14,
        out_specs=(ANY,) * 5,
        scratch_shapes=[pltpu.VMEM(big, F32)] * 8
        + [
            pltpu.VMEM((2, LAYERS, rows, depth), BF16),
            pltpu.VMEM((2, 2, width, 16, depth), BF16),
            pltpu.VMEM((2, 2, 2, DEEP, 16, depth), BF16),
            pltpu.VMEM((width + 2 * DEEP, 16, depth), F32),
            pltpu.SemaphoreType.DMA((8,)),
            pltpu.SemaphoreType.DMA((6,)),
            pltpu.SemaphoreType.DMA((5,)),
        ],
        compiler_params=params(48),
        name="wave",
    )(scal, *receivers, data, *fields, *halos)


def image_kernel(scal, own, other, y_own, y_other, xs_own, xs_other, *refs):
    ps, out = refs[:NT], refs[NT]
    snaps, strips, wide, sems = refs[NT + 1 :]
    core, off_x, off_y = scal[0], scal[1], scal[2]
    width, rows, depth = own.shape[1:]
    chunk = out.shape[0]
    step = pl.program_id(0)

    @pl.when(step == 0)
    def _():
        mains = [
            (own, snaps.at[pl.ds(2 * core, 2), pl.ds(HMAX, width)]),
            (other, snaps.at[pl.ds(2 - 2 * core, 2), pl.ds(HMAX, width)]),
        ]
        copies = copy_all(mains, sems)
        x_side = jnp.where(off_x > 0, 0, 1)
        y_side = jnp.where(off_y > 0, 0, 1)
        to = jnp.where(off_x > 0, 0, HMAX + width)

        def halo(xs):
            pairs = [
                (xs.at[pl.ds(t * HMAX, HMAX)], snaps.at[t, pl.ds(to, HMAX)]) for t in range(NT)
            ]
            for pair in range(2):
                for layer in range(HMAX):
                    pairs.append(
                        (
                            xs.at[NT * HMAX + 2 * y_side + pair, pl.ds(16 * layer, 16)],
                            strips.at[pair, to + layer],
                        )
                    )
            wait_all(copy_all(pairs, sems.at[pl.ds(3, 4 + 2 * HMAX)]))

        def edge(ref):
            pairs = [(ref.at[pl.ds(2, 2)], strips.at[:, pl.ds(HMAX, width)])]
            wait_all(copy_all(pairs, sems.at[pl.ds(2, 1)]))

        pl.when(x_side == core)(lambda: halo(xs_own))
        pl.when(x_side != core)(lambda: halo(xs_other))
        pl.when(y_side == core)(lambda: edge(y_own))
        pl.when(y_side != core)(lambda: edge(y_other))
        wait_all(copies)

    low = off_y > 0
    for i in range(chunk):
        x = step * chunk + i + HMAX - off_x
        total = None
        for pair in range(2):
            strip = strips[pair, x].astype(F32)
            for j in range(2):
                t = 2 * pair + j
                slot = t + NT * (i % 2)
                rim = strip[8 * j : 8 * j + 8]
                wide[slot, pl.ds(HMAX, rows), :] = snaps[t, x].astype(F32)
                wide[slot, pl.ds(0, HMAX), :] = rim
                wide[slot, pl.ds(HMAX + rows, HMAX), :] = rim
                term = wide[slot, pl.ds(HMAX - off_y, rows), :] * ps[NT - 1 - t][i]
                total = term if total is None else total + term
        out[i] = total


def image(scal, own, other, y_own, y_other, xs_own, xs_other, ps):
    shape = ps[0].shape
    width, rows, depth = shape
    chunk = 4
    block = pl.BlockSpec((chunk, rows, depth), lambda i: (i, 0, 0))
    return pl.pallas_call(
        image_kernel,
        grid=(width // chunk,),
        out_shape=jax.ShapeDtypeStruct(shape, F32),
        in_specs=[SMEM] + [ANY] * 6 + [block] * NT,
        out_specs=block,
        scratch_shapes=[
            pltpu.VMEM((NT, width + 2 * HMAX, rows, depth), BF16),
            pltpu.VMEM((2, width + 2 * HMAX, 16, depth), BF16),
            pltpu.VMEM((2 * NT, rows + 2 * HMAX, depth), F32),
            pltpu.SemaphoreType.DMA((3 + 4 + 2 * HMAX,)),
        ],
        compiler_params=params(32),
        name="image",
    )(scal, own, other, y_own, y_other, xs_own, xs_other, *ps)


def body(
    src_hist, rec_p, rec_q, prev_p, prev_q, horiz, vert, ratio, tilt, rec_pos, rec_data, lag_offs
):
    width, rows, depth = rec_p.shape
    core = lax.axis_index("mem")
    scal = jnp.concatenate([core[None].astype(jnp.int32), lag_offs[0]])
    fields = (rec_p, rec_q, prev_p, prev_q, horiz, vert, ratio, tilt)

    def swap(v):
        return lax.ppermute(v, "mem", [(0, 1), (1, 0)])

    def outward(v, axis):
        count = lax.axis_size(axis)
        up = [(2 * i, 2 * i + 2) for i in range(count - 1)]
        down = [(2 * i + 3, 2 * i + 1) for i in range(count - 1)]
        return lax.ppermute(v, (axis, "mem"), up + down)

    plane = rows * lax.axis_size("gy") * depth
    x = rec_pos // plane - lax.axis_index("gx") * width + DEEP
    rest = rec_pos % plane
    y = rest // depth - lax.axis_index("gy") * rows + ROW0
    z = rest % depth
    inside = (x >= 0) & (x < width + 2 * DEEP)
    inside &= (y >= ROW0 - DEEP) & (y < ROW0 + rows + DEEP)
    receivers = pick(jnp.where(inside, (x << 16) + (y << 8) + z, -1))

    other = swap(src_hist)
    xw = outward(pack_x(scal, fields), "gx")
    ys = outward(pack_y(scal, fields, src_hist, other), "gy")
    ys_other = swap(ys)
    xc, xs = pack_corner(scal, ys, ys_other, src_hist, other)
    xc = outward(xc, "gx")
    xs = outward(xs, "gx")
    halos = (xw, swap(xw), ys, ys_other, xc, swap(xc))
    p1, p2, p3, p4, q4 = wave(scal, receivers, rec_data, fields, halos)
    picture = image(scal, src_hist, other, ys, ys_other, xs, swap(xs), (rec_p, p1, p2, p3))
    return picture[None], p4, q4


def solution(mesh):
    block = P("gx", "gy", None)
    return jax.shard_map(
        body,
        mesh=mesh,
        in_specs=(P("mem", "gx", "gy", None),) + (block,) * 8 + (P(), P(), P("mem", None)),
        out_specs=(P("mem", "gx", "gy", None), block, block),
        check_vma=False,
    )
```

time: 365 us -> 181 us (0.50)
  other arithmetic: 171 us -> 1.34 us
  Pallas kernels: 0 us -> 85.6 us
  starting transfers between devices: 97.2 us -> 47.8 us
  local copies, waits for them, and re-layouts: 63.5 us -> 21.8 us
  between operations: 16.7 us -> 0.82 us
  waiting for transfers between devices: 11.8 us -> 20.8 us
    pallas_call x0 -> x6, Pallas kernels: none -> 85.6 us  [the longest x1 70.2 us: wave(): pl.pallas_call(wave_kernel, out_shape=(jax.ShapeDtypeStruct(shape, F32),)...]
    add x12 -> x0, other arithmetic: 77.2 us -> none  [the longest x4 28 us: advance(): new_p = 2.0 * p - old_p + horizontal + upright]
    scatter-add x8 -> x0, other arithmetic: 60.6 us -> none  [the longest x4 33.3 us: advance_step(): new_q = new_q.reshape(-1).at[target].add(amount, mode='drop').reshape(shape)]
    ppermute x32 -> x9, starting transfers between devices: 97.2 us -> 47.8 us  [the longest x5 29.6 us: swap(): return lax.ppermute(v, 'mem', [(0, 1), (1, 0)])]
    while x40 -> x0, local copies, waits for them, and re-layouts: 36 us -> none
    unnamed x6 -> x50, local copies, waits for them, and re-layouts: 0.01 us -> 21.8 us
    ppermute x32 -> x9, waiting for transfers between devices: 3.52 us -> 20.8 us  [the longest x4 15.6 us: outward(): return lax.ppermute(v, (axis, 'mem'), up + down)]
    another operation x5 -> x0, other arithmetic: 16.2 us -> none  [the longest x4 9.06 us: advance_step(): return (jnp.stack([new_p, new_q]), fields, image)]
  transfers between devices with their start and end apart: 33 -> 9, of which waited for: 5 -> 5; matrix products, arithmetic and copies ran while one was open for 46% -> 1% of each run, Pallas kernels for 0% -> 43%
where the time goes in v1:
time: 181 us; the launch traced here: 178 us
  Pallas kernels  85.6 us (47%)
  starting transfers between devices  47.8 us (26%)
  local copies, waits for them, and re-layouts  21.8 us (12%)
  waiting for transfers between devices  20.8 us (11%)
    pallas_call x1, Pallas kernels, wave(): pl.pallas_call(wave_kernel, out_shape=(jax.ShapeDtypeStruct(shape, F32),)...  70.2 us
    ppermute x5, starting transfers between devices, swap(): return lax.ppermute(v, 'mem', [(0, 1), (1, 0)])  29.6 us
    unnamed x50, local copies, waits for them, and re-layouts  21.8 us
    ppermute x4, starting transfers between devices, outward(): return lax.ppermute(v, (axis, 'mem'), up + down)  18.2 us
    ppermute x4, waiting for transfers between devices, outward(): return lax.ppermute(v, (axis, 'mem'), up + down)  15.6 us
    pallas_call x1, Pallas kernels, image(): pl.pallas_call(image_kernel, grid=(width // chunk,), out_shape=jax.ShapeD...  6.19 us
    ppermute x5, waiting for transfers between devices, swap(): return lax.ppermute(v, 'mem', [(0, 1), (1, 0)])  5.18 us
    pallas_call x1, Pallas kernels, pick(): pl.pallas_call(pick_kernel, out_shape=(jax.ShapeDtypeStruct((1,), jnp.int...  4.57 us
  transfers between devices with their start and end apart: 9, of which 5 were waited for; matrix products, arithmetic and copies ran while one was open for 1% of the time, Pallas kernels for 43%

profile of v1, /device:TPU:0, one launch (start us, length us, event | category | flops | bytes accessed | tf_op | source)
XLA Modules:
  0.0 178.1 jit_solution(9745211607386068070)
XLA Ops:
  1.1 0.7 pad_add_fusion.scal
  1.9 3.3 %collective-permute-done.refs_9_.other = bf16[2,32,128,128]{3,2,1,0:T(8,128)(2,1)S(1)} collective-permute-done((bf16[2,32,128,128]{3,2,1,0:T(8,128)(2,1)}, bf16[2,32,128,128]{3,2,1,0:T(8,128)(2,1)S(1)}, u32[]{:S(2)}, u32[]{:S(2)}) %collective-permute-start) | collective-permute-done | bytes 2097184 | tf_op jit(solution)/shard_map/ppermute | solution.py:392
  5.1 1.6 copy-done
  6.7 1.6 copy-done.3
  8.3 1.6 copy-done.5
  9.9 1.6 copy-done.7
  11.5 1.6 copy-done.9
  13.1 1.6 copy-done.10
  14.7 1.6 copy-done.11
  16.3 1.6 copy-done.12
  17.9 1.6 copy-done.13
  19.5 1.1 pack_y.1
  20.6 1.3 copy-done.16
  21.9 5.1 %collective-permute-start.1 = (bf16[4,32,16,128]{3,2,1,0:T(8,128)(2,1)S(1)}, bf16[4,32,16,128]{3,2,1,0:T(8,128)(2,1)S(1)}, u32[]{:S(2)}, u32[]{:S(2)}) collective-permute-start(bf16[4,32,16,128]{3,2,1,0:T(8,128)(2,1)S(1)} %pack_y.1), channel_id=1, source_target_pairs={{0,2},{2,4},{4,6},{3,1},{5,3},{7,5},{8,10},{10,12},{12,14},{11,9},... | collective-permute-start | bytes 1572872 | tf_op jit(solution)/shard_map/ppermute | solution.py:398
  27.0 6.6 %collective-permute-done.1.y_own.refs_10_ = bf16[4,32,16,128]{3,2,1,0:T(8,128)(2,1)S(1)} collective-permute-done((bf16[4,32,16,128]{3,2,1,0:T(8,128)(2,1)S(1)}, bf16[4,32,16,128]{3,2,1,0:T(8,128)(2,1)S(1)}, u32[]{:S(2)}, u32[]{:S(2)}) %collective-permute-start.1) | collective-permute-done | bytes 524320 | tf_op jit(solution)/shard_map/ppermute | solution.py:398
  33.7 1.9 %collective-permute-done.2.y_other.refs_11_ = bf16[4,32,16,128]{3,2,1,0:T(8,128)(2,1)S(1)} collective-permute-done((bf16[4,32,16,128]{3,2,1,0:T(8,128)(2,1)S(1)}, bf16[4,32,16,128]{3,2,1,0:T(8,128)(2,1)S(1)}, u32[]{:S(2)}, u32[]{:S(2)}) %collective-permute-start.2) | collective-permute-done | bytes 524320 | tf_op jit(solution)/shard_map/ppermute | solution.py:392
  35.6 1.6 copy-done.17
  37.2 1.3 pack_corner.1
  38.5 4.5 %collective-permute-start.3 = (bf16[36,128,128]{2,1,0:T(8,128)(2,1)S(1)}, bf16[36,128,128]{2,1,0:T(8,128)(2,1)}, u32[]{:S(2)}, u32[]{:S(2)}) collective-permute-start(bf16[36,128,128]{2,1,0:T(8,128)(2,1)S(1)} %get-tuple-element.13), channel_id=1, source_target_pairs={{0,8},{8,16},{16,24},{9,1},{17,9},{25,17},{2,10},{10,18},{18,26},{... | collective-permute-start | bytes 3538952 | tf_op jit(solution)/shard_map/ppermute | solution.py:398
  42.9 2.3 %pack_x.1 = bf16[26,128,128]{2,1,0:T(8,128)(2,1)S(1)} custom-call(s32[3]{0:T(128)S(1)} %pad_add_fusion.scal, f32[32,128,128]{2,1,0:T(8,128)S(1)} %copy-done.1, f32[32,128,128]{2,1,0:T(8,128)S(1)} %copy-done.4, f32[32,128,128]{2,1,0:T(8,128)S(1)} %copy-done.6, f32[32,128,128]{2,1,0:T(8,128)S(1)} %copy-done.8, f32[32,128,128]{2,1,0:T(8,128)S(1)} %copy-done.9, ...), custom_call_target="tpu_custom_call" | custom-call | tf_op jit(solution)/shard_map/pack_x/pallas_call | solution.py:56
  45.2 3.3 %collective-permute-start.5 = (bf16[26,128,128]{2,1,0:T(8,128)(2,1)S(1)}, bf16[26,128,128]{2,1,0:T(8,128)(2,1)}, u32[]{:S(2)}, u32[]{:S(2)}) collective-permute-start(bf16[26,128,128]{2,1,0:T(8,128)(2,1)S(1)} %pack_x.1), channel_id=1, source_target_pairs={{0,8},{8,16},{16,24},{9,1},{17,9},{25,17},{2,10},{10,18},{18,26},{... | collective-permute-start | bytes 2555912 | tf_op jit(solution)/shard_map/ppermute | solution.py:398
  48.5 7.0 %collective-permute-done.3.xs_own = bf16[36,128,128]{2,1,0:T(8,128)(2,1)} collective-permute-done((bf16[36,128,128]{2,1,0:T(8,128)(2,1)S(1)}, bf16[36,128,128]{2,1,0:T(8,128)(2,1)}, u32[]{:S(2)}, u32[]{:S(2)}) %collective-permute-start.3) | collective-permute-done | bytes 1179680 | tf_op jit(solution)/shard_map/ppermute | solution.py:398
  55.6 10.9 %collective-permute-start.4 = (bf16[36,128,128]{2,1,0:T(8,128)(2,1)}, bf16[36,128,128]{2,1,0:T(8,128)(2,1)S(1)}, u32[]{:S(2)}, u32[]{:S(2)}) collective-permute-start(bf16[36,128,128]{2,1,0:T(8,128)(2,1)} %collective-permute-done.3.xs_own), channel_id=1, source_target_pairs={{0,1},{1,0},{2,3},{3,2},{4,5},{5,4},{6,7},{7,6},{8,9},{9,8},{10,11... | collective-permute-start | bytes 3538952 | tf_op jit(solution)/shard_map/ppermute | solution.py:392
  66.5 18.3 %collective-permute-start.6 = (bf16[26,128,128]{2,1,0:T(8,128)(2,1)}, bf16[26,128,128]{2,1,0:T(8,128)(2,1)}, u32[]{:S(2)}, u32[]{:S(2)}) collective-permute-start(bf16[26,128,128]{2,1,0:T(8,128)(2,1)} %collective-permute-done.5.refs_8_), channel_id=1, source_target_pairs={{0,1},{1,0},{2,3},{3,2},{4,5},{5,4},{6,7},{7,6},{8,9},{9,8},{10,11... | collective-permute-start | bytes 2555912 | tf_op jit(solution)/shard_map/ppermute | solution.py:392
  84.7 5.3 %collective-permute-start.7 = (bf16[2,2,4,16,128]{4,3,2,1,0:T(8,128)(2,1)S(1)}, bf16[2,2,4,16,128]{4,3,2,1,0:T(8,128)(2,1)S(1)}, u32[]{:S(2)}, u32[]{:S(2)}) collective-permute-start(bf16[2,2,4,16,128]{4,3,2,1,0:T(8,128)(2,1)S(1)} %get-tuple-element.17), channel_id=1, source_target_pairs={{0,8},{8,16},{16,24},{9,1},{17,9},{25,17},{2,10},{10,18},{18,26},{... | collective-permute-start | bytes 196616 | tf_op jit(solution)/shard_map/ppermute | solution.py:398
  90.0 1.9 %collective-permute-done.7.refs_12_ = bf16[2,2,4,16,128]{4,3,2,1,0:T(8,128)(2,1)S(1)} collective-permute-done((bf16[2,2,4,16,128]{4,3,2,1,0:T(8,128)(2,1)S(1)}, bf16[2,2,4,16,128]{4,3,2,1,0:T(8,128)(2,1)S(1)}, u32[]{:S(2)}, u32[]{:S(2)}) %collective-permute-start.7) | collective-permute-done | bytes 65568 | tf_op jit(solution)/shard_map/ppermute | solution.py:398
  92.5 4.6 %pick_receivers.1 = (s32[1]{0:T(128)}, s32[1025]{0:T(1024)}, s32[1025]{0:T(1024)}) custom-call(s32[1024]{0:T(1024)} %fusion.5.target), custom_call_target="tpu_custom_call" | custom-call | tf_op jit(solution)/shard_map/pick_receivers/pallas_call | solution.py:163
  97.8 0.7 copy-done.23
  98.5 70.2 %wave.1 = (f32[32,128,128]{2,1,0:T(8,128)S(1)}, f32[32,128,128]{2,1,0:T(8,128)}, f32[32,128,128]{2,1,0:T(8,128)}, f32[32,128,128]{2,1,0:T(8,128)}, f32[32,128,128]{2,1,0:T(8,128)}) custom-call(s32[3]{0:T(128)S(1)} %pad_add_fusion.scal, s32[1]{0:T(128)} %get-tuple-element.14.count, s32[1025]{0:T(1024)S(1)} %copy-done.22, s32[1025]{0:T(1024)S(1)} %copy-done.23, ...), custom_call_target="tpu_custom_call" | custom-call | tf_op jit(solution)/shard_map/wave/pallas_call | solution.py:280
  168.8 1.6 copy-done.19
  170.4 1.6 copy-done.20
  171.9 6.2 %image.1 = f32[32,128,128]{2,1,0:T(8,128)} custom-call(s32[3]{0:T(128)S(1)} %pad_add_fusion.scal, bf16[2,32,128,128]{3,2,1,0:T(8,128)(2,1)S(1)} %copy-done.15, bf16[2,32,128,128]{3,2,1,0:T(8,128)(2,1)S(1)} %copy-done.18, bf16[4,32,16,128]{3,2,1,0:T(8,128)(2,1)S(1)} %collective-permute-done.1.y_own.refs_10_, ...), custom_call_target="tpu_custom_call" | custom-call | tf_op jit(solution)/shard_map/image/pallas_call | solution.py:366
  (44 shorter events, 1.9 us)
Async XLA Ops:
  0.6 4.5 %collective-permute-start = (bf16[2,32,128,128]{3,2,1,0:T(8,128)(2,1)}, bf16[2,32,128,128]{3,2,1,0:T(8,128)(2,1)S(1)}, u32[]{:S(2)}, u32[]{:S(2)}) collective-permute-start(bf16[2,32,128,128]{3,2,1,0:T(8,128)(2,1)} %own.3), channel_id=1, source_target_pairs={{0,1},{1,0},{2,3},{3,2},{4,5},{5,4},{6,7},{7,6},{8,9},{9,8},{10,11... | collective-permute-start | bytes 6291464 | tf_op jit(solution)/shard_map/ppermute | solution.py:392
  5.1 1.6 copy-start
  6.7 1.6 copy-start.3
  8.3 1.6 copy-start.5
  9.9 1.6 copy-start.7
  11.5 1.6 copy-start.9
  13.1 1.6 copy-start.10
  14.7 1.6 copy-start.11
  16.3 1.6 copy-start.12
  17.9 1.6 copy-start.13
  19.5 16.1 %copy-start.14 = (bf16[2,32,128,128]{3,2,1,0:T(8,128)(2,1)S(1)}, bf16[2,32,128,128]{3,2,1,0:T(8,128)(2,1)}, u32[]{:S(2)}) copy-start(bf16[2,32,128,128]{3,2,1,0:T(8,128)(2,1)} %own.3) | copy-start | bytes 6291460
  19.5 23.5 %copy-start.6 = (f32[32,128,128]{2,1,0:T(8,128)S(1)}, f32[32,128,128]{2,1,0:T(8,128)}, u32[]{:S(2)}) copy-start(f32[32,128,128]{2,1,0:T(8,128)} %refs_2_.5) | copy-start | bytes 6291460
  19.5 23.5 %copy-start.8 = (f32[32,128,128]{2,1,0:T(8,128)S(1)}, f32[32,128,128]{2,1,0:T(8,128)}, u32[]{:S(2)}) copy-start(f32[32,128,128]{2,1,0:T(8,128)} %refs_3_.5) | copy-start | bytes 6291460
  20.6 1.3 copy-start.16
  21.9 21.0 %copy-start.1 = (f32[32,128,128]{2,1,0:T(8,128)S(1)}, f32[32,128,128]{2,1,0:T(8,128)}, u32[]{:S(2)}) copy-start(f32[32,128,128]{2,1,0:T(8,128)} %refs_0_.7) | copy-start | bytes 6291460
  21.9 21.0 %copy-start.4 = (f32[32,128,128]{2,1,0:T(8,128)S(1)}, f32[32,128,128]{2,1,0:T(8,128)}, u32[]{:S(2)}) copy-start(f32[32,128,128]{2,1,0:T(8,128)} %refs_1_.5) | copy-start | bytes 6291460
  21.9 11.8 %collective-permute-start.1 = (bf16[4,32,16,128]{3,2,1,0:T(8,128)(2,1)S(1)}, bf16[4,32,16,128]{3,2,1,0:T(8,128)(2,1)S(1)}, u32[]{:S(2)}, u32[]{:S(2)}) collective-permute-start(bf16[4,32,16,128]{3,2,1,0:T(8,128)(2,1)S(1)} %pack_y.1), channel_id=1, source_target_pairs={{0,2},{2,4},{4,6},{3,1},{5,3},{7,5},{8,10},{10,12},{12,14},{11,9},... | collective-permute-start | bytes 1572872 | tf_op jit(solution)/shard_map/ppermute | solution.py:398
  33.7 1.9 %collective-permute-start.2 = (bf16[4,32,16,128]{3,2,1,0:T(8,128)(2,1)S(1)}, bf16[4,32,16,128]{3,2,1,0:T(8,128)(2,1)S(1)}, u32[]{:S(2)}, u32[]{:S(2)}) collective-permute-start(bf16[4,32,16,128]{3,2,1,0:T(8,128)(2,1)S(1)} %collective-permute-done.1.y_own.refs_10_), channel_id=1, source_target_pairs={{0,1},{1,0},{2,3},{3,2},{4,5},{5,4},{6,7},{7,6},{8,9},{9,8},{10,11... | collective-permute-start | bytes 1572872 | tf_op jit(solution)/shard_map/ppermute | solution.py:392
  35.6 1.6 copy-start.17
  38.5 53.4 %copy-start.24 = (s32[1024]{0:T(1024)S(1)}, s32[1024]{0:T(1024)}, u32[]{:S(2)}) copy-start(s32[1024]{0:T(1024)} %param.21) | copy-start | bytes 12292
  38.5 58.6 %copy-start.21 = (f32[4,1024]{1,0:T(4,128)S(1)}, f32[4,1024]{1,0:T(4,128)}, u32[]{:S(2)}) copy-start(f32[4,1024]{1,0:T(4,128)} %data.1) | copy-start | bytes 49156
  38.5 17.1 %collective-permute-start.3 = (bf16[36,128,128]{2,1,0:T(8,128)(2,1)S(1)}, bf16[36,128,128]{2,1,0:T(8,128)(2,1)}, u32[]{:S(2)}, u32[]{:S(2)}) collective-permute-start(bf16[36,128,128]{2,1,0:T(8,128)(2,1)S(1)} %get-tuple-element.13), channel_id=1, source_target_pairs={{0,8},{8,16},{16,24},{9,1},{17,9},{25,17},{2,10},{10,18},{18,26},{... | collective-permute-start | bytes 3538952 | tf_op jit(solution)/shard_map/ppermute | solution.py:398
  45.2 21.2 %collective-permute-start.5 = (bf16[26,128,128]{2,1,0:T(8,128)(2,1)S(1)}, bf16[26,128,128]{2,1,0:T(8,128)(2,1)}, u32[]{:S(2)}, u32[]{:S(2)}) collective-permute-start(bf16[26,128,128]{2,1,0:T(8,128)(2,1)S(1)} %pack_x.1), channel_id=1, source_target_pairs={{0,8},{8,16},{16,24},{9,1},{17,9},{25,17},{2,10},{10,18},{18,26},{... | collective-permute-start | bytes 2555912 | tf_op jit(solution)/shard_map/ppermute | solution.py:398
  55.6 113.1 %collective-permute-start.4 = (bf16[36,128,128]{2,1,0:T(8,128)(2,1)}, bf16[36,128,128]{2,1,0:T(8,128)(2,1)S(1)}, u32[]{:S(2)}, u32[]{:S(2)}) collective-permute-start(bf16[36,128,128]{2,1,0:T(8,128)(2,1)} %collective-permute-done.3.xs_own), channel_id=1, source_target_pairs={{0,1},{1,0},{2,3},{3,2},{4,5},{5,4},{6,7},{7,6},{8,9},{9,8},{10,11... | collective-permute-start | bytes 3538952 | tf_op jit(solution)/shard_map/ppermute | solution.py:392
  66.5 30.6 %collective-permute-start.6 = (bf16[26,128,128]{2,1,0:T(8,128)(2,1)}, bf16[26,128,128]{2,1,0:T(8,128)(2,1)}, u32[]{:S(2)}, u32[]{:S(2)}) collective-permute-start(bf16[26,128,128]{2,1,0:T(8,128)(2,1)} %collective-permute-done.5.refs_8_), channel_id=1, source_target_pairs={{0,1},{1,0},{2,3},{3,2},{4,5},{5,4},{6,7},{7,6},{8,9},{9,8},{10,11... | collective-permute-start | bytes 2555912 | tf_op jit(solution)/shard_map/ppermute | solution.py:392
  84.7 7.2 %collective-permute-start.7 = (bf16[2,2,4,16,128]{4,3,2,1,0:T(8,128)(2,1)S(1)}, bf16[2,2,4,16,128]{4,3,2,1,0:T(8,128)(2,1)S(1)}, u32[]{:S(2)}, u32[]{:S(2)}) collective-permute-start(bf16[2,2,4,16,128]{4,3,2,1,0:T(8,128)(2,1)S(1)} %get-tuple-element.17), channel_id=1, source_target_pairs={{0,8},{8,16},{16,24},{9,1},{17,9},{25,17},{2,10},{10,18},{18,26},{... | collective-permute-start | bytes 196616 | tf_op jit(solution)/shard_map/ppermute | solution.py:398
  91.9 5.2 %collective-permute-start.8 = (bf16[2,2,4,16,128]{4,3,2,1,0:T(8,128)(2,1)S(1)}, bf16[2,2,4,16,128]{4,3,2,1,0:T(8,128)(2,1)S(1)}, u32[]{:S(2)}, u32[]{:S(2)}) collective-permute-start(bf16[2,2,4,16,128]{4,3,2,1,0:T(8,128)(2,1)S(1)} %collective-permute-done.7.refs_12_), channel_id=1, source_target_pairs={{0,1},{1,0},{2,3},{3,2},{4,5},{5,4},{6,7},{7,6},{8,9},{9,8},{10,11... | collective-permute-start | bytes 196616 | tf_op jit(solution)/shard_map/ppermute | solution.py:392
  98.5 70.2 %copy-start.2 = (f32[32,128,128]{2,1,0:T(8,128)S(1)}, f32[32,128,128]{2,1,0:T(8,128)}, u32[]{:S(2)}) copy-start(f32[32,128,128]{2,1,0:T(8,128)} %refs_0_.7) | copy-start | bytes 6291460
  98.5 70.2 %copy-start.15 = (bf16[2,32,128,128]{3,2,1,0:T(8,128)(2,1)S(1)}, bf16[2,32,128,128]{3,2,1,0:T(8,128)(2,1)}, u32[]{:S(2)}) copy-start(bf16[2,32,128,128]{3,2,1,0:T(8,128)(2,1)} %own.3) | copy-start | bytes 6291460
  98.5 70.2 %copy-start.18 = (bf16[2,32,128,128]{3,2,1,0:T(8,128)(2,1)S(1)}, bf16[2,32,128,128]{3,2,1,0:T(8,128)(2,1)}, u32[]{:S(2)}) copy-start(bf16[2,32,128,128]{3,2,1,0:T(8,128)(2,1)} %copy-done.16) | copy-start | bytes 6291460
  168.8 1.6 copy-start.19
  170.3 1.6 copy-start.20
  (2 other events, 1.4 us)

commit v2 on v0

v2 whole, which is shorter than its diff:
```python
import functools

import jax
import jax.numpy as jnp
from jax import lax
from jax.experimental import pallas as pl
from jax.experimental.pallas import tpu as pltpu
from jax.sharding import PartitionSpec as P

NT = 4
HMAX = 8
DEEP = NT
ROW0 = 16
F32 = jnp.float32
BF16 = jnp.bfloat16
HBM = pl.BlockSpec(memory_space=pltpu.HBM)
SMEM = pl.BlockSpec(memory_space=pltpu.SMEM)
VMEM = pl.BlockSpec(memory_space=pltpu.VMEM)
DEPTHS = (DEEP, DEEP) + (DEEP - 1,) * 6
STARTS = tuple(sum(DEPTHS[:i]) for i in range(8))
LAYERS = sum(DEPTHS)


def pin(arrays, space=pltpu.HBM):
    return [pltpu.with_memory_space_constraint(a, space) for a in arrays]


def params(mib=63):
    return pltpu.CompilerParams(vmem_limit_bytes=mib * 2**20)


def copy_all(pairs, sems):
    copies = [pltpu.make_async_copy(a, b, sems.at[i]) for i, (a, b) in enumerate(pairs)]
    for c in copies:
        c.start()
    return copies


def wait_all(copies):
    for c in copies:
        c.wait()


def pack_x_kernel(*refs):
    fields, out, stage, small, sems, out_sems = refs[:8], *refs[8:]
    core = lax.axis_index("mem")
    width = fields[0].shape[0]
    pairs = []
    for f, s, d in zip(fields, STARTS, DEPTHS):
        begin = jnp.where(core == 0, width - d, 0)
        pairs.append((f.at[pl.ds(begin, d)], stage.at[pl.ds(s, d)]))
    copies = copy_all(pairs, sems)
    sent = []
    for i, (s, d) in enumerate(zip(STARTS, DEPTHS)):
        copies[i].wait()
        small[s : s + d] = stage[s : s + d].astype(BF16)
        part = pl.ds(s, d)
        sent.append(pltpu.make_async_copy(small.at[part], out.at[part], out_sems.at[i]))
        sent[-1].start()
    wait_all(sent)


def pack_x(fields):
    shape = (LAYERS,) + fields[0].shape[1:]
    return pl.pallas_call(
        pack_x_kernel,
        out_shape=jax.ShapeDtypeStruct(shape, BF16),
        in_specs=[HBM] * 8,
        out_specs=HBM,
        scratch_shapes=[
            pltpu.VMEM(shape, F32),
            pltpu.VMEM(shape, BF16),
            pltpu.SemaphoreType.DMA((8,)),
            pltpu.SemaphoreType.DMA((8,)),
        ],
        compiler_params=params(),
        name="pack_x",
    )(*pin(fields))


def pack_rest_kernel(*refs):
    fields, own, other, _ = refs[:8], *refs[8:11]
    ys, same, cross, xs = refs[11:15]
    stage, snaps, edges, stage_c, snaps_c, mixed, s_ys, s_same, s_cross, sems, out_sems = refs[15:]
    core = lax.axis_index("mem")
    width, rows, _ = fields[0].shape
    near, far = width - DEEP, width - HMAX
    to_low = core == 1
    x_near, x_far = jnp.where(to_low, 0, near), jnp.where(to_low, 0, far)

    def y_at(low, size):
        return pl.multiple_of(jnp.where(low, 0, rows - size), size)

    pairs = []
    for i, f in enumerate(fields):
        pairs.append((f.at[:, pl.ds(y_at(to_low, 8), 8)], stage.at[i]))
        pairs.append((f.at[pl.ds(x_near, DEEP), pl.ds(y_at(~to_low, 8), 8)], stage_c.at[i]))
    for ref, half in ((own, core), (other, 1 - core)):
        pairs.append((ref.at[:, :, pl.ds(y_at(to_low, 16), 16)], snaps.at[half]))
        rim = ref.at[:, pl.ds(x_far, HMAX), pl.ds(y_at(~to_low, 16), 16)]
        pairs.append((rim, snaps_c.at[half]))
        pairs.append((ref.at[:, pl.ds(x_far, HMAX)], edges.at[pl.ds(2 * half, 2)]))
    copies = copy_all(pairs, sems)
    sent = []

    def send(a, b):
        sent.append(pltpu.make_async_copy(a, b, out_sems.at[len(sent)]))
        sent[-1].start()

    wait_all(copies[:16])
    skip, skip_c = jnp.where(to_low, 0, 4), jnp.where(to_low, 4, 0)
    for slab in range(2):
        for i in range(4):
            at = pl.ds(4 * i, 4)
            mixed[:width, at, :] = stage[4 * slab + i, :, pl.ds(skip, 4), :]
            mixed[width : width + DEEP, at, :] = stage_c[4 * slab + i, :, pl.ds(skip_c, 4), :]
        s_ys[slab] = mixed[:width].astype(BF16)
        s_cross[slab * DEEP : (slab + 1) * DEEP] = mixed[width : width + DEEP].astype(BF16)
    wait_all(copies[16:])
    for pair in range(2):
        for i in range(2):
            at = slice(8 * i, 8 * i + 8)
            both = snaps[pair, i].astype(F32)
            mixed[:width, at, :] = jnp.where(to_low, both[:, :8], both[:, 8:])
            both = snaps_c[pair, i].astype(F32)
            mixed[width : width + HMAX, at, :] = jnp.where(to_low, both[:, 8:], both[:, :8])
        s_ys[2 + pair] = mixed[:width].astype(BF16)
        begin = 2 * DEEP + pair * HMAX
        s_cross[begin : begin + HMAX] = mixed[width : width + HMAX].astype(BF16)
    send(s_ys, ys)
    send(s_cross, cross)
    send(edges, xs)
    for slab in range(2):
        begin = slab * DEEP
        s_same[begin : begin + DEEP] = s_ys[slab, pl.ds(x_near, DEEP)]
        begin = 2 * DEEP + slab * HMAX
        s_same[begin : begin + HMAX] = s_ys[2 + slab, pl.ds(x_far, HMAX)]
    send(s_same, same)
    wait_all(sent)


def pack_rest(fields, own, other, earlier):
    width, rows, depth = fields[0].shape
    corner = (2 * DEEP + 2 * HMAX, 16, depth)
    return pl.pallas_call(
        pack_rest_kernel,
        out_shape=(
            jax.ShapeDtypeStruct((4, width, 16, depth), BF16),
            jax.ShapeDtypeStruct(corner, BF16),
            jax.ShapeDtypeStruct(corner, BF16),
            jax.ShapeDtypeStruct((NT, HMAX, rows, depth), BF16),
        ),
        in_specs=[HBM] * 11,
        out_specs=(HBM,) * 4,
        scratch_shapes=[
            pltpu.VMEM((8, width, 8, depth), F32),
            pltpu.VMEM((2, 2, width, 16, depth), BF16),
            pltpu.VMEM((NT, HMAX, rows, depth), BF16),
            pltpu.VMEM((8, DEEP, 8, depth), F32),
            pltpu.VMEM((2, 2, HMAX, 16, depth), BF16),
            pltpu.VMEM((width + HMAX, 16, depth), F32),
            pltpu.VMEM((4, width, 16, depth), BF16),
            pltpu.VMEM(corner, BF16),
            pltpu.VMEM(corner, BF16),
            pltpu.SemaphoreType.DMA((22,)),
            pltpu.SemaphoreType.DMA((4,)),
        ],
        compiler_params=params(),
        name="pack_rest",
    )(*pin((*fields, own, other, earlier)))


def load_kernel(target, *refs):
    fields, bufs, (count, chosen, places, sems) = refs[:8], refs[8:16], refs[16:]
    width, rows, _ = fields[0].shape
    mid = (pl.ds(DEEP, width), pl.ds(ROW0, rows))
    copies = copy_all([(f, b.at[mid]) for f, b in zip(fields, bufs)], sems)

    def one(r, n):
        place = target[r]
        chosen[n] = r
        places[n] = place
        return n + jnp.where(place >= 0, 1, 0)

    count[0] = lax.fori_loop(0, target.shape[0], one, jnp.int32(0), unroll=8)
    wait_all(copies)


def load(target, fields, earlier):
    width, rows, depth = fields[0].shape
    n = target.shape[0]
    ints = jax.ShapeDtypeStruct((n + 1,), jnp.int32)
    out = pl.pallas_call(
        lambda target, *refs: load_kernel(target, *refs[:8], *refs[9:]),
        out_shape=(pltpu.VMEM((width + 2 * DEEP, rows + 2 * ROW0, depth), F32),) * 8
        + (jax.ShapeDtypeStruct((1,), jnp.int32), ints, ints),
        in_specs=[SMEM] + [HBM] * 9,
        out_specs=(VMEM,) * 8 + (SMEM,) * 3,
        scratch_shapes=[pltpu.SemaphoreType.DMA((8,))],
        compiler_params=params(8),
        name="load",
    )(target, *pin((*fields, earlier)))
    return out[:8], out[8:]


def wave_kernel(count, chosen, places, data, offs, *refs):
    halo_refs, own, other = refs[:8], refs[8], refs[9]
    p_out, q_out, image, p_rims = refs[18:22]
    bufs = refs[22:30]
    s_xw, s_y, s_xc, stage, snaps, wide, total, sem_halo, sem_in, sem_out = refs[30:]
    core, off_x, off_y = lax.axis_index("mem"), offs[0, 0], offs[0, 1]
    width, rows, depth = p_out.shape
    mid = (pl.ds(DEEP, width), pl.ds(ROW0, rows))
    pairs = []
    for i, side in ((0, core), (1, 1 - core)):
        xw, ys, same, cross = halo_refs[i::2]
        wave_part = pl.ds(0, 2 * DEEP)
        pairs.append((xw, s_xw.at[side]))
        pairs.append((ys, s_y.at[side]))
        pairs.append((same.at[wave_part], s_xc.at[side, side]))
        pairs.append((cross.at[wave_part], s_xc.at[side, 1 - side]))
    halos = copy_all(pairs, sem_halo)
    mains = copy_all(
        [(own, snaps.at[pl.ds(2 * core, 2)]), (other, snaps.at[pl.ds(2 - 2 * core, 2)])], sem_in
    )
    wait_all(halos)
    for side in range(2):
        for f in range(8):
            d = DEPTHS[f]
            to = DEEP - d if side == 0 else DEEP + width
            part = s_xw[side, STARTS[f] : STARTS[f] + d]
            bufs[f][to : to + d, ROW0 : ROW0 + rows, :] = part.astype(F32)
    for yside in range(2):
        to = ROW0 - DEEP if yside == 0 else ROW0 + rows
        for slab in range(2):
            stage[DEEP : DEEP + width] = s_y[yside, slab].astype(F32)
            for xside in range(2):
                at = 0 if xside == 0 else DEEP + width
                part = s_xc[xside, yside, slab * DEEP : slab * DEEP + DEEP]
                stage[at : at + DEEP] = part.astype(F32)
            for i in range(4):
                bufs[4 * slab + i][:, to : to + DEEP, :] = stage[:, 4 * i : 4 * i + 4, :]
    wait_all(mains)

    horiz, vert, ratio, tilt = bufs[4:]
    thin = lax.broadcasted_iota(jnp.int32, (1, depth), 1)

    def slopes(v):
        lane = lax.broadcasted_iota(jnp.int32, v.shape, 1)
        up = jnp.where(lane == depth - 1, 0.0, pltpu.roll(v, depth - 1, 1))
        down = jnp.where(lane == 0, 0.0, pltpu.roll(v, 1, 1))
        return up + down, up - down

    def step(k, p, q, old_p, old_q):
        low, high = 1 + k, width + 2 * DEEP - 1 - k
        begin, end = (ROW0 - 8, ROW0 + rows + 8) if k < NT - 1 else (ROW0, ROW0 + rows)
        size = 24 if (end - begin) % 24 == 0 else 32 if (end - begin) % 32 == 0 else 8

        def strip(i, _):
            r = pl.multiple_of(begin + i * size, 8)
            at = pl.ds(r, size)
            p_m, p_c, q_c = p[low - 1, at, :], p[low, at, :], q[low, at, :]
            _, d_m = slopes(q[low - 1, at, :])
            s_c, d_c = slopes(q_c)
            for x in range(low, high):
                p_n, q_n = p[x + 1, at, :], q[x + 1, at, :]
                s_n, d_n = slopes(q_n)
                beside = p[x, pl.ds(r - 1, size), :] + p[x, pl.ds(r + 1, size), :]
                lateral = ((p_m + p_n) + beside) - 4.0 * p_c
                q_2 = 2.0 * q_c
                horizontal = horiz[x, at, :] * lateral
                mixed = (0.25 * tilt[x, at, :]) * (d_n - d_m)
                upright = vert[x, at, :] * ((s_c - q_2) + mixed)
                old_p[x, at, :] = (2.0 * p_c - old_p[x, at, :]) + (horizontal + upright)
                old_q[x, at, :] = (q_2 - old_q[x, at, :]) + (ratio[x, at, :] * horizontal + upright)
                p_m, p_c, q_c, s_c, d_m, d_c = p_c, p_n, q_n, s_n, d_c, d_n
            return 0

        lax.fori_loop(0, (end - begin) // size, strip, 0)

        def inject(j, _):
            place = places[j]
            amount = data[NT - 1 - k, chosen[j]]
            x, y, z = place >> 16, (place >> 8) & 255, place & 255
            add = jnp.where(thin == z, amount, 0.0)
            old_p[x, pl.ds(y, 1), :] = old_p[x, pl.ds(y, 1), :] + add
            old_q[x, pl.ds(y, 1), :] = old_q[x, pl.ds(y, 1), :] + add
            return 0

        lax.fori_loop(0, count[0], inject, 0)

    y_side = jnp.where(off_y > 0, 0, 1)

    def add_image(k, p):
        t = NT - 1 - k
        pair, half = t // 2, t % 2

        def layer(x, _):
            at = jnp.clip(x - off_x, 0, width - 1)
            slot = x % 4
            rim = s_y[y_side, 2 + pair, at].astype(F32)[8 * half : 8 * half + 8]
            wide[slot, HMAX : HMAX + rows, :] = snaps[t, at].astype(F32)
            wide[slot, 0:HMAX, :] = rim
            wide[slot, HMAX + rows :, :] = rim
            term = wide[slot, pl.ds(HMAX - off_y, rows), :] * p[x + DEEP, ROW0 : ROW0 + rows, :]
            total[x] = term if k == 0 else total[x] + term
            return 0

        lax.fori_loop(0, width, layer, 0, unroll=4)

    p_now, q_now, p_old, q_old = bufs[:4]
    rim_at = pl.ds(jnp.where(off_x > 0, DEEP, DEEP + width - HMAX), HMAX)
    for k in range(NT):
        keep = pltpu.make_async_copy(p_now.at[rim_at, mid[1]], p_rims.at[k], sem_out.at[k])
        keep.start()
        add_image(k, p_now)
        step(k, p_now, q_now, p_old, q_old)
        p_now, p_old, q_now, q_old = p_old, p_now, q_old, q_now
        keep.wait()
    results = [(total, image), (p_now.at[mid], p_out), (q_now.at[mid], q_out)]
    wait_all(copy_all(results, sem_out))


def wave(receivers, data, offs, halos, own, other, bufs):
    width, rows, depth = own.shape[1:]
    block = jax.ShapeDtypeStruct((width, rows, depth), F32)
    return pl.pallas_call(
        wave_kernel,
        out_shape=(block, block, block, jax.ShapeDtypeStruct((NT, HMAX, rows, depth), F32))
        + tuple(pltpu.VMEM(b.shape, F32) for b in bufs),
        in_specs=[SMEM] * 5 + [HBM] * 10 + [VMEM] * 8,
        out_specs=(HBM,) * 4 + (VMEM,) * 8,
        input_output_aliases={15 + i: 4 + i for i in range(8)},
        scratch_shapes=[
            pltpu.VMEM((2, LAYERS, rows, depth), BF16),
            pltpu.VMEM((2, 4, width, 16, depth), BF16),
            pltpu.VMEM((2, 2, 2 * DEEP, 16, depth), BF16),
            pltpu.VMEM((width + 2 * DEEP, 16, depth), F32),
            pltpu.VMEM((NT, width, rows, depth), BF16),
            pltpu.VMEM((4, rows + 2 * HMAX, depth), F32),
            pltpu.VMEM((width, rows, depth), F32),
            pltpu.SemaphoreType.DMA((8,)),
            pltpu.SemaphoreType.DMA((2,)),
            pltpu.SemaphoreType.DMA((NT,)),
        ],
        compiler_params=params(24),
        name="wave",
    )(*receivers, data, offs, *halos, *pin((own, other)), *pin(bufs, pltpu.VMEM))[:4]


def rim_kernel(offs, *refs):
    halos, p_rims, image = refs[:6], refs[6], refs[8]
    snaps, strips, ps, wide, total, sems, sem_out = refs[9:]
    core, off_x, off_y = lax.axis_index("mem"), offs[0, 0], offs[0, 1]
    width, rows, _ = image.shape
    low = off_x > 0
    layers = jnp.abs(off_x)
    x_side = jnp.where(low, 0, 1)
    y_side = jnp.where(off_y > 0, 0, 1)
    rims = pltpu.make_async_copy(p_rims, ps, sems.at[2])
    rims.start()

    def fetch(xs, corner):
        source = corner.at[pl.ds(2 * DEEP, 2 * HMAX)]
        wait_all(copy_all([(xs, snaps), (source, strips)], sems))

    for i in range(2):
        xs, same, cross = halos[i::2]
        mine = x_side == (core if i == 0 else 1 - core)
        pl.when(mine & (x_side == y_side))(lambda xs=xs, c=same: fetch(xs, c))
        pl.when(mine & (x_side != y_side))(lambda xs=xs, c=cross: fetch(xs, c))
    rims.wait()

    def out_copy(i):
        x = jnp.where(low, i, width - layers + i)
        return pltpu.make_async_copy(total.at[i], image.at[x], sem_out.at[i])

    for i in range(HMAX):

        @pl.when(i < layers)
        def _(i=i):
            at = jnp.where(low, HMAX - layers + i, i)
            mine = jnp.where(low, i, HMAX - layers + i)
            result = None
            for pair in range(2):
                strip = strips[pair * HMAX + at].astype(F32)
                for half in range(2):
                    t = 2 * pair + half
                    rim = strip[8 * half : 8 * half + 8]
                    wide[t, HMAX : HMAX + rows, :] = snaps[t, at].astype(F32)
                    wide[t, 0:HMAX, :] = rim
                    wide[t, HMAX + rows :, :] = rim
                    term = wide[t, pl.ds(HMAX - off_y, rows), :] * ps[NT - 1 - t, mine]
                    result = term if result is None else result + term
            total[i] = result
            out_copy(i).start()

    for i in range(HMAX):
        pl.when(i < layers)(lambda i=i: out_copy(i).wait())


def rim_image(offs, halos, p_rims, image):
    width, rows, depth = image.shape
    return pl.pallas_call(
        rim_kernel,
        out_shape=jax.ShapeDtypeStruct(image.shape, F32),
        in_specs=[SMEM] + [HBM] * 8,
        out_specs=HBM,
        input_output_aliases={8: 0},
        scratch_shapes=[
            pltpu.VMEM((NT, HMAX, rows, depth), BF16),
            pltpu.VMEM((2 * HMAX, 16, depth), BF16),
            pltpu.VMEM((NT, HMAX, rows, depth), F32),
            pltpu.VMEM((NT, rows + 2 * HMAX, depth), F32),
            pltpu.VMEM((HMAX, rows, depth), F32),
            pltpu.SemaphoreType.DMA((3,)),
            pltpu.SemaphoreType.DMA((HMAX,)),
        ],
        compiler_params=params(),
        name="rim_image",
    )(offs, *halos, *pin((p_rims, image)))


def body(
    src_hist, rec_p, rec_q, prev_p, prev_q, horiz, vert, ratio, tilt, rec_pos, rec_data, lag_offs
):
    width, rows, depth = rec_p.shape
    fields = (rec_p, rec_q, prev_p, prev_q, horiz, vert, ratio, tilt)

    def swap(v):
        return lax.ppermute(v, "mem", [(0, 1), (1, 0)])

    def after(v, earlier):
        return lax.optimization_barrier((v, earlier))[0]

    def outward(v, step_x, step_y):
        count_x, count_y = lax.axis_size("gx"), lax.axis_size("gy")
        pairs = []
        for x in range(count_x):
            for y in range(count_y):
                for core, sign in ((0, 1), (1, -1)):
                    to_x, to_y = x + sign * step_x, y + sign * step_y
                    if 0 <= to_x < count_x and 0 <= to_y < count_y:
                        pairs.append(((x * count_y + y) * 2 + core, (to_x * count_y + to_y) * 2 + core))
        return lax.ppermute(v, ("gx", "gy", "mem"), pairs)

    plane = rows * lax.axis_size("gy") * depth
    x = rec_pos // plane - lax.axis_index("gx") * width + DEEP
    rest = rec_pos % plane
    y = rest // depth - lax.axis_index("gy") * rows + ROW0
    z = rest % depth
    inside = (x >= 0) & (x < width + 2 * DEEP)
    inside &= (y >= ROW0 - DEEP) & (y < ROW0 + rows + DEEP)
    target = jnp.where(inside, (x << 16) + (y << 8) + z, -1)

    other = swap(src_hist)
    packed = pack_x(fields)
    xw = outward(packed, 1, 0)
    ys, same, cross, xs = pack_rest(fields, src_hist, other, packed)
    ys, same, cross = outward(ys, 0, 1), outward(same, 1, 1), outward(cross, 1, -1)
    xs = outward(after(xs, (same, cross)), 1, 0)
    bufs, receivers = load(target, fields, packed)
    same, cross = (same, swap(same)), (cross, swap(cross))
    halos = (xw, swap(xw), ys, swap(ys)) + same + cross
    p, q, image, p_rims = wave(receivers, rec_data, lag_offs, halos, src_hist, other, bufs)
    image = rim_image(lag_offs, (xs, swap(after(xs, p))) + same + cross, p_rims, image)
    return image[None], p, q


def solution(mesh):
    block = P("gx", "gy", None)
    return jax.shard_map(
        body,
        mesh=mesh,
        in_specs=(P("mem", "gx", "gy", None),) + (block,) * 8 + (P(), P(), P("mem", None)),
        out_specs=(P("mem", "gx", "gy", None), block, block),
        check_vma=False,
    )
```

time: 365 us -> 72 us (0.20)
  the two profiles are of different devices: /device:TPU:0 before, /device:TPU:12 now
where the time goes in v2:
time: 72 us; the launch traced here: 71.5 us
  Pallas kernels  40.8 us (57%)
  starting transfers between devices  15.2 us (21%)
  waiting for transfers between devices  14.5 us (20%)
  between operations  0.86 us (1%)
    pallas_call x1, Pallas kernels, wave(): pl.pallas_call(wave_kernel, out_shape=(block, block, block, jax.ShapeDtyp...  24.2 us
    ppermute x5, starting transfers between devices, outward(): return lax.ppermute(v, ('gx', 'gy', 'mem'), pairs)  14 us
    ppermute x5, waiting for transfers between devices, outward(): return lax.ppermute(v, ('gx', 'gy', 'mem'), pairs)  11.6 us
    pallas_call x1, Pallas kernels, load(): pl.pallas_call(lambda target, *refs: load_kernel(target, *refs[:8], *refs...  7.29 us
    pallas_call x1, Pallas kernels, rim_image(): pl.pallas_call(rim_kernel, out_shape=jax.ShapeDtypeStruct(image.shape, F3...  3.69 us
    pallas_call x1, Pallas kernels, pack_rest(): pl.pallas_call(pack_rest_kernel, out_shape=(jax.ShapeDtypeStruct((4, widt...  3.48 us
    ppermute x6, waiting for transfers between devices, swap(): return lax.ppermute(v, 'mem', [(0, 1), (1, 0)])  2.97 us
    pallas_call x1, Pallas kernels, pack_x(): pl.pallas_call(pack_x_kernel, out_shape=jax.ShapeDtypeStruct(shape, BF16)...  2.18 us
  transfers between devices with their start and end apart: 11, of which 3 were waited for; matrix products, arithmetic and copies ran while one was open for 0% of the time, Pallas kernels for 52%

profile of v2, /device:TPU:12, one launch (start us, length us, event | category | flops | bytes accessed | tf_op | source)
XLA Modules:
  0.0 71.5 jit_solution(4356587468454259590)
XLA Ops:
  0.6 0.1 collective-permute-start
  0.7 2.2 %pack_x.1.refs_10_.refs_8_ = bf16[26,128,128]{2,1,0:T(8,128)(2,1)} custom-call(f32[32,128,128]{2,1,0:T(8,128)} %refs_0_.5, f32[32,128,128]{2,1,0:T(8,128)} %refs_1_.5, f32[32,128,128]{2,1,0:T(8,128)} %refs_2_.5, f32[32,128,128]{2,1,0:T(8,128)} %refs_3_.5, f32[32,128,128]{2,1,0:T(8,128)} %refs_4_.5, f32[32,128,128]{2,1,0:T(8,128)} %refs_5_.5, ...), custom_call_target="tpu_custom_call" | custom-call | tf_op jit(solution)/shard_map/pack_x/pallas_call | solution.py:65
  2.9 0.0 copy-start.6
  2.9 3.4 %collective-permute-start.4 = (bf16[26,128,128]{2,1,0:T(8,128)(2,1)}, bf16[26,128,128]{2,1,0:T(8,128)(2,1)S(1)}, u32[]{:S(2)}, u32[]{:S(2)}) collective-permute-start(bf16[26,128,128]{2,1,0:T(8,128)(2,1)} %pack_x.1.refs_10_.refs_8_), channel_id=1, source_target_pairs={{0,8},{2,10},{4,12},{6,14},{8,16},{9,1},{10,18},{11,3},{12,20},{13... | collective-permute-start | bytes 2555912 | tf_op jit(solution)/shard_map/ppermute | solution.py:445
  6.3 0.0 collective-permute-done.refs_9_
  6.3 3.5 %pack_rest.1 = (bf16[4,32,16,128]{3,2,1,0:T(8,128)(2,1)}, bf16[24,16,128]{2,1,0:T(8,128)(2,1)}, bf16[24,16,128]{2,1,0:T(8,128)(2,1)}, bf16[4,8,128,128]{3,2,1,0:T(8,128)(2,1)}) custom-call(f32[32,128,128]{2,1,0:T(8,128)} %refs_0_.5, f32[32,128,128]{2,1,0:T(8,128)} %refs_1_.5, f32[32,128,128]{2,1,0:T(8,128)} %refs_2_.5, f32[32,128,128]{2,1,0:T(8,128)} %refs_3_.5, ...), custom_call_target="tpu_custom_call" | custom-call | tf_op jit(solution)/shard_map/pack_rest/pallas_call | solution.py:145
  9.8 3.3 %collective-permute-start.1 = (bf16[24,16,128]{2,1,0:T(8,128)(2,1)}, bf16[24,16,128]{2,1,0:T(8,128)(2,1)S(1)}, u32[]{:S(2)}, u32[]{:S(2)}) collective-permute-start(bf16[24,16,128]{2,1,0:T(8,128)(2,1)} %get-tuple-element.25), channel_id=1, source_target_pairs={{0,10},{2,12},{4,14},{8,18},{10,20},{11,1},{12,22},{13,3},{15,5},{... | collective-permute-start | bytes 294920 | tf_op jit(solution)/shard_map/ppermute | solution.py:445
  13.1 1.9 %collective-permute-start.2 = (bf16[24,16,128]{2,1,0:T(8,128)(2,1)}, bf16[24,16,128]{2,1,0:T(8,128)(2,1)S(1)}, u32[]{:S(2)}, u32[]{:S(2)}) collective-permute-start(bf16[24,16,128]{2,1,0:T(8,128)(2,1)} %get-tuple-element.26), channel_id=1, source_target_pairs={{2,8},{4,10},{6,12},{9,3},{10,16},{11,5},{12,18},{13,7},{14,20},{1... | collective-permute-start | bytes 294920 | tf_op jit(solution)/shard_map/ppermute | solution.py:445
  15.0 3.5 %collective-permute-start.6 = (bf16[4,32,16,128]{3,2,1,0:T(8,128)(2,1)}, bf16[4,32,16,128]{3,2,1,0:T(8,128)(2,1)S(1)}, u32[]{:S(2)}, u32[]{:S(2)}) collective-permute-start(bf16[4,32,16,128]{3,2,1,0:T(8,128)(2,1)} %get-tuple-element.31), channel_id=1, source_target_pairs={{0,2},{2,4},{3,1},{4,6},{5,3},{7,5},{8,10},{10,12},{11,9},{12,14},... | collective-permute-start | bytes 1572872 | tf_op jit(solution)/shard_map/ppermute | solution.py:445
  18.5 0.0 collective-permute-done.1.refs_4_.refs_2_
  18.5 0.0 copy-start
  18.5 4.2 %collective-permute-done.2.refs_6_.refs_4_ = bf16[24,16,128]{2,1,0:T(8,128)(2,1)S(1)} collective-permute-done((bf16[24,16,128]{2,1,0:T(8,128)(2,1)}, bf16[24,16,128]{2,1,0:T(8,128)(2,1)S(1)}, u32[]{:S(2)}, u32[]{:S(2)}) %collective-permute-start.2) | collective-permute-done | bytes 98336 | tf_op jit(solution)/shard_map/ppermute | solution.py:445
  22.7 1.9 %collective-permute-start.3 = (bf16[4,8,128,128]{3,2,1,0:T(8,128)(2,1)}, bf16[4,8,128,128]{3,2,1,0:T(8,128)(2,1)}, u32[]{:S(2)}, u32[]{:S(2)}) collective-permute-start(bf16[4,8,128,128]{3,2,1,0:T(8,128)(2,1)} %get-tuple-element.27), channel_id=1, source_target_pairs={{0,8},{2,10},{4,12},{6,14},{8,16},{9,1},{10,18},{11,3},{12,20},{13... | collective-permute-start | bytes 3145736 | tf_op jit(solution)/shard_map/ppermute | solution.py:445
  24.6 7.4 %collective-permute-done.4.refs_0_ = bf16[26,128,128]{2,1,0:T(8,128)(2,1)S(1)} collective-permute-done((bf16[26,128,128]{2,1,0:T(8,128)(2,1)}, bf16[26,128,128]{2,1,0:T(8,128)(2,1)S(1)}, u32[]{:S(2)}, u32[]{:S(2)}) %collective-permute-start.4) | collective-permute-done | bytes 852000 | tf_op jit(solution)/shard_map/ppermute | solution.py:445
  32.0 0.0 collective-permute-start.5
  32.0 0.0 collective-permute-done.6.refs_2_
  32.0 0.5 collective-permute-start.7
  32.5 0.0 collective-permute-start.8
  32.5 0.5 collective-permute-start.9
  33.1 0.0 copy-start.4
  33.1 0.0 copy-start.5
  33.1 7.3 %load.1 = (f32[40,160,128]{2,1,0:T(8,128)S(1)}, f32[40,160,128]{2,1,0:T(8,128)S(1)}, f32[40,160,128]{2,1,0:T(8,128)S(1)}, f32[40,160,128]{2,1,0:T(8,128)S(1)}, f...) custom-call(s32[1024]{0:T(1024)S(1)} %fusion.5.target, ...), custom_call_target="tpu_custom_call" | custom-call | tf_op jit(solution)/shard_map/load/pallas_call | solution.py:193
  40.4 0.0 collective-permute-done.5.refs_1_
  40.4 0.0 collective-permute-done.8.refs_5_.refs_3_
  40.4 0.0 copy-start.2
  40.4 0.0 collective-permute-done.9.refs_7_.refs_5_
  40.4 0.0 collective-permute-done.7.refs_3_
  40.5 24.2 %wave.1 = (f32[32,128,128]{2,1,0:T(8,128)}, f32[32,128,128]{2,1,0:T(8,128)}, f32[32,128,128]{2,1,0:T(8,128)}, f32[4,8,128,128]{3,2,1,0:T(8,128)}, f32[40,160,128...) custom-call(s32[1]{0:T(128)} %get-tuple-element.28.count, ...), custom_call_target="tpu_custom_call", output_to_operand_aliasing={{4}: (15, {}), {5}: (16, {}), {6}: (17, {}), {7}: (18, {}),... | custom-call | tf_op jit(solution)/shard_map/wave/pallas_call | solution.py:327
  64.7 0.0 collective-permute-done.3.refs_0_
  64.7 0.1 collective-permute-start.10
  64.8 3.0 %collective-permute-done.10.refs_1_ = bf16[4,8,128,128]{3,2,1,0:T(8,128)(2,1)} collective-permute-done((bf16[4,8,128,128]{3,2,1,0:T(8,128)(2,1)}, bf16[4,8,128,128]{3,2,1,0:T(8,128)(2,1)}, u32[]{:S(2)}, u32[]{:S(2)}) %collective-permute-start.10) | collective-permute-done | bytes 1048608 | tf_op jit(solution)/shard_map/ppermute | solution.py:431
  67.8 3.7 %rim_image.1 = f32[32,128,128]{2,1,0:T(8,128)} custom-call(s32[1,2]{1,0:T(1,128)} %offs.3, bf16[4,8,128,128]{3,2,1,0:T(8,128)(2,1)} %collective-permute-done.3.refs_0_, bf16[4,8,128,128]{3,2,1,0:T(8,128)(2,1)} %collective-permute-done.10.refs_1_, bf16[24,16,128]{2,1,0:T(8,128)(2,1)} %copy-done, ...), custom_call_target="tpu_custom_call", output_to_operand_aliasing={{}: (8, {})} | custom-call | tf_op jit(solution)/shard_map/rim_image/pallas_call | solution.py:404
  (10 shorter events, 0.0 us)
Async XLA Ops:
  0.6 5.7 %collective-permute-start = (bf16[2,32,128,128]{3,2,1,0:T(8,128)(2,1)}, bf16[2,32,128,128]{3,2,1,0:T(8,128)(2,1)}, u32[]{:S(2)}, u32[]{:S(2)}) collective-permute-start(bf16[2,32,128,128]{3,2,1,0:T(8,128)(2,1)} %refs_8_.3), channel_id=1, source_target_pairs={{0,1},{1,0},{2,3},{3,2},{4,5},{5,4},{6,7},{7,6},{8,9},{9,8},{10,11... | collective-permute-start | bytes 6291464 | tf_op jit(solution)/shard_map/ppermute | solution.py:431
  2.9 30.1 %copy-start.6 = (s32[1024]{0:T(1024)S(1)}, s32[1024]{0:T(1024)}, u32[]{:S(2)}) copy-start(s32[1024]{0:T(1024)} %param.21) | copy-start | bytes 12292
  2.9 29.1 %collective-permute-start.4 = (bf16[26,128,128]{2,1,0:T(8,128)(2,1)}, bf16[26,128,128]{2,1,0:T(8,128)(2,1)S(1)}, u32[]{:S(2)}, u32[]{:S(2)}) collective-permute-start(bf16[26,128,128]{2,1,0:T(8,128)(2,1)} %pack_x.1.refs_10_.refs_8_), channel_id=1, source_target_pairs={{0,8},{2,10},{4,12},{6,14},{8,16},{9,1},{10,18},{11,3},{12,20},{13... | collective-permute-start | bytes 2555912 | tf_op jit(solution)/shard_map/ppermute | solution.py:445
  9.8 8.7 %collective-permute-start.1 = (bf16[24,16,128]{2,1,0:T(8,128)(2,1)}, bf16[24,16,128]{2,1,0:T(8,128)(2,1)S(1)}, u32[]{:S(2)}, u32[]{:S(2)}) collective-permute-start(bf16[24,16,128]{2,1,0:T(8,128)(2,1)} %get-tuple-element.25), channel_id=1, source_target_pairs={{0,10},{2,12},{4,14},{8,18},{10,20},{11,1},{12,22},{13,3},{15,5},{... | collective-permute-start | bytes 294920 | tf_op jit(solution)/shard_map/ppermute | solution.py:445
  13.1 9.6 %collective-permute-start.2 = (bf16[24,16,128]{2,1,0:T(8,128)(2,1)}, bf16[24,16,128]{2,1,0:T(8,128)(2,1)S(1)}, u32[]{:S(2)}, u32[]{:S(2)}) collective-permute-start(bf16[24,16,128]{2,1,0:T(8,128)(2,1)} %get-tuple-element.26), channel_id=1, source_target_pairs={{2,8},{4,10},{6,12},{9,3},{10,16},{11,5},{12,18},{13,7},{14,20},{1... | collective-permute-start | bytes 294920 | tf_op jit(solution)/shard_map/ppermute | solution.py:445
  15.0 17.0 %collective-permute-start.6 = (bf16[4,32,16,128]{3,2,1,0:T(8,128)(2,1)}, bf16[4,32,16,128]{3,2,1,0:T(8,128)(2,1)S(1)}, u32[]{:S(2)}, u32[]{:S(2)}) collective-permute-start(bf16[4,32,16,128]{3,2,1,0:T(8,128)(2,1)} %get-tuple-element.31), channel_id=1, source_target_pairs={{0,2},{2,4},{3,1},{4,6},{5,3},{7,5},{8,10},{10,12},{11,9},{12,14},... | collective-permute-start | bytes 1572872 | tf_op jit(solution)/shard_map/ppermute | solution.py:445
  18.5 21.9 %copy-start = (bf16[24,16,128]{2,1,0:T(8,128)(2,1)}, bf16[24,16,128]{2,1,0:T(8,128)(2,1)S(1)}, u32[]{:S(2)}) copy-start(bf16[24,16,128]{2,1,0:T(8,128)(2,1)S(1)} %collective-permute-done.1.refs_4_.refs_2_) | copy-start | bytes 294916
  22.7 17.7 %copy-start.1 = (bf16[24,16,128]{2,1,0:T(8,128)(2,1)}, bf16[24,16,128]{2,1,0:T(8,128)(2,1)S(1)}, u32[]{:S(2)}) copy-start(bf16[24,16,128]{2,1,0:T(8,128)(2,1)S(1)} %collective-permute-done.2.refs_6_.refs_4_) | copy-start | bytes 294916
  22.7 42.0 %collective-permute-start.3 = (bf16[4,8,128,128]{3,2,1,0:T(8,128)(2,1)}, bf16[4,8,128,128]{3,2,1,0:T(8,128)(2,1)}, u32[]{:S(2)}, u32[]{:S(2)}) collective-permute-start(bf16[4,8,128,128]{3,2,1,0:T(8,128)(2,1)} %get-tuple-element.27), channel_id=1, source_target_pairs={{0,8},{2,10},{4,12},{6,14},{8,16},{9,1},{10,18},{11,3},{12,20},{13... | collective-permute-start | bytes 3145736 | tf_op jit(solution)/shard_map/ppermute | solution.py:445
  32.0 8.4 %collective-permute-start.5 = (bf16[26,128,128]{2,1,0:T(8,128)(2,1)S(1)}, bf16[26,128,128]{2,1,0:T(8,128)(2,1)S(1)}, u32[]{:S(2)}, u32[]{:S(2)}) collective-permute-start(bf16[26,128,128]{2,1,0:T(8,128)(2,1)S(1)} %collective-permute-done.4.refs_0_), channel_id=1, source_target_pairs={{0,1},{1,0},{2,3},{3,2},{4,5},{5,4},{6,7},{7,6},{8,9},{9,8},{10,11... | collective-permute-start | bytes 2555912 | tf_op jit(solution)/shard_map/ppermute | solution.py:431
  32.0 8.4 %collective-permute-start.7 = (bf16[4,32,16,128]{3,2,1,0:T(8,128)(2,1)S(1)}, bf16[4,32,16,128]{3,2,1,0:T(8,128)(2,1)}, u32[]{:S(2)}, u32[]{:S(2)}) collective-permute-start(bf16[4,32,16,128]{3,2,1,0:T(8,128)(2,1)S(1)} %collective-permute-done.6.refs_2_), channel_id=1, source_target_pairs={{0,1},{1,0},{2,3},{3,2},{4,5},{5,4},{6,7},{7,6},{8,9},{9,8},{10,11... | collective-permute-start | bytes 1572872 | tf_op jit(solution)/shard_map/ppermute | solution.py:431
  32.5 7.9 %collective-permute-start.8 = (bf16[24,16,128]{2,1,0:T(8,128)(2,1)S(1)}, bf16[24,16,128]{2,1,0:T(8,128)(2,1)S(1)}, u32[]{:S(2)}, u32[]{:S(2)}) collective-permute-start(bf16[24,16,128]{2,1,0:T(8,128)(2,1)S(1)} %collective-permute-done.1.refs_4_.refs_2_), channel_id=1, source_target_pairs={{0,1},{1,0},{2,3},{3,2},{4,5},{5,4},{6,7},{7,6},{8,9},{9,8},{10,11... | collective-permute-start | bytes 294920 | tf_op jit(solution)/shard_map/ppermute | solution.py:431
  32.5 7.9 %collective-permute-start.9 = (bf16[24,16,128]{2,1,0:T(8,128)(2,1)S(1)}, bf16[24,16,128]{2,1,0:T(8,128)(2,1)S(1)}, u32[]{:S(2)}, u32[]{:S(2)}) collective-permute-start(bf16[24,16,128]{2,1,0:T(8,128)(2,1)S(1)} %collective-permute-done.2.refs_6_.refs_4_), channel_id=1, source_target_pairs={{0,1},{1,0},{2,3},{3,2},{4,5},{5,4},{6,7},{7,6},{8,9},{9,8},{10,11... | collective-permute-start | bytes 294920 | tf_op jit(solution)/shard_map/ppermute | solution.py:431
  33.1 7.4 %copy-start.4 = (f32[4,1024]{1,0:T(4,128)S(1)}, f32[4,1024]{1,0:T(4,128)}, u32[]{:S(2)}) copy-start(f32[4,1024]{1,0:T(4,128)} %data.1) | copy-start | bytes 49156
  33.1 7.4 %copy-start.5 = (s32[1,2]{1,0:T(1,128)S(1)}, s32[1,2]{1,0:T(1,128)}, u32[]{:S(2)}) copy-start(s32[1,2]{1,0:T(1,128)} %offs.3) | copy-start | bytes 28
  40.4 24.3 %copy-start.2 = (bf16[24,16,128]{2,1,0:T(8,128)(2,1)}, bf16[24,16,128]{2,1,0:T(8,128)(2,1)S(1)}, u32[]{:S(2)}) copy-start(bf16[24,16,128]{2,1,0:T(8,128)(2,1)S(1)} %collective-permute-done.8.refs_5_.refs_3_) | copy-start | bytes 294916
  40.4 24.3 %copy-start.3 = (bf16[24,16,128]{2,1,0:T(8,128)(2,1)}, bf16[24,16,128]{2,1,0:T(8,128)(2,1)S(1)}, u32[]{:S(2)}) copy-start(bf16[24,16,128]{2,1,0:T(8,128)(2,1)S(1)} %collective-permute-done.9.refs_7_.refs_5_) | copy-start | bytes 294916
  64.7 3.1 %collective-permute-start.10 = (bf16[4,8,128,128]{3,2,1,0:T(8,128)(2,1)}, bf16[4,8,128,128]{3,2,1,0:T(8,128)(2,1)}, u32[]{:S(2)}, u32[]{:S(2)}) collective-permute-start(bf16[4,8,128,128]{3,2,1,0:T(8,128)(2,1)} %collective-permute-done.3.refs_0_), channel_id=1, source_target_pairs={{0,1},{1,0},{2,3},{3,2},{4,5},{5,4},{6,7},{7,6},{8,9},{9,8},{10,11... | collective-permute-start | bytes 3145736 | tf_op jit(solution)/shard_map/ppermute | solution.py:431

commit v3 on v2

--- a/solution.py
+++ b/solution.py
@@ -11,6 +11,7 @@
 HMAX = 8
 DEEP = NT
 ROW0 = 16
+GROUP = 4
 F32 = jnp.float32
 BF16 = jnp.bfloat16
 HBM = pl.BlockSpec(memory_space=pltpu.HBM)
@@ -171,7 +172,8 @@
 
 
 def load_kernel(target, *refs):
-    fields, bufs, (count, chosen, places, sems) = refs[:8], refs[8:16], refs[16:]
+    n = (len(refs) - 5) // 2
+    fields, bufs, (count, chosen, places, sems) = refs[:n], refs[n + 1 : 2 * n + 1], refs[2 * n + 1 :]
     width, rows, _ = fields[0].shape
     mid = (pl.ds(DEEP, width), pl.ds(ROW0, rows))
     copies = copy_all([(f, b.at[mid]) for f, b in zip(fields, bufs)], sems)
@@ -182,25 +184,29 @@
         places[n] = place
         return n + jnp.where(place >= 0, 1, 0)
 
-    count[0] = lax.fori_loop(0, target.shape[0], one, jnp.int32(0), unroll=8)
+    found = lax.fori_loop(0, target.shape[0], one, jnp.int32(0), unroll=8)
+    for i in range(GROUP):
+        chosen[found + i] = 0
+        places[found + i] = 0
+    count[0] = (found + GROUP - 1) // GROUP
     wait_all(copies)
 
 
-def load(target, fields, earlier):
+def load(target, fields, earlier, name):
     width, rows, depth = fields[0].shape
-    n = target.shape[0]
-    ints = jax.ShapeDtypeStruct((n + 1,), jnp.int32)
+    n, m = target.shape[0], len(fields)
+    ints = jax.ShapeDtypeStruct((n + GROUP,), jnp.int32)
     out = pl.pallas_call(
-        lambda target, *refs: load_kernel(target, *refs[:8], *refs[9:]),
-        out_shape=(pltpu.VMEM((width + 2 * DEEP, rows + 2 * ROW0, depth), F32),) * 8
+        load_kernel,
+        out_shape=(pltpu.VMEM((width + 2 * DEEP, rows + 2 * ROW0, depth), F32),) * m
         + (jax.ShapeDtypeStruct((1,), jnp.int32), ints, ints),
-        in_specs=[SMEM] + [HBM] * 9,
-        out_specs=(VMEM,) * 8 + (SMEM,) * 3,
-        scratch_shapes=[pltpu.SemaphoreType.DMA((8,))],
+        in_specs=[SMEM] + [HBM] * (m + 1),
+        out_specs=(VMEM,) * m + (SMEM,) * 3,
+        scratch_shapes=[pltpu.SemaphoreType.DMA((m,))],
         compiler_params=params(8),
-        name="load",
+        name=name,
     )(target, *pin((*fields, earlier)))
-    return out[:8], out[8:]
+    return out[:m], out[m:]
 
 
 def wave_kernel(count, chosen, places, data, offs, *refs):
@@ -240,7 +246,6 @@
                 stage[at : at + DEEP] = part.astype(F32)
             for i in range(4):
                 bufs[4 * slab + i][:, to : to + DEEP, :] = stage[:, 4 * i : 4 * i + 4, :]
-    wait_all(mains)
 
     horiz, vert, ratio, tilt = bufs[4:]
     thin = lax.broadcasted_iota(jnp.int32, (1, depth), 1)
@@ -274,20 +279,35 @@
                 old_p[x, at, :] = (2.0 * p_c - old_p[x, at, :]) + (horizontal + upright)
                 old_q[x, at, :] = (q_2 - old_q[x, at, :]) + (ratio[x, at, :] * horizontal + upright)
                 p_m, p_c, q_c, s_c, d_m, d_c = p_c, p_n, q_n, s_n, d_c, d_n
+            if k == NT - 1:
+                wait_or_start(old_p, old_q, r - ROW0, size, i, True)
             return 0
 
-        lax.fori_loop(0, (end - begin) // size, strip, 0)
-
-        def inject(j, _):
-            place = places[j]
-            amount = data[NT - 1 - k, chosen[j]]
-            x, y, z = place >> 16, (place >> 8) & 255, place & 255
-            add = jnp.where(thin == z, amount, 0.0)
-            old_p[x, pl.ds(y, 1), :] = old_p[x, pl.ds(y, 1), :] + add
-            old_q[x, pl.ds(y, 1), :] = old_q[x, pl.ds(y, 1), :] + add
+        parts = (end - begin) // size
+        lax.fori_loop(0, parts, strip, 0)
+        if k == NT - 1:
+            for i in range(parts):
+                wait_or_start(old_p, old_q, i * size, size, i, False)
+
+    def wait_or_start(p, q, at, size, i, start):
+        for j, (buf, out) in enumerate(((p, p_out), (q, q_out))):
+            here = buf.at[mid[0], pl.ds(ROW0 + at, size)]
+            c = pltpu.make_async_copy(here, out.at[:, pl.ds(at, size)], sem_out.at[j, i])
+            c.start() if start else c.wait()
+
+    def inject(k, old_p, old_q):
+        def group(g, _):
+            for i in range(GROUP):
+                j = g * GROUP + i
+                place = places[j]
+                amount = data[NT - 1 - k, chosen[j]]
+                x, y, z = place >> 16, (place >> 8) & 255, place & 255
+                add = jnp.where(thin == z, amount, 0.0)
+                old_p[x, pl.ds(y, 1), :] = old_p[x, pl.ds(y, 1), :] - add
+                old_q[x, pl.ds(y, 1), :] = old_q[x, pl.ds(y, 1), :] - add
             return 0
 
-        lax.fori_loop(0, count[0], inject, 0)
+        lax.fori_loop(0, count[0], group, 0)
 
     y_side = jnp.where(off_y > 0, 0, 1)
 
@@ -309,16 +329,21 @@
         lax.fori_loop(0, width, layer, 0, unroll=4)
 
     p_now, q_now, p_old, q_old = bufs[:4]
-    rim_at = pl.ds(jnp.where(off_x > 0, DEEP, DEEP + width - HMAX), HMAX)
+    rim_x = jnp.where(off_x > 0, DEEP, DEEP + width - HMAX)
+    finished = pltpu.make_async_copy(total, image, sem_in.at[0])
     for k in range(NT):
-        keep = pltpu.make_async_copy(p_now.at[rim_at, mid[1]], p_rims.at[k], sem_out.at[k])
-        keep.start()
-        add_image(k, p_now)
+        p_rims[k] = p_now[pl.ds(rim_x, HMAX), ROW0 : ROW0 + rows, :]
+        if k == 1:
+            wait_all(mains)
+        if k >= 1:
+            add_image(k - 1, p_old)
+        if k == NT - 1:
+            add_image(k, p_now)
+            finished.start()
+        inject(k, p_old, q_old)
         step(k, p_now, q_now, p_old, q_old)
         p_now, p_old, q_now, q_old = p_old, p_now, q_old, q_now
-        keep.wait()
-    results = [(total, image), (p_now.at[mid], p_out), (q_now.at[mid], q_out)]
-    wait_all(copy_all(results, sem_out))
+    finished.wait()
 
 
 def wave(receivers, data, offs, halos, own, other, bufs):
@@ -326,10 +351,10 @@
     block = jax.ShapeDtypeStruct((width, rows, depth), F32)
     return pl.pallas_call(
         wave_kernel,
-        out_shape=(block, block, block, jax.ShapeDtypeStruct((NT, HMAX, rows, depth), F32))
+        out_shape=(block, block, block, pltpu.VMEM((NT, HMAX, rows, depth), F32))
         + tuple(pltpu.VMEM(b.shape, F32) for b in bufs),
         in_specs=[SMEM] * 5 + [HBM] * 10 + [VMEM] * 8,
-        out_specs=(HBM,) * 4 + (VMEM,) * 8,
+        out_specs=(HBM,) * 3 + (VMEM,) * 9,
         input_output_aliases={15 + i: 4 + i for i in range(8)},
         scratch_shapes=[
             pltpu.VMEM((2, LAYERS, rows, depth), BF16),
@@ -341,7 +366,7 @@
             pltpu.VMEM((width, rows, depth), F32),
             pltpu.SemaphoreType.DMA((8,)),
             pltpu.SemaphoreType.DMA((2,)),
-            pltpu.SemaphoreType.DMA((NT,)),
+            pltpu.SemaphoreType.DMA((2, rows // 8)),
         ],
         compiler_params=params(24),
         name="wave",
@@ -350,15 +375,13 @@
 
 def rim_kernel(offs, *refs):
     halos, p_rims, image = refs[:6], refs[6], refs[8]
-    snaps, strips, ps, wide, total, sems, sem_out = refs[9:]
+    snaps, strips, wide, total, sems, sem_out = refs[9:]
     core, off_x, off_y = lax.axis_index("mem"), offs[0, 0], offs[0, 1]
     width, rows, _ = image.shape
     low = off_x > 0
     layers = jnp.abs(off_x)
     x_side = jnp.where(low, 0, 1)
     y_side = jnp.where(off_y > 0, 0, 1)
-    rims = pltpu.make_async_copy(p_rims, ps, sems.at[2])
-    rims.start()
 
     def fetch(xs, corner):
         source = corner.at[pl.ds(2 * DEEP, 2 * HMAX)]
@@ -369,7 +392,6 @@
         mine = x_side == (core if i == 0 else 1 - core)
         pl.when(mine & (x_side == y_side))(lambda xs=xs, c=same: fetch(xs, c))
         pl.when(mine & (x_side != y_side))(lambda xs=xs, c=cross: fetch(xs, c))
-    rims.wait()
 
     def out_copy(i):
         x = jnp.where(low, i, width - layers + i)
@@ -390,7 +412,7 @@
                     wide[t, HMAX : HMAX + rows, :] = snaps[t, at].astype(F32)
                     wide[t, 0:HMAX, :] = rim
                     wide[t, HMAX + rows :, :] = rim
-                    term = wide[t, pl.ds(HMAX - off_y, rows), :] * ps[NT - 1 - t, mine]
+                    term = wide[t, pl.ds(HMAX - off_y, rows), :] * p_rims[NT - 1 - t, mine]
                     result = term if result is None else result + term
             total[i] = result
             out_copy(i).start()
@@ -404,21 +426,20 @@
     return pl.pallas_call(
         rim_kernel,
         out_shape=jax.ShapeDtypeStruct(image.shape, F32),
-        in_specs=[SMEM] + [HBM] * 8,
+        in_specs=[SMEM] + [HBM] * 6 + [VMEM, HBM],
         out_specs=HBM,
         input_output_aliases={8: 0},
         scratch_shapes=[
             pltpu.VMEM((NT, HMAX, rows, depth), BF16),
             pltpu.VMEM((2 * HMAX, 16, depth), BF16),
-            pltpu.VMEM((NT, HMAX, rows, depth), F32),
             pltpu.VMEM((NT, rows + 2 * HMAX, depth), F32),
             pltpu.VMEM((HMAX, rows, depth), F32),
-            pltpu.SemaphoreType.DMA((3,)),
+            pltpu.SemaphoreType.DMA((2,)),
             pltpu.SemaphoreType.DMA((HMAX,)),
         ],
-        compiler_params=params(),
+        compiler_params=params(16),
         name="rim_image",
-    )(offs, *halos, *pin((p_rims, image)))
+    )(offs, *halos, *pin((p_rims,), pltpu.VMEM), *pin((image,)))
 
 
 def body(
@@ -458,8 +479,10 @@
     xw = outward(packed, 1, 0)
     ys, same, cross, xs = pack_rest(fields, src_hist, other, packed)
     ys, same, cross = outward(ys, 0, 1), outward(same, 1, 1), outward(cross, 1, -1)
-    xs = outward(after(xs, (same, cross)), 1, 0)
-    bufs, receivers = load(target, fields, packed)
+    factors, receivers = load(target, fields[4:], packed, "load_factors")
+    xs = outward(after(xs, (same, cross, receivers)), 1, 0)
+    states, _ = load(target[:8], fields[:4], receivers[2], "load_states")
+    bufs = (*states, *factors)
     same, cross = (same, swap(same)), (cross, swap(cross))
     halos = (xw, swap(xw), ys, swap(ys)) + same + cross
     p, q, image, p_rims = wave(receivers, rec_data, lag_offs, halos, src_hist, other, bufs)

time: 72 us -> 64.9 us (0.901)
  the two profiles are of different devices: /device:TPU:12 before, /device:TPU:21 now
where the time goes in v3:
time: 64.9 us; the launch traced here: 64.7 us
  Pallas kernels  38.2 us (59%)
  starting transfers between devices  17.2 us (27%)
  waiting for transfers between devices  6.94 us (11%)
  local copies, waits for them, and re-layouts  1.48 us (2%)
  between operations  0.83 us (1%)
    pallas_call x1, Pallas kernels, wave(): pl.pallas_call(wave_kernel, out_shape=(block, block, block, pltpu.VMEM((N...  21.5 us
    ppermute x5, starting transfers between devices, outward(): return lax.ppermute(v, ('gx', 'gy', 'mem'), pairs)  12.2 us
    pallas_call x2, Pallas kernels, load(): pl.pallas_call(load_kernel, out_shape=(pltpu.VMEM((width + 2 * DEEP, rows...  9.43 us
    ppermute x6, starting transfers between devices, swap(): return lax.ppermute(v, 'mem', [(0, 1), (1, 0)])  5.07 us
    ppermute x5, waiting for transfers between devices, outward(): return lax.ppermute(v, ('gx', 'gy', 'mem'), pairs)  4.64 us
    pallas_call x1, Pallas kernels, pack_rest(): pl.pallas_call(pack_rest_kernel, out_shape=(jax.ShapeDtypeStruct((4, widt...  3.47 us
    ppermute x6, waiting for transfers between devices, swap(): return lax.ppermute(v, 'mem', [(0, 1), (1, 0)])  2.3 us
    pallas_call x1, Pallas kernels, pack_x(): pl.pallas_call(pack_x_kernel, out_shape=jax.ShapeDtypeStruct(shape, BF16)...  2.17 us
  transfers between devices with their start and end apart: 11, of which 2 were waited for; matrix products, arithmetic and copies ran while one was open for 0% of the time, Pallas kernels for 57%

profile of v3, /device:TPU:21, one launch (start us, length us, event | category | flops | bytes accessed | tf_op | source)
XLA Modules:
  0.0 64.7 jit_solution(6834769579016853202)
XLA Ops:
  0.6 0.7 %collective-permute-start = (bf16[2,32,128,128]{3,2,1,0:T(8,128)(2,1)}, bf16[2,32,128,128]{3,2,1,0:T(8,128)(2,1)}, u32[]{:S(2)}, u32[]{:S(2)}) collective-permute-start(bf16[2,32,128,128]{3,2,1,0:T(8,128)(2,1)} %refs_8_.3), channel_id=1, source_target_pairs={{0,1},{1,0},{2,3},{3,2},{4,5},{5,4},{6,7},{7,6},{8,9},{9,8},{10,11... | collective-permute-start | bytes 6291464 | tf_op jit(solution)/shard_map/ppermute | solution.py:452
  1.4 2.2 %pack_x.1.refs_10_.refs_4_ = bf16[26,128,128]{2,1,0:T(8,128)(2,1)} custom-call(f32[32,128,128]{2,1,0:T(8,128)} %refs_0_.7, f32[32,128,128]{2,1,0:T(8,128)} %refs_1_.7, f32[32,128,128]{2,1,0:T(8,128)} %refs_2_.7, f32[32,128,128]{2,1,0:T(8,128)} %refs_3_.7, f32[32,128,128]{2,1,0:T(8,128)} %refs_0_.6, f32[32,128,128]{2,1,0:T(8,128)} %refs_1_.6, ...), custom_call_target="tpu_custom_call" | custom-call | tf_op jit(solution)/shard_map/pack_x/pallas_call | solution.py:66
  3.5 3.1 %collective-permute-start.4 = (bf16[26,128,128]{2,1,0:T(8,128)(2,1)}, bf16[26,128,128]{2,1,0:T(8,128)(2,1)S(1)}, u32[]{:S(2)}, u32[]{:S(2)}) collective-permute-start(bf16[26,128,128]{2,1,0:T(8,128)(2,1)} %pack_x.1.refs_10_.refs_4_), channel_id=1, source_target_pairs={{0,8},{2,10},{4,12},{6,14},{8,16},{9,1},{10,18},{11,3},{12,20},{13... | collective-permute-start | bytes 2555912 | tf_op jit(solution)/shard_map/ppermute | solution.py:466
  6.6 0.0 copy-start.5
  6.6 0.0 collective-permute-done.refs_9_
  6.6 3.5 %pack_rest.1 = (bf16[4,32,16,128]{3,2,1,0:T(8,128)(2,1)}, bf16[24,16,128]{2,1,0:T(8,128)(2,1)}, bf16[24,16,128]{2,1,0:T(8,128)(2,1)}, bf16[4,8,128,128]{3,2,1,0:T(8,128)(2,1)}) custom-call(f32[32,128,128]{2,1,0:T(8,128)} %refs_0_.7, f32[32,128,128]{2,1,0:T(8,128)} %refs_1_.7, f32[32,128,128]{2,1,0:T(8,128)} %refs_2_.7, f32[32,128,128]{2,1,0:T(8,128)} %refs_3_.7, ...), custom_call_target="tpu_custom_call" | custom-call | tf_op jit(solution)/shard_map/pack_rest/pallas_call | solution.py:146
  10.1 2.0 %collective-permute-start.1 = (bf16[24,16,128]{2,1,0:T(8,128)(2,1)}, bf16[24,16,128]{2,1,0:T(8,128)(2,1)S(1)}, u32[]{:S(2)}, u32[]{:S(2)}) collective-permute-start(bf16[24,16,128]{2,1,0:T(8,128)(2,1)} %get-tuple-element.25), channel_id=1, source_target_pairs={{0,10},{2,12},{4,14},{8,18},{10,20},{11,1},{12,22},{13,3},{15,5},{... | collective-permute-start | bytes 294920 | tf_op jit(solution)/shard_map/ppermute | solution.py:466
  12.2 2.9 %collective-permute-start.2 = (bf16[24,16,128]{2,1,0:T(8,128)(2,1)}, bf16[24,16,128]{2,1,0:T(8,128)(2,1)S(1)}, u32[]{:S(2)}, u32[]{:S(2)}) collective-permute-start(bf16[24,16,128]{2,1,0:T(8,128)(2,1)} %get-tuple-element.26), channel_id=1, source_target_pairs={{2,8},{4,10},{6,12},{9,3},{10,16},{11,5},{12,18},{13,7},{14,20},{1... | collective-permute-start | bytes 294920 | tf_op jit(solution)/shard_map/ppermute | solution.py:466
  15.1 2.2 %collective-permute-start.6 = (bf16[4,32,16,128]{3,2,1,0:T(8,128)(2,1)}, bf16[4,32,16,128]{3,2,1,0:T(8,128)(2,1)S(1)}, u32[]{:S(2)}, u32[]{:S(2)}) collective-permute-start(bf16[4,32,16,128]{3,2,1,0:T(8,128)(2,1)} %get-tuple-element.31), channel_id=1, source_target_pairs={{0,2},{2,4},{3,1},{4,6},{5,3},{7,5},{8,10},{10,12},{11,9},{12,14},... | collective-permute-start | bytes 1572872 | tf_op jit(solution)/shard_map/ppermute | solution.py:466
  17.4 0.0 copy-start.6
  17.4 4.9 %load_factors.1 = (f32[40,160,128]{2,1,0:T(8,128)S(1)}, f32[40,160,128]{2,1,0:T(8,128)S(1)}, f32[40,160,128]{2,1,0:T(8,128)S(1)}, f32[40,160,128]{2,1,0:T(8,128)...) custom-call(s32[1024]{0:T(1024)S(1)} %fusion.5.target, f32[32,128,128]{2,1,0:T(8,128)} %refs_0_.6, ...), custom_call_target="tpu_custom_call" | custom-call | tf_op jit(solution)/shard_map/load_factors/pallas_call | solution.py:199
  22.2 0.6 copy-done
  22.8 0.0 collective-permute-done.1.refs_4_.refs_2_
  22.8 0.0 collective-permute-done.2.refs_6_.refs_4_
  22.8 1.9 %collective-permute-start.3 = (bf16[4,8,128,128]{3,2,1,0:T(8,128)(2,1)S(1)}, bf16[4,8,128,128]{3,2,1,0:T(8,128)(2,1)S(1)}, u32[]{:S(2)}, u32[]{:S(2)}) collective-permute-start(bf16[4,8,128,128]{3,2,1,0:T(8,128)(2,1)S(1)} %copy-done.6), channel_id=1, source_target_pairs={{0,8},{2,10},{4,12},{6,14},{8,16},{9,1},{10,18},{11,3},{12,20},{13... | collective-permute-start | bytes 3145736 | tf_op jit(solution)/shard_map/ppermute | solution.py:466
  24.8 4.6 %collective-permute-done.4.refs_0_ = bf16[26,128,128]{2,1,0:T(8,128)(2,1)S(1)} collective-permute-done((bf16[26,128,128]{2,1,0:T(8,128)(2,1)}, bf16[26,128,128]{2,1,0:T(8,128)(2,1)S(1)}, u32[]{:S(2)}, u32[]{:S(2)}) %collective-permute-start.4) | collective-permute-done | bytes 852000 | tf_op jit(solution)/shard_map/ppermute | solution.py:466
  29.4 3.3 %collective-permute-start.5 = (bf16[26,128,128]{2,1,0:T(8,128)(2,1)S(1)}, bf16[26,128,128]{2,1,0:T(8,128)(2,1)S(1)}, u32[]{:S(2)}, u32[]{:S(2)}) collective-permute-start(bf16[26,128,128]{2,1,0:T(8,128)(2,1)S(1)} %collective-permute-done.4.refs_0_), channel_id=1, source_target_pairs={{0,1},{1,0},{2,3},{3,2},{4,5},{5,4},{6,7},{7,6},{8,9},{9,8},{10,11... | collective-permute-start | bytes 2555912 | tf_op jit(solution)/shard_map/ppermute | solution.py:452
  32.7 0.0 collective-permute-done.6.refs_2_
  32.7 0.0 collective-permute-start.7
  32.7 0.5 collective-permute-start.8
  33.2 0.0 collective-permute-start.9
  33.2 0.0 copy-start.3
  33.2 4.6 %load_states.1 = (f32[40,160,128]{2,1,0:T(8,128)S(1)}, f32[40,160,128]{2,1,0:T(8,128)S(1)}, f32[40,160,128]{2,1,0:T(8,128)S(1)}, f32[40,160,128]{2,1,0:T(8,128)S...) custom-call(s32[8]{0:T(128)S(1)} %slice.3.target, f32[32,128,128]{2,1,0:T(8,128)} %refs_0_.7, f32[32,128,128]{2,1,0:T(8,128)} %refs_1_.7, ...), custom_call_target="tpu_custom_call" | custom-call | tf_op jit(solution)/shard_map/load_states/pallas_call | solution.py:199
  37.8 0.0 collective-permute-done.5.refs_1_
  37.8 0.0 collective-permute-done.9.refs_7_.refs_5_
  37.8 0.0 collective-permute-done.7.refs_3_
  37.9 0.9 %copy-done.4 = bf16[26,128,128]{2,1,0:T(8,128)(2,1)} copy-done((bf16[26,128,128]{2,1,0:T(8,128)(2,1)}, bf16[26,128,128]{2,1,0:T(8,128)(2,1)S(1)}, u32[]{:S(2)}) %copy-start.4) | copy-done | bytes 851992
  38.7 21.5 %wave.1 = (f32[32,128,128]{2,1,0:T(8,128)}, f32[32,128,128]{2,1,0:T(8,128)}, f32[32,128,128]{2,1,0:T(8,128)}, f32[4,8,128,128]{3,2,1,0:T(8,128)S(1)}, f32[40,160...) custom-call(s32[1]{0:T(128)} %get-tuple-element.27.count, ...), custom_call_target="tpu_custom_call", output_to_operand_aliasing={{4}: (15, {}), {5}: (16, {}), {6}: (17, {}), {7}: (18, {}),... | custom-call | tf_op jit(solution)/shard_map/wave/pallas_call | solution.py:352
  60.2 0.0 collective-permute-done.3.refs_0_
  60.2 0.5 collective-permute-start.10
  60.8 2.3 %collective-permute-done.10.refs_1_ = bf16[4,8,128,128]{3,2,1,0:T(8,128)(2,1)S(1)} collective-permute-done((bf16[4,8,128,128]{3,2,1,0:T(8,128)(2,1)S(1)}, bf16[4,8,128,128]{3,2,1,0:T(8,128)(2,1)S(1)}, u32[]{:S(2)}, u32[]{:S(2)}) %collective-permute-start.10) | collective-permute-done | bytes 1048608 | tf_op jit(solution)/shard_map/ppermute | solution.py:452
  63.1 1.7 %rim_image.1 = f32[32,128,128]{2,1,0:T(8,128)} custom-call(s32[1,2]{1,0:T(1,128)S(1)} %copy-done.3, bf16[4,8,128,128]{3,2,1,0:T(8,128)(2,1)S(1)} %collective-permute-done.3.refs_0_, bf16[4,8,128,128]{3,2,1,0:T(8,128)(2,1)S(1)} %collective-permute-done.10.refs_1_, ...), custom_call_target="tpu_custom_call", output_to_operand_aliasing={{}: (8, {})} | custom-call | tf_op jit(solution)/shard_map/rim_image/pallas_call | solution.py:426
  (12 shorter events, 0.0 us)
Async XLA Ops:
  0.6 6.0 %collective-permute-start = (bf16[2,32,128,128]{3,2,1,0:T(8,128)(2,1)}, bf16[2,32,128,128]{3,2,1,0:T(8,128)(2,1)}, u32[]{:S(2)}, u32[]{:S(2)}) collective-permute-start(bf16[2,32,128,128]{3,2,1,0:T(8,128)(2,1)} %refs_8_.3), channel_id=1, source_target_pairs={{0,1},{1,0},{2,3},{3,2},{4,5},{5,4},{6,7},{7,6},{8,9},{9,8},{10,11... | collective-permute-start | bytes 6291464 | tf_op jit(solution)/shard_map/ppermute | solution.py:452
  3.5 25.9 %collective-permute-start.4 = (bf16[26,128,128]{2,1,0:T(8,128)(2,1)}, bf16[26,128,128]{2,1,0:T(8,128)(2,1)S(1)}, u32[]{:S(2)}, u32[]{:S(2)}) collective-permute-start(bf16[26,128,128]{2,1,0:T(8,128)(2,1)} %pack_x.1.refs_10_.refs_4_), channel_id=1, source_target_pairs={{0,8},{2,10},{4,12},{6,14},{8,16},{9,1},{10,18},{11,3},{12,20},{13... | collective-permute-start | bytes 2555912 | tf_op jit(solution)/shard_map/ppermute | solution.py:466
  6.6 10.7 %copy-start.5 = (s32[1024]{0:T(1024)S(1)}, s32[1024]{0:T(1024)}, u32[]{:S(2)}) copy-start(s32[1024]{0:T(1024)} %param.21) | copy-start | bytes 12292
  10.1 12.7 %collective-permute-start.1 = (bf16[24,16,128]{2,1,0:T(8,128)(2,1)}, bf16[24,16,128]{2,1,0:T(8,128)(2,1)S(1)}, u32[]{:S(2)}, u32[]{:S(2)}) collective-permute-start(bf16[24,16,128]{2,1,0:T(8,128)(2,1)} %get-tuple-element.25), channel_id=1, source_target_pairs={{0,10},{2,12},{4,14},{8,18},{10,20},{11,1},{12,22},{13,3},{15,5},{... | collective-permute-start | bytes 294920 | tf_op jit(solution)/shard_map/ppermute | solution.py:466
  12.2 10.7 %collective-permute-start.2 = (bf16[24,16,128]{2,1,0:T(8,128)(2,1)}, bf16[24,16,128]{2,1,0:T(8,128)(2,1)S(1)}, u32[]{:S(2)}, u32[]{:S(2)}) collective-permute-start(bf16[24,16,128]{2,1,0:T(8,128)(2,1)} %get-tuple-element.26), channel_id=1, source_target_pairs={{2,8},{4,10},{6,12},{9,3},{10,16},{11,5},{12,18},{13,7},{14,20},{1... | collective-permute-start | bytes 294920 | tf_op jit(solution)/shard_map/ppermute | solution.py:466
  15.1 17.6 %collective-permute-start.6 = (bf16[4,32,16,128]{3,2,1,0:T(8,128)(2,1)}, bf16[4,32,16,128]{3,2,1,0:T(8,128)(2,1)S(1)}, u32[]{:S(2)}, u32[]{:S(2)}) collective-permute-start(bf16[4,32,16,128]{3,2,1,0:T(8,128)(2,1)} %get-tuple-element.31), channel_id=1, source_target_pairs={{0,2},{2,4},{3,1},{4,6},{5,3},{7,5},{8,10},{10,12},{11,9},{12,14},... | collective-permute-start | bytes 1572872 | tf_op jit(solution)/shard_map/ppermute | solution.py:466
  17.4 5.5 %copy-start.6 = (bf16[4,8,128,128]{3,2,1,0:T(8,128)(2,1)S(1)}, bf16[4,8,128,128]{3,2,1,0:T(8,128)(2,1)}, u32[]{:S(2)}) copy-start(bf16[4,8,128,128]{3,2,1,0:T(8,128)(2,1)} %get-tuple-element.30) | copy-start | bytes 3145732
  22.2 0.6 copy-start
  22.8 37.4 %collective-permute-start.3 = (bf16[4,8,128,128]{3,2,1,0:T(8,128)(2,1)S(1)}, bf16[4,8,128,128]{3,2,1,0:T(8,128)(2,1)S(1)}, u32[]{:S(2)}, u32[]{:S(2)}) collective-permute-start(bf16[4,8,128,128]{3,2,1,0:T(8,128)(2,1)S(1)} %copy-done.6), channel_id=1, source_target_pairs={{0,8},{2,10},{4,12},{6,14},{8,16},{9,1},{10,18},{11,3},{12,20},{13... | collective-permute-start | bytes 3145736 | tf_op jit(solution)/shard_map/ppermute | solution.py:466
  29.4 8.4 %collective-permute-start.5 = (bf16[26,128,128]{2,1,0:T(8,128)(2,1)S(1)}, bf16[26,128,128]{2,1,0:T(8,128)(2,1)S(1)}, u32[]{:S(2)}, u32[]{:S(2)}) collective-permute-start(bf16[26,128,128]{2,1,0:T(8,128)(2,1)S(1)} %collective-permute-done.4.refs_0_), channel_id=1, source_target_pairs={{0,1},{1,0},{2,3},{3,2},{4,5},{5,4},{6,7},{7,6},{8,9},{9,8},{10,11... | collective-permute-start | bytes 2555912 | tf_op jit(solution)/shard_map/ppermute | solution.py:452
  32.7 5.2 %collective-permute-start.7 = (bf16[4,32,16,128]{3,2,1,0:T(8,128)(2,1)S(1)}, bf16[4,32,16,128]{3,2,1,0:T(8,128)(2,1)S(1)}, u32[]{:S(2)}, u32[]{:S(2)}) collective-permute-start(bf16[4,32,16,128]{3,2,1,0:T(8,128)(2,1)S(1)} %collective-permute-done.6.refs_2_), channel_id=1, source_target_pairs={{0,1},{1,0},{2,3},{3,2},{4,5},{5,4},{6,7},{7,6},{8,9},{9,8},{10,11... | collective-permute-start | bytes 1572872 | tf_op jit(solution)/shard_map/ppermute | solution.py:452
  32.7 5.1 %collective-permute-start.8 = (bf16[24,16,128]{2,1,0:T(8,128)(2,1)S(1)}, bf16[24,16,128]{2,1,0:T(8,128)(2,1)S(1)}, u32[]{:S(2)}, u32[]{:S(2)}) collective-permute-start(bf16[24,16,128]{2,1,0:T(8,128)(2,1)S(1)} %collective-permute-done.1.refs_4_.refs_2_), channel_id=1, source_target_pairs={{0,1},{1,0},{2,3},{3,2},{4,5},{5,4},{6,7},{7,6},{8,9},{9,8},{10,11... | collective-permute-start | bytes 294920 | tf_op jit(solution)/shard_map/ppermute | solution.py:452
  33.2 4.6 %collective-permute-start.9 = (bf16[24,16,128]{2,1,0:T(8,128)(2,1)S(1)}, bf16[24,16,128]{2,1,0:T(8,128)(2,1)S(1)}, u32[]{:S(2)}, u32[]{:S(2)}) collective-permute-start(bf16[24,16,128]{2,1,0:T(8,128)(2,1)S(1)} %collective-permute-done.2.refs_6_.refs_4_), channel_id=1, source_target_pairs={{0,1},{1,0},{2,3},{3,2},{4,5},{5,4},{6,7},{7,6},{8,9},{9,8},{10,11... | collective-permute-start | bytes 294920 | tf_op jit(solution)/shard_map/ppermute | solution.py:452
  33.2 5.5 %copy-start.1 = (s32[1028]{0:T(1024)S(1)}, s32[1028]{0:T(1024)}, u32[]{:S(2)}) copy-start(s32[1028]{0:T(1024)} %copy-done) | copy-start | bytes 12340
  33.2 5.5 %copy-start.2 = (f32[4,1024]{1,0:T(4,128)S(1)}, f32[4,1024]{1,0:T(4,128)}, u32[]{:S(2)}) copy-start(f32[4,1024]{1,0:T(4,128)} %data.1) | copy-start | bytes 49156
  33.2 5.5 %copy-start.3 = (s32[1,2]{1,0:T(1,128)S(1)}, s32[1,2]{1,0:T(1,128)}, u32[]{:S(2)}) copy-start(s32[1,2]{1,0:T(1,128)} %offs.3) | copy-start | bytes 28
  37.8 0.9 %copy-start.4 = (bf16[26,128,128]{2,1,0:T(8,128)(2,1)}, bf16[26,128,128]{2,1,0:T(8,128)(2,1)S(1)}, u32[]{:S(2)}) copy-start(bf16[26,128,128]{2,1,0:T(8,128)(2,1)S(1)} %collective-permute-done.5.refs_1_) | copy-start | bytes 2555908
  60.2 2.8 %collective-permute-start.10 = (bf16[4,8,128,128]{3,2,1,0:T(8,128)(2,1)S(1)}, bf16[4,8,128,128]{3,2,1,0:T(8,128)(2,1)S(1)}, u32[]{:S(2)}, u32[]{:S(2)}) collective-permute-start(bf16[4,8,128,128]{3,2,1,0:T(8,128)(2,1)S(1)} %collective-permute-done.3.refs_0_), channel_id=1, source_target_pairs={{0,1},{1,0},{2,3},{3,2},{4,5},{5,4},{6,7},{7,6},{8,9},{9,8},{10,11... | collective-permute-start | bytes 3145736 | tf_op jit(solution)/shard_map/ppermute | solution.py:452

commit v4 on v3

v4 whole, which is shorter than its diff:
```python
import functools

import jax
import jax.numpy as jnp
from jax import lax
from jax.experimental import pallas as pl
from jax.experimental.pallas import tpu as pltpu
from jax.sharding import PartitionSpec as P

NT = 4
HMAX = 8
DEEP = NT
ROW0 = 16
GROUP = 4
HEAD = 8
F32 = jnp.float32
BF16 = jnp.bfloat16
HBM = pl.BlockSpec(memory_space=pltpu.HBM)
SMEM = pl.BlockSpec(memory_space=pltpu.SMEM)
VMEM = pl.BlockSpec(memory_space=pltpu.VMEM)
DEPTHS = (DEEP, DEEP) + (DEEP - 1,) * 6
STARTS = tuple(sum(DEPTHS[:i]) for i in range(8))
SENT = tuple(d - 1 for d in DEPTHS)
SENT_AT = tuple(sum(SENT[:i]) for i in range(8))
AHEAD = sum(SENT)
LAYERS = AHEAD + 3


def pin(arrays, space=pltpu.HBM):
    return [pltpu.with_memory_space_constraint(a, space) for a in arrays]


def params(mib=63):
    return pltpu.CompilerParams(vmem_limit_bytes=mib * 2**20)


def copy_all(pairs, sems):
    copies = [pltpu.make_async_copy(a, b, sems.at[i]) for i, (a, b) in enumerate(pairs)]
    for c in copies:
        c.start()
    return copies


def wait_all(copies):
    for c in copies:
        c.wait()


def slopes(v):
    depth = v.shape[-1]
    lane = lax.broadcasted_iota(jnp.int32, v.shape, 1)
    up = jnp.where(lane == depth - 1, 0.0, pltpu.roll(v, depth - 1, 1))
    down = jnp.where(lane == 0, 0.0, pltpu.roll(v, 1, 1))
    return up + down, up - down


def pack_x_kernel(*refs):
    fields, out, stage, small, sems, out_sems = refs[:8], *refs[8:]
    core = lax.axis_index("mem")
    width, rows, _ = fields[0].shape
    pairs = []
    for f, s, d in zip(fields, STARTS, DEPTHS):
        begin = jnp.where(core == 0, width - d, 0)
        pairs.append((f.at[pl.ds(begin, d)], stage.at[pl.ds(s, d)]))
    copies = copy_all(pairs, sems)
    sent = []

    def send(i, begin, size):
        part = pl.ds(begin, size)
        sent.append(pltpu.make_async_copy(small.at[part], out.at[part], out_sems.at[i]))
        sent[-1].start()

    for i in range(8):
        copies[i].wait()
        small[SENT_AT[i] : SENT_AT[i] + SENT[i]] = stage[pl.ds(STARTS[i] + 1 - core, SENT[i])].astype(BF16)
        send(i, SENT_AT[i], SENT[i])
    at = [s + (1 + core if i < 2 else 2 * core) for i, s in enumerate(STARTS)]
    p, q, old_p, old_q, horiz, vert, ratio, tilt = [stage[j] for j in at]
    row = lax.broadcasted_iota(jnp.int32, p.shape, 0)
    beside = jnp.where(row == 0, 0.0, pltpu.roll(p, 1, 0))
    beside += jnp.where(row == rows - 1, 0.0, pltpu.roll(p, rows - 1, 0))
    lateral = stage[at[0] - 1] + stage[at[0] + 1] + beside - 4.0 * p
    mixed = slopes(stage[at[1] + 1])[1] - slopes(stage[at[1] - 1])[1]
    horizontal = horiz * lateral
    upright = vert * ((slopes(q)[0] - 2.0 * q) + (0.25 * tilt) * mixed)
    small[AHEAD] = ((2.0 * p - old_p) + (horizontal + upright)).astype(BF16)
    small[AHEAD + 1] = ((2.0 * q - old_q) + (ratio * horizontal + upright)).astype(BF16)
    both = ratio * horiz
    ends = jnp.where(row == 0, horiz[:1], jnp.where(row == 1, horiz[rows - 1 :], 0.0))
    ends = jnp.where(row == 2, both[:1], jnp.where(row == 3, both[rows - 1 :], ends))
    small[AHEAD + 2] = ends.astype(BF16)
    send(8, AHEAD, 3)
    wait_all(sent)


def pack_x(fields):
    shape = fields[0].shape[1:]
    return pl.pallas_call(
        pack_x_kernel,
        out_shape=jax.ShapeDtypeStruct((LAYERS,) + shape, BF16),
        in_specs=[HBM] * 8,
        out_specs=HBM,
        scratch_shapes=[
            pltpu.VMEM((sum(DEPTHS),) + shape, F32),
            pltpu.VMEM((LAYERS,) + shape, BF16),
            pltpu.SemaphoreType.DMA((8,)),
            pltpu.SemaphoreType.DMA((9,)),
        ],
        compiler_params=params(),
        name="pack_x",
    )(*pin(fields))


def pack_rest_kernel(*refs):
    fields, own, other, _ = refs[:8], *refs[8:11]
    ys, same, cross, xs = refs[11:15]
    stage, snaps, edges, stage_c, snaps_c, mixed, s_ys, s_same, s_cross, sems, out_sems = refs[15:]
    core = lax.axis_index("mem")
    width, rows, _ = fields[0].shape
    near, far = width - DEEP, width - HMAX
    to_low = core == 1
    x_near, x_far = jnp.where(to_low, 0, near), jnp.where(to_low, 0, far)

    def y_at(low, size):
        return pl.multiple_of(jnp.where(low, 0, rows - size), size)

    pairs = []
    for i, f in enumerate(fields):
        pairs.append((f.at[:, pl.ds(y_at(to_low, 8), 8)], stage.at[i]))
        pairs.append((f.at[pl.ds(x_near, DEEP), pl.ds(y_at(~to_low, 8), 8)], stage_c.at[i]))
    for ref, half in ((own, core), (other, 1 - core)):
        pairs.append((ref.at[:, :, pl.ds(y_at(to_low, 16), 16)], snaps.at[half]))
        rim = ref.at[:, pl.ds(x_far, HMAX), pl.ds(y_at(~to_low, 16), 16)]
        pairs.append((rim, snaps_c.at[half]))
        pairs.append((ref.at[:, pl.ds(x_far, HMAX)], edges.at[pl.ds(2 * half, 2)]))
    copies = copy_all(pairs, sems)
    sent = []

    def send(a, b):
        sent.append(pltpu.make_async_copy(a, b, out_sems.at[len(sent)]))
        sent[-1].start()

    wait_all(copies[:16])
    skip, skip_c = jnp.where(to_low, 0, 4), jnp.where(to_low, 4, 0)
    for slab in range(2):
        for i in range(4):
            at = pl.ds(4 * i, 4)
            mixed[:width, at, :] = stage[4 * slab + i, :, pl.ds(skip, 4), :]
            mixed[width : width + DEEP, at, :] = stage_c[4 * slab + i, :, pl.ds(skip_c, 4), :]
        s_ys[slab] = mixed[:width].astype(BF16)
        s_cross[slab * DEEP : (slab + 1) * DEEP] = mixed[width : width + DEEP].astype(BF16)
    wait_all(copies[16:])
    for pair in range(2):
        for i in range(2):
            at = slice(8 * i, 8 * i + 8)
            both = snaps[pair, i].astype(F32)
            mixed[:width, at, :] = jnp.where(to_low, both[:, :8], both[:, 8:])
            both = snaps_c[pair, i].astype(F32)
            mixed[width : width + HMAX, at, :] = jnp.where(to_low, both[:, 8:], both[:, :8])
        s_ys[2 + pair] = mixed[:width].astype(BF16)
        begin = 2 * DEEP + pair * HMAX
        s_cross[begin : begin + HMAX] = mixed[width : width + HMAX].astype(BF16)
    send(s_ys, ys)
    send(s_cross, cross)
    send(edges, xs)
    for slab in range(2):
        begin = slab * DEEP
        s_same[begin : begin + DEEP] = s_ys[slab, pl.ds(x_near, DEEP)]
        begin = 2 * DEEP + slab * HMAX
        s_same[begin : begin + HMAX] = s_ys[2 + slab, pl.ds(x_far, HMAX)]
    send(s_same, same)
    wait_all(sent)


def pack_rest(fields, own, other, earlier):
    width, rows, depth = fields[0].shape
    corner = (2 * DEEP + 2 * HMAX, 16, depth)
    return pl.pallas_call(
        pack_rest_kernel,
        out_shape=(
            jax.ShapeDtypeStruct((4, width, 16, depth), BF16),
            jax.ShapeDtypeStruct(corner, BF16),
            jax.ShapeDtypeStruct(corner, BF16),
            jax.ShapeDtypeStruct((NT, HMAX, rows, depth), BF16),
        ),
        in_specs=[HBM] * 11,
        out_specs=(HBM,) * 4,
        scratch_shapes=[
            pltpu.VMEM((8, width, 8, depth), F32),
            pltpu.VMEM((2, 2, width, 16, depth), BF16),
            pltpu.VMEM((NT, HMAX, rows, depth), BF16),
            pltpu.VMEM((8, DEEP, 8, depth), F32),
            pltpu.VMEM((2, 2, HMAX, 16, depth), BF16),
            pltpu.VMEM((width + HMAX, 16, depth), F32),
            pltpu.VMEM((4, width, 16, depth), BF16),
            pltpu.VMEM(corner, BF16),
            pltpu.VMEM(corner, BF16),
            pltpu.SemaphoreType.DMA((22,)),
            pltpu.SemaphoreType.DMA((4,)),
        ],
        compiler_params=params(),
        name="pack_rest",
    )(*pin((*fields, own, other, earlier)))


def load_kernel(target, *refs):
    fields, bufs, (ints, listed, s_target, sems, sem_target, sem_ints) = refs[:8], refs[-14:-6], refs[-6:]
    core = lax.axis_index("mem")
    n = target.shape[0] - 4
    fetch = pltpu.make_async_copy(target, s_target, sem_target)
    fetch.start()
    width, rows, _ = fields[0].shape
    inner = width // 2 + DEEP
    pairs = []
    for f, b in zip(fields, bufs):
        to = b.at[pl.ds(DEEP * (1 - core), inner), pl.ds(ROW0, rows)]
        pairs.append((f.at[pl.ds((width - inner) * core, inner)], to))
    copies = copy_all(pairs, sems)
    fetch.wait()

    def one(r, at):
        place = s_target[r]
        listed[at] = r
        listed[at + n + GROUP] = place
        return at + jnp.where(place >= 0, 1, 0)

    end = lax.fori_loop(0, n, one, jnp.int32(HEAD), unroll=16)
    for i in range(GROUP):
        listed[end + i] = 0
        listed[end + i + n + GROUP] = 0
    listed[0] = (end - HEAD + GROUP - 1) // GROUP
    for i in range(4):
        listed[1 + i] = s_target[n + i]
    save = pltpu.make_async_copy(listed, ints, sem_ints)
    save.start()
    wait_all(copies + [save])


def load(fields, earlier, target):
    width, rows, depth = fields[0].shape
    any_space = pl.BlockSpec(memory_space=pl.ANY)
    n = target.shape[0] - 4
    listed = (HEAD + 2 * (n + GROUP),)
    shape = (width // 2 + 2 * DEEP, rows + 2 * ROW0, depth)
    return pl.pallas_call(
        load_kernel,
        out_shape=(pltpu.VMEM(shape, F32),) * 8 + (jax.ShapeDtypeStruct(listed, jnp.int32),),
        in_specs=[any_space] + [HBM] * 8 + [any_space],
        out_specs=(VMEM,) * 8 + (any_space,),
        scratch_shapes=[
            pltpu.SMEM(listed, jnp.int32),
            pltpu.SMEM((n + 4,), jnp.int32),
            pltpu.SemaphoreType.DMA((8,)),
            pltpu.SemaphoreType.DMA,
            pltpu.SemaphoreType.DMA,
        ],
        compiler_params=params(8),
        name="load",
    )(target, *pin(fields), earlier)


def wave_kernel(ints, amounts, *refs):
    xw, y_own, y_other, same, cross, own, other = refs[:7]
    p_out, q_out, *totals, p_rims = refs[16:21]
    bufs = refs[21:29]
    listed, data, stage, snaps, wide, outer, sem_in = refs[29:]
    core = lax.axis_index("mem")
    half, rows, depth = p_out.shape
    lists = copy_all([(ints, listed), (amounts, data)], sem_in)
    near = pl.ds(core * HMAX, half + HMAX)
    mains = copy_all(
        [
            (own.at[:, near], snaps.at[pl.ds(2 * core, 2)]),
            (other.at[:, near], snaps.at[pl.ds(2 - 2 * core, 2)]),
        ],
        sem_in.at[pl.ds(2, 2)],
    )
    face = core * (half + DEEP)
    inner = half + DEEP
    for f in range(8):
        d = SENT[f]
        to = jnp.where(core == 0, DEEP - d, half + DEEP)
        part = xw[SENT_AT[f] : SENT_AT[f] + d]
        bufs[f][pl.ds(to, d), ROW0 : ROW0 + rows, :] = part.astype(F32)
    for ys, corner, side in ((y_own, same, core), (y_other, cross, 1 - core)):
        to = jnp.where(side == 0, ROW0 - DEEP, ROW0 + rows)
        for slab in range(2):
            part = ys[slab, pl.ds(core * (half - DEEP), inner)]
            stage[pl.ds(DEEP * (1 - core), inner)] = part.astype(F32)
            part = corner[slab * DEEP : slab * DEEP + DEEP]
            stage[pl.ds(face, DEEP)] = part.astype(F32)
            for i in range(4):
                bufs[4 * slab + i][:, pl.ds(to, DEEP), :] = stage[:, 4 * i : 4 * i + 4, :]

    wait_all(lists)
    horiz, vert, ratio, tilt = bufs[4:]
    thin = lax.broadcasted_iota(jnp.int32, (1, depth), 1)

    def step(k, p, q, old_p, old_q):
        low, high = 1 + k, half + 2 * DEEP - 1 - k
        begin, end = (ROW0 - 8, ROW0 + rows + 8) if k < NT - 1 else (ROW0, ROW0 + rows)
        size = 24 if (end - begin) % 24 == 0 else 32 if (end - begin) % 32 == 0 else 8

        def strip(i, _):
            r = pl.multiple_of(begin + i * size, 8)
            at = pl.ds(r, size)
            p_m, p_c, q_c = p[low - 1, at, :], p[low, at, :], q[low, at, :]
            _, d_m = slopes(q[low - 1, at, :])
            s_c, d_c = slopes(q_c)
            for x in range(low, high):
                p_n, q_n = p[x + 1, at, :], q[x + 1, at, :]
                s_n, d_n = slopes(q_n)
                beside = p[x, pl.ds(r - 1, size), :] + p[x, pl.ds(r + 1, size), :]
                lateral = ((p_m + p_n) + beside) - 4.0 * p_c
                q_2 = 2.0 * q_c
                horizontal = horiz[x, at, :] * lateral
                mixed = (0.25 * tilt[x, at, :]) * (d_n - d_m)
                upright = vert[x, at, :] * ((s_c - q_2) + mixed)
                p_new = (2.0 * p_c - old_p[x, at, :]) + (horizontal + upright)
                q_new = (q_2 - old_q[x, at, :]) + (ratio[x, at, :] * horizontal + upright)
                if k < NT - 1:
                    old_p[x, at, :] = p_new
                    old_q[x, at, :] = q_new
                else:
                    out_at = pl.ds(pl.multiple_of(r - ROW0, 8), size)
                    p_out[x - DEEP, out_at, :] = p_new
                    q_out[x - DEEP, out_at, :] = q_new
                p_m, p_c, q_c, s_c, d_m, d_c = p_c, p_n, q_n, s_n, d_c, d_n
            return 0

        lax.fori_loop(0, (end - begin) // size, strip, 0)

    def inject(k, old_p, old_q):
        def group(g, _):
            for i in range(GROUP):
                j = HEAD + g * GROUP + i
                place = listed[j + (listed.shape[0] - HEAD) // 2]
                amount = data[NT - 1 - k, listed[j]]
                x, y, z = place >> 16, (place >> 8) & 255, place & 255
                add = jnp.where(thin == z, amount, 0.0)
                old_p[x, pl.ds(y, 1), :] = old_p[x, pl.ds(y, 1), :] - add
                old_q[x, pl.ds(y, 1), :] = old_q[x, pl.ds(y, 1), :] - add
            return 0

        lax.fori_loop(0, listed[0], group, 0)

    def add_image(k, p, lag):
        off_x, off_y = listed[1 + 2 * lag], listed[2 + 2 * lag]
        t = NT - 1 - k
        pair, part = t // 2, t % 2
        from_own = core == jnp.where(off_y > 0, 0, 1)

        def layer(i, _):
            at = jnp.clip(core * HMAX + i - off_x, 0, half + HMAX - 1)
            slot = i % 4
            mine, others = y_own[2 + pair, core * HMAX + at], y_other[2 + pair, core * HMAX + at]
            rim = jnp.where(from_own, mine.astype(F32), others.astype(F32))
            rim = rim[8 * part : 8 * part + 8]
            wide[slot, HMAX : HMAX + rows, :] = snaps[t, at].astype(F32)
            wide[slot, 0:HMAX, :] = rim
            wide[slot, HMAX + rows :, :] = rim
            term = wide[slot, pl.ds(HMAX - off_y, rows), :] * p[i + DEEP, ROW0 : ROW0 + rows, :]
            totals[lag][i] = term if k == 0 else totals[lag][i] + term
            return 0

        lax.fori_loop(0, half, layer, 0, unroll=4)

    p_now, q_now, p_old, q_old = bufs[:4]
    main = slice(ROW0, ROW0 + rows)
    far = jnp.where(core == 0, DEEP - 3, half + DEEP + 2)
    for buf in (p_old, q_old):
        buf[far, main, :] = jnp.zeros((rows, depth), F32)
    for k in range(NT):
        inject(k, p_old, q_old)
        if k == 0:
            row = lax.broadcasted_iota(jnp.int32, (rows, depth), 0)
            ends = xw[AHEAD + 2].astype(F32)
            before, behind = p_now[far, pl.ds(ROW0 - 1, 1), :], p_now[far, pl.ds(ROW0 + rows, 1), :]
            for i, buf in enumerate((p_old, q_old)):
                value = xw[AHEAD + i].astype(F32) - buf[far, main, :]
                value += jnp.where(row == 0, ends[2 * i : 2 * i + 1] * before, 0.0)
                value += jnp.where(row == rows - 1, ends[2 * i + 1 : 2 * i + 2] * behind, 0.0)
                outer[i] = value
        p_rims[k] = p_now[pl.ds(DEEP + core * HMAX, HMAX), ROW0 : ROW0 + rows, :]
        step(k, p_now, q_now, p_old, q_old)
        if k == 0:
            for i, buf in enumerate((p_old, q_old)):
                buf[far, main, :] = outer[i]
            wait_all(mains)
        for lag in range(2):
            add_image(k, p_now, lag)
        p_now, p_old, q_now, q_old = p_old, p_now, q_old, q_now


def wave(ints, data, halos, own, other, earlier, bufs):
    width, rows, depth = own.shape[1:]
    half = width // 2
    any_space = pl.BlockSpec(memory_space=pl.ANY)
    return pl.pallas_call(
        wave_kernel,
        out_shape=(
            *(pltpu.VMEM((half, rows, depth), F32),) * 4,
            pltpu.VMEM((NT, HMAX, rows, depth), F32),
        )
        + tuple(pltpu.VMEM(b.shape, F32) for b in bufs),
        in_specs=[any_space] * 2 + [VMEM] * 5 + [HBM] * 2 + [any_space] + [VMEM] * 8,
        out_specs=(VMEM,) * 13,
        input_output_aliases={10 + i: 5 + i for i in range(8)},
        scratch_shapes=[
            pltpu.SMEM(ints.shape, jnp.int32),
            pltpu.SMEM(data.shape, F32),
            pltpu.VMEM((half + 2 * DEEP, 16, depth), F32),
            pltpu.VMEM((NT, half + HMAX, rows, depth), BF16),
            pltpu.VMEM((4, rows + 2 * HMAX, depth), F32),
            pltpu.VMEM((2, rows, depth), F32),
            pltpu.SemaphoreType.DMA((4,)),
        ],
        compiler_params=params(8),
        name="wave",
    )(ints, data, *pin(halos, pltpu.VMEM), *pin((own, other)), earlier, *pin(bufs, pltpu.VMEM))[:5]


def merge_kernel(*refs):
    halves, outs, sems = refs[:6], refs[6:9], refs[9]
    core = lax.axis_index("mem")
    half = outs[0].shape[0] // 2
    pairs = []
    for i, out in enumerate(outs):
        pairs.append((halves[2 * i], out.at[pl.ds(half * core, half)]))
        pairs.append((halves[2 * i + 1], out.at[pl.ds(half - half * core, half)]))
    wait_all(copy_all(pairs, sems))


def merge(p, p_other, q, q_other, total, image_other):
    block = jax.ShapeDtypeStruct((2 * p.shape[0],) + p.shape[1:], F32)
    return pl.pallas_call(
        merge_kernel,
        out_shape=(block,) * 3,
        in_specs=[VMEM] * 6,
        out_specs=(HBM,) * 3,
        scratch_shapes=[pltpu.SemaphoreType.DMA((6,))],
        compiler_params=params(8),
        name="merge",
    )(*pin((p, p_other, q, q_other, total, image_other), pltpu.VMEM))


def rim_kernel(offs, offs_other, xs, same, cross, p_rims, _, total, given, wide):
    core = lax.axis_index("mem")
    half, rows, _ = total.shape
    for lag, off in enumerate((offs, offs_other)):
        off_x, off_y = off[0, 0], off[0, 1]
        layers = jnp.maximum(jnp.where(core == 0, off_x, -off_x), 0)
        from_same = core == jnp.where(off_y > 0, 0, 1)

        def layer(i, lag=lag, off_y=off_y, layers=layers, from_same=from_same):
            at = jnp.where(core == 0, HMAX - layers + i, i)
            mine = jnp.where(core == 0, i, HMAX - layers + i)
            result = None
            for pair in range(2):
                place = 2 * DEEP + pair * HMAX + at
                strip = jnp.where(from_same, same[place].astype(F32), cross[place].astype(F32))
                for part in range(2):
                    t = 2 * pair + part
                    rim = strip[8 * part : 8 * part + 8]
                    wide[t, HMAX : HMAX + rows, :] = xs[t, at].astype(F32)
                    wide[t, 0:HMAX, :] = rim
                    wide[t, HMAX + rows :, :] = rim
                    term = wide[t, pl.ds(HMAX - off_y, rows), :] * p_rims[NT - 1 - t, mine]
                    result = term if result is None else result + term
            if lag == 1:
                given[i] = result
            else:
                total[jnp.where(core == 0, i, half - layers + i)] = result

        for i in range(HMAX):
            pl.when(i < layers)(lambda i=i, layer=layer: layer(i))


def rim_image(offs, offs_other, halos, p_rims, total):
    half, rows, depth = total.shape
    return pl.pallas_call(
        rim_kernel,
        out_shape=(
            pltpu.VMEM(total.shape, F32),
            pltpu.VMEM((HMAX, rows, depth), F32),
        ),
        in_specs=[SMEM] * 2 + [VMEM] * 5,
        out_specs=(VMEM, VMEM),
        input_output_aliases={6: 0},
        scratch_shapes=[pltpu.VMEM((NT, rows + 2 * HMAX, depth), F32)],
        compiler_params=params(8),
        name="rim_image",
    )(offs, offs_other, *pin((*halos, p_rims, total), pltpu.VMEM))


def place_kernel(offs, given, _, image, sem_out):
    core = lax.axis_index("mem")
    width = image.shape[0]
    layers = jnp.maximum(jnp.where(core == 0, -offs[0, 0], offs[0, 0]), 0)

    def out_copy(i):
        x = jnp.where(core == 0, width - layers + i, i)
        return pltpu.make_async_copy(given.at[i], image.at[x], sem_out.at[i])

    for i in range(HMAX):
        pl.when(i < layers)(lambda i=i: out_copy(i).start())
    for i in range(HMAX):
        pl.when(i < layers)(lambda i=i: out_copy(i).wait())


def place_rim(offs, given, image):
    return pl.pallas_call(
        place_kernel,
        out_shape=jax.ShapeDtypeStruct(image.shape, F32),
        in_specs=[SMEM, VMEM, HBM],
        out_specs=HBM,
        input_output_aliases={2: 0},
        scratch_shapes=[pltpu.SemaphoreType.DMA((HMAX,))],
        compiler_params=params(8),
        name="place_rim",
    )(offs, *pin((given,), pltpu.VMEM), *pin((image,)))


def body(
    src_hist, rec_p, rec_q, prev_p, prev_q, horiz, vert, ratio, tilt, rec_pos, rec_data, lag_offs
):
    width, rows, depth = rec_p.shape
    fields = (rec_p, rec_q, prev_p, prev_q, horiz, vert, ratio, tilt)

    def swap(v):
        return lax.ppermute(v, "mem", [(0, 1), (1, 0)])

    def after(v, earlier):
        return lax.optimization_barrier((v, earlier))[0]

    def outward(v, step_x, step_y):
        count_x, count_y = lax.axis_size("gx"), lax.axis_size("gy")
        pairs = []
        for x in range(count_x):
            for y in range(count_y):
                for core, sign in ((0, 1), (1, -1)):
                    to_x, to_y = x + sign * step_x, y + sign * step_y
                    if 0 <= to_x < count_x and 0 <= to_y < count_y:
                        pairs.append(((x * count_y + y) * 2 + core, (to_x * count_y + to_y) * 2 + core))
        return lax.ppermute(v, ("gx", "gy", "mem"), pairs)

    plane = rows * lax.axis_size("gy") * depth
    half = width // 2
    x = rec_pos // plane - lax.axis_index("gx") * width - lax.axis_index("mem") * half + DEEP
    rest = rec_pos % plane
    y = rest // depth - lax.axis_index("gy") * rows + ROW0
    z = rest % depth
    inside = (x >= 0) & (x < half + 2 * DEEP)
    inside &= (y >= ROW0 - DEEP) & (y < ROW0 + rows + DEEP)
    target = jnp.where(inside, (x << 16) + (y << 8) + z, -1)
    offs_other = swap(lag_offs)
    target = jnp.concatenate([target, lag_offs[0], offs_other[0]])

    other = swap(src_hist)
    packed = pack_x(fields)
    xw = outward(packed, 1, 0)
    ys, same, cross, xs = pack_rest(fields, src_hist, other, packed)
    ys, same, cross = outward(ys, 0, 1), outward(same, 1, 1), outward(cross, 1, -1)
    *bufs, ints = load(fields, packed, target)
    xs = outward(after(xs, (same, cross)), 1, 0)
    halos = (xw, ys, swap(ys), same, cross)
    token = swap(xw[0, :16])
    p, q, total, total_other, p_rims = wave(ints, rec_data, halos, src_hist, other, token, bufs)
    parts = (swap(p), swap(q), swap(total_other))
    total, given = rim_image(lag_offs, offs_other, (after(xs, p), same, cross), p_rims, total)
    p, q, image = merge(p, parts[0], q, parts[1], total, parts[2])
    image = place_rim(lag_offs, swap(given), image)
    return image[None], p, q


def solution(mesh):
    block = P("gx", "gy", None)
    return jax.shard_map(
        body,
        mesh=mesh,
        in_specs=(P("mem", "gx", "gy", None),) + (block,) * 8 + (P(), P(), P("mem", None)),
        out_specs=(P("mem", "gx", "gy", None), block, block),
        check_vma=False,
    )
```

time: 64.9 us -> 58.6 us (0.903)
  the two profiles are of different devices: /device:TPU:21 before, /device:TPU:0 now
where the time goes in v4:
time: 58.6 us; the launch traced here: 57.8 us
  Pallas kernels  27 us (46%)
  starting transfers between devices  22 us (38%)
  waiting for transfers between devices  7.13 us (12%)
  between operations  0.82 us (1%)
  local copies, waits for them, and re-layouts  0.78 us (1%)
    ppermute x5, starting transfers between devices, outward(): return lax.ppermute(v, ('gx', 'gy', 'mem'), pairs)  19.8 us
    pallas_call x1, Pallas kernels, wave(): pl.pallas_call(wave_kernel, out_shape=(*(pltpu.VMEM((half, rows, depth),...  12.1 us
    pallas_call x1, Pallas kernels, load(): pl.pallas_call(load_kernel, out_shape=(pltpu.VMEM(shape, F32),) * 8 + (ja...  4.4 us
    ppermute x5, waiting for transfers between devices, outward(): return lax.ppermute(v, ('gx', 'gy', 'mem'), pairs)  3.79 us
    pallas_call x1, Pallas kernels, pack_rest(): pl.pallas_call(pack_rest_kernel, out_shape=(jax.ShapeDtypeStruct((4, widt...  3.45 us
    ppermute x8, waiting for transfers between devices, swap(): return lax.ppermute(v, 'mem', [(0, 1), (1, 0)])  3.34 us
    pallas_call x1, Pallas kernels, merge(): pl.pallas_call(merge_kernel, out_shape=(block,) * 3, in_specs=[VMEM] * 6,...  2.72 us
    pallas_call x1, Pallas kernels, pack_x(): pl.pallas_call(pack_x_kernel, out_shape=jax.ShapeDtypeStruct((LAYERS,) +...  2.36 us
  transfers between devices with their start and end apart: 13, of which 5 were waited for; matrix products, arithmetic and copies ran while one was open for 1% of the time, Pallas kernels for 46%

profile of v4, /device:TPU:0, one launch (start us, length us, event | category | flops | bytes accessed | tf_op | source)
XLA Modules:
  0.0 57.8 jit_solution(16070312139643348692)
XLA Ops:
  0.6 0.5 collective-permute-start.1
  1.1 2.4 %pack_x.1.refs_10_.refs_8_ = bf16[21,128,128]{2,1,0:T(8,128)(2,1)} custom-call(f32[32,128,128]{2,1,0:T(8,128)} %refs_0_.5, f32[32,128,128]{2,1,0:T(8,128)} %refs_1_.5, f32[32,128,128]{2,1,0:T(8,128)} %refs_2_.5, f32[32,128,128]{2,1,0:T(8,128)} %refs_3_.5, f32[32,128,128]{2,1,0:T(8,128)} %refs_4_.5, f32[32,128,128]{2,1,0:T(8,128)} %refs_5_.6, ...), custom_call_target="tpu_custom_call" | custom-call | tf_op jit(solution)/shard_map/pack_x/pallas_call | solution.py:98
  3.5 0.0 copy-start.2
  3.5 0.0 copy-start.3
  3.5 0.0 copy-start
  3.5 5.4 %collective-permute-start.5 = (bf16[21,128,128]{2,1,0:T(8,128)(2,1)}, bf16[21,128,128]{2,1,0:T(8,128)(2,1)}, u32[]{:S(2)}, u32[]{:S(2)}) collective-permute-start(bf16[21,128,128]{2,1,0:T(8,128)(2,1)} %pack_x.1.refs_10_.refs_8_), channel_id=1, source_target_pairs={{0,8},{2,10},{4,12},{6,14},{8,16},{9,1},{10,18},{11,3},{12,20},{13... | collective-permute-start | bytes 2064392 | tf_op jit(solution)/shard_map/ppermute | solution.py:545
  9.0 0.0 collective-permute-done.1.refs_9_.refs_6_
  9.0 3.4 %pack_rest.1 = (bf16[4,32,16,128]{3,2,1,0:T(8,128)(2,1)}, bf16[24,16,128]{2,1,0:T(8,128)(2,1)}, bf16[24,16,128]{2,1,0:T(8,128)(2,1)}, bf16[4,8,128,128]{3,2,1,0:T(8,128)(2,1)}) custom-call(f32[32,128,128]{2,1,0:T(8,128)} %refs_0_.5, f32[32,128,128]{2,1,0:T(8,128)} %refs_1_.5, f32[32,128,128]{2,1,0:T(8,128)} %refs_2_.5, f32[32,128,128]{2,1,0:T(8,128)} %refs_3_.5, ...), custom_call_target="tpu_custom_call" | custom-call | tf_op jit(solution)/shard_map/pack_rest/pallas_call | solution.py:178
  12.4 3.5 %collective-permute-start.6 = (bf16[4,32,16,128]{3,2,1,0:T(8,128)(2,1)}, bf16[4,32,16,128]{3,2,1,0:T(8,128)(2,1)S(1)}, u32[]{:S(2)}, u32[]{:S(2)}) collective-permute-start(bf16[4,32,16,128]{3,2,1,0:T(8,128)(2,1)} %get-tuple-element.33), channel_id=1, source_target_pairs={{0,2},{2,4},{3,1},{4,6},{5,3},{7,5},{8,10},{10,12},{11,9},{12,14},... | collective-permute-start | bytes 1572872 | tf_op jit(solution)/shard_map/ppermute | solution.py:545
  16.0 3.5 %collective-permute-start.2 = (bf16[24,16,128]{2,1,0:T(8,128)(2,1)}, bf16[24,16,128]{2,1,0:T(8,128)(2,1)S(1)}, u32[]{:S(2)}, u32[]{:S(2)}) collective-permute-start(bf16[24,16,128]{2,1,0:T(8,128)(2,1)} %get-tuple-element.29), channel_id=1, source_target_pairs={{0,10},{2,12},{4,14},{8,18},{10,20},{11,1},{12,22},{13,3},{15,5},{... | collective-permute-start | bytes 294920 | tf_op jit(solution)/shard_map/ppermute | solution.py:545
  19.5 0.7 %collective-permute-start.3 = (bf16[24,16,128]{2,1,0:T(8,128)(2,1)}, bf16[24,16,128]{2,1,0:T(8,128)(2,1)S(1)}, u32[]{:S(2)}, u32[]{:S(2)}) collective-permute-start(bf16[24,16,128]{2,1,0:T(8,128)(2,1)} %get-tuple-element.30), channel_id=1, source_target_pairs={{2,8},{4,10},{6,12},{9,3},{10,16},{11,5},{12,18},{13,7},{14,20},{1... | collective-permute-start | bytes 294920 | tf_op jit(solution)/shard_map/ppermute | solution.py:545
  20.2 2.7 %collective-permute-done.6.refs_1_ = bf16[4,32,16,128]{3,2,1,0:T(8,128)(2,1)S(1)} collective-permute-done((bf16[4,32,16,128]{3,2,1,0:T(8,128)(2,1)}, bf16[4,32,16,128]{3,2,1,0:T(8,128)(2,1)S(1)}, u32[]{:S(2)}, u32[]{:S(2)}) %collective-permute-start.6) | collective-permute-done | bytes 524320 | tf_op jit(solution)/shard_map/ppermute | solution.py:545
  22.9 0.0 collective-permute-start.7
  22.9 1.0 %collective-permute-done.2.refs_3_.same = bf16[24,16,128]{2,1,0:T(8,128)(2,1)S(1)} collective-permute-done((bf16[24,16,128]{2,1,0:T(8,128)(2,1)}, bf16[24,16,128]{2,1,0:T(8,128)(2,1)S(1)}, u32[]{:S(2)}, u32[]{:S(2)}) %collective-permute-start.2) | collective-permute-done | bytes 98336 | tf_op jit(solution)/shard_map/ppermute | solution.py:545
  24.0 0.0 collective-permute-done.3.refs_4_.cross
  24.0 6.6 %collective-permute-start.4 = (bf16[4,8,128,128]{3,2,1,0:T(8,128)(2,1)}, bf16[4,8,128,128]{3,2,1,0:T(8,128)(2,1)S(1)}, u32[]{:S(2)}, u32[]{:S(2)}) collective-permute-start(bf16[4,8,128,128]{3,2,1,0:T(8,128)(2,1)} %get-tuple-element.31), channel_id=1, source_target_pairs={{0,8},{2,10},{4,12},{6,14},{8,16},{9,1},{10,18},{11,3},{12,20},{13... | collective-permute-start | bytes 3145736 | tf_op jit(solution)/shard_map/ppermute | solution.py:545
  30.6 0.1 collective-permute-start
  30.7 0.7 %slice_bitcast_fusion = bf16[16,128]{1,0:T(8,128)(2,1)S(1)} fusion(bf16[21,128,128]{2,1,0:T(8,128)(2,1)} %collective-permute-done.5.refs_0_), kind=kLoop, calls=%fused_computation.17 | loop fusion | bytes 8192 | tf_op jit(solution)/shard_map/squeeze | solution.py:567
  31.4 0.5 collective-permute-start.8
  31.9 0.1 concatenate.3.target
  32.0 4.4 %load.1 = (f32[24,160,128]{2,1,0:T(8,128)S(1)}, f32[24,160,128]{2,1,0:T(8,128)S(1)}, f32[24,160,128]{2,1,0:T(8,128)S(1)}, f32[24,160,128]{2,1,0:T(8,128)S(1)}, f...) custom-call(s32[1028]{0:T(1024)S(1)} %concatenate.3.target, ...), custom_call_target="tpu_custom_call" | custom-call | tf_op jit(solution)/shard_map/load/pallas_call | solution.py:245
  36.4 12.1 %wave.1 = (f32[16,128,128]{2,1,0:T(8,128)S(1)}, f32[16,128,128]{2,1,0:T(8,128)S(1)}, f32[16,128,128]{2,1,0:T(8,128)S(1)}, f32[16,128,128]{2,1,0:T(8,128)S(1)}, f...) custom-call(s32[2064]{0:T(1024)S(1)} %get-tuple-element.32.ints, ...), custom_call_target="tpu_custom_call", output_to_operand_aliasing={{5}: (10, {}), {6}: (11, {}), {7}: (12, {}), {8}: (13, {}),... | custom-call | tf_op jit(solution)/shard_map/wave/pallas_call | solution.py:399
  48.5 0.6 %collective-permute-start.12 = (f32[16,128,128]{2,1,0:T(8,128)S(1)}, f32[16,128,128]{2,1,0:T(8,128)S(1)}, u32[]{:S(2)}, u32[]{:S(2)}) collective-permute-start(f32[16,128,128]{2,1,0:T(8,128)S(1)} %get-tuple-element.49), channel_id=1, source_target_pairs={{0,1},{1,0},{2,3},{3,2},{4,5},{5,4},{6,7},{7,6},{8,9},{9,8},{10,11... | collective-permute-start | bytes 3145736 | tf_op jit(solution)/shard_map/ppermute | solution.py:531
  49.2 0.1 collective-permute-start.11
  49.2 0.4 collective-permute-start.10
  49.7 1.4 %rim_image.1 = (f32[16,128,128]{2,1,0:T(8,128)S(1)}, f32[8,128,128]{2,1,0:T(8,128)S(1)}) custom-call(s32[1,2]{1,0:T(1,128)S(1)} %copy-done.2, s32[1,2]{1,0:T(1,128)S(1)} %collective-permute-done.offs_other, bf16[4,8,128,128]{3,2,1,0:T(8,128)(2,1)S(1)} %collective-permute-done.4.xs, ...), custom_call_target="tpu_custom_call", output_to_operand_aliasing={{0}: (6, {})} | custom-call | tf_op jit(solution)/shard_map/rim_image/pallas_call | solution.py:481
  51.0 0.1 collective-permute-start.9
  51.1 0.3 collective-permute-done.12.refs_5_
  51.5 1.5 %collective-permute-done.11.refs_3_ = f32[16,128,128]{2,1,0:T(8,128)S(1)} collective-permute-done((f32[16,128,128]{2,1,0:T(8,128)S(1)}, f32[16,128,128]{2,1,0:T(8,128)S(1)}, u32[]{:S(2)}, u32[]{:S(2)}) %collective-permute-start.11) | collective-permute-done | bytes 1048608 | tf_op jit(solution)/shard_map/ppermute | solution.py:531
  52.9 1.5 %collective-permute-done.10.refs_1_ = f32[16,128,128]{2,1,0:T(8,128)S(1)} collective-permute-done((f32[16,128,128]{2,1,0:T(8,128)S(1)}, f32[16,128,128]{2,1,0:T(8,128)S(1)}, u32[]{:S(2)}, u32[]{:S(2)}) %collective-permute-start.10) | collective-permute-done | bytes 1048608 | tf_op jit(solution)/shard_map/ppermute | solution.py:531
  54.4 2.7 %merge.1 = (f32[32,128,128]{2,1,0:T(8,128)}, f32[32,128,128]{2,1,0:T(8,128)}, f32[32,128,128]{2,1,0:T(8,128)}) custom-call(f32[16,128,128]{2,1,0:T(8,128)S(1)} %get-tuple-element.42.refs_0_, f32[16,128,128]{2,1,0:T(8,128)S(1)} %collective-permute-done.10.refs_1_, f32[16,128,128]{2,1,0:T(8,128)S(1)} %get-tuple-element.47.refs_2_, ...), custom_call_target="tpu_custom_call" | custom-call | tf_op jit(solution)/shard_map/merge/pallas_call | solution.py:436
  57.2 0.6 %place_rim.1 = f32[32,128,128]{2,1,0:T(8,128)} custom-call(s32[1,2]{1,0:T(1,128)S(1)} %copy-done.2, f32[8,128,128]{2,1,0:T(8,128)S(1)} %collective-permute-done.9.given, f32[32,128,128]{2,1,0:T(8,128)} %get-tuple-element.50._), custom_call_target="tpu_custom_call", output_to_operand_aliasing={{}: (2, {})} | custom-call | tf_op jit(solution)/shard_map/place_rim/pallas_call | solution.py:512
  (12 shorter events, 0.1 us)
Async XLA Ops:
  0.6 8.4 %collective-permute-start.1 = (bf16[2,32,128,128]{3,2,1,0:T(8,128)(2,1)}, bf16[2,32,128,128]{3,2,1,0:T(8,128)(2,1)}, u32[]{:S(2)}, u32[]{:S(2)}) collective-permute-start(bf16[2,32,128,128]{3,2,1,0:T(8,128)(2,1)} %refs_5_.7), channel_id=1, source_target_pairs={{0,1},{1,0},{2,3},{3,2},{4,5},{5,4},{6,7},{7,6},{8,9},{9,8},{10,11... | collective-permute-start | bytes 6291464 | tf_op jit(solution)/shard_map/ppermute | solution.py:531
  3.5 27.1 %copy-start.2 = (s32[1,2]{1,0:T(1,128)S(1)}, s32[1,2]{1,0:T(1,128)}, u32[]{:S(2)}) copy-start(s32[1,2]{1,0:T(1,128)} %offs.3) | copy-start | bytes 28
  3.5 28.3 %copy-start.3 = (s32[1024]{0:T(1024)S(1)}, s32[1024]{0:T(1024)}, u32[]{:S(2)}) copy-start(s32[1024]{0:T(1024)} %param.21) | copy-start | bytes 12292
  3.5 28.4 %copy-start = (bf16[21,128,128]{2,1,0:T(8,128)(2,1)S(1)}, bf16[21,128,128]{2,1,0:T(8,128)(2,1)}, u32[]{:S(2)}) copy-start(bf16[21,128,128]{2,1,0:T(8,128)(2,1)} %pack_x.1.refs_10_.refs_8_) | copy-start | bytes 2064388
  3.5 27.1 %collective-permute-start.5 = (bf16[21,128,128]{2,1,0:T(8,128)(2,1)}, bf16[21,128,128]{2,1,0:T(8,128)(2,1)}, u32[]{:S(2)}, u32[]{:S(2)}) collective-permute-start(bf16[21,128,128]{2,1,0:T(8,128)(2,1)} %pack_x.1.refs_10_.refs_8_), channel_id=1, source_target_pairs={{0,8},{2,10},{4,12},{6,14},{8,16},{9,1},{10,18},{11,3},{12,20},{13... | collective-permute-start | bytes 2064392 | tf_op jit(solution)/shard_map/ppermute | solution.py:545
  12.4 10.5 %collective-permute-start.6 = (bf16[4,32,16,128]{3,2,1,0:T(8,128)(2,1)}, bf16[4,32,16,128]{3,2,1,0:T(8,128)(2,1)S(1)}, u32[]{:S(2)}, u32[]{:S(2)}) collective-permute-start(bf16[4,32,16,128]{3,2,1,0:T(8,128)(2,1)} %get-tuple-element.33), channel_id=1, source_target_pairs={{0,2},{2,4},{3,1},{4,6},{5,3},{7,5},{8,10},{10,12},{11,9},{12,14},... | collective-permute-start | bytes 1572872 | tf_op jit(solution)/shard_map/ppermute | solution.py:545
  16.0 8.0 %collective-permute-start.2 = (bf16[24,16,128]{2,1,0:T(8,128)(2,1)}, bf16[24,16,128]{2,1,0:T(8,128)(2,1)S(1)}, u32[]{:S(2)}, u32[]{:S(2)}) collective-permute-start(bf16[24,16,128]{2,1,0:T(8,128)(2,1)} %get-tuple-element.29), channel_id=1, source_target_pairs={{0,10},{2,12},{4,14},{8,18},{10,20},{11,1},{12,22},{13,3},{15,5},{... | collective-permute-start | bytes 294920 | tf_op jit(solution)/shard_map/ppermute | solution.py:545
  19.5 4.5 %collective-permute-start.3 = (bf16[24,16,128]{2,1,0:T(8,128)(2,1)}, bf16[24,16,128]{2,1,0:T(8,128)(2,1)S(1)}, u32[]{:S(2)}, u32[]{:S(2)}) collective-permute-start(bf16[24,16,128]{2,1,0:T(8,128)(2,1)} %get-tuple-element.30), channel_id=1, source_target_pairs={{2,8},{4,10},{6,12},{9,3},{10,16},{11,5},{12,18},{13,7},{14,20},{1... | collective-permute-start | bytes 294920 | tf_op jit(solution)/shard_map/ppermute | solution.py:545
  22.9 13.5 %collective-permute-start.7 = (bf16[4,32,16,128]{3,2,1,0:T(8,128)(2,1)S(1)}, bf16[4,32,16,128]{3,2,1,0:T(8,128)(2,1)S(1)}, u32[]{:S(2)}, u32[]{:S(2)}) collective-permute-start(bf16[4,32,16,128]{3,2,1,0:T(8,128)(2,1)S(1)} %collective-permute-done.6.refs_1_), channel_id=1, source_target_pairs={{0,1},{1,0},{2,3},{3,2},{4,5},{5,4},{6,7},{7,6},{8,9},{9,8},{10,11... | collective-permute-start | bytes 1572872 | tf_op jit(solution)/shard_map/ppermute | solution.py:531
  24.0 25.7 %collective-permute-start.4 = (bf16[4,8,128,128]{3,2,1,0:T(8,128)(2,1)}, bf16[4,8,128,128]{3,2,1,0:T(8,128)(2,1)S(1)}, u32[]{:S(2)}, u32[]{:S(2)}) collective-permute-start(bf16[4,8,128,128]{3,2,1,0:T(8,128)(2,1)} %get-tuple-element.31), channel_id=1, source_target_pairs={{0,8},{2,10},{4,12},{6,14},{8,16},{9,1},{10,18},{11,3},{12,20},{13... | collective-permute-start | bytes 3145736 | tf_op jit(solution)/shard_map/ppermute | solution.py:545
  30.6 1.3 %collective-permute-start = (s32[1,2]{1,0:T(1,128)S(1)}, s32[1,2]{1,0:T(1,128)S(1)}, u32[]{:S(2)}, u32[]{:S(2)}) collective-permute-start(s32[1,2]{1,0:T(1,128)S(1)} %copy-done.2), channel_id=1, source_target_pairs={{0,1},{1,0},{2,3},{3,2},{4,5},{5,4},{6,7},{7,6},{8,9},{9,8},{10,11... | collective-permute-start | bytes 32 | tf_op jit(solution)/shard_map/ppermute | solution.py:531
  31.4 5.0 %collective-permute-start.8 = (bf16[16,128]{1,0:T(8,128)(2,1)S(1)}, bf16[16,128]{1,0:T(8,128)(2,1)S(1)}, u32[]{:S(2)}, u32[]{:S(2)}) collective-permute-start(bf16[16,128]{1,0:T(8,128)(2,1)S(1)} %slice_bitcast_fusion), channel_id=1, source_target_pairs={{0,1},{1,0},{2,3},{3,2},{4,5},{5,4},{6,7},{7,6},{8,9},{9,8},{10,11... | collective-permute-start | bytes 12296 | tf_op jit(solution)/shard_map/ppermute | solution.py:531
  32.0 4.4 %copy-start.1 = (f32[4,1024]{1,0:T(4,128)S(1)}, f32[4,1024]{1,0:T(4,128)}, u32[]{:S(2)}) copy-start(f32[4,1024]{1,0:T(4,128)} %amounts.1) | copy-start | bytes 49156
  48.5 2.9 %collective-permute-start.12 = (f32[16,128,128]{2,1,0:T(8,128)S(1)}, f32[16,128,128]{2,1,0:T(8,128)S(1)}, u32[]{:S(2)}, u32[]{:S(2)}) collective-permute-start(f32[16,128,128]{2,1,0:T(8,128)S(1)} %get-tuple-element.49), channel_id=1, source_target_pairs={{0,1},{1,0},{2,3},{3,2},{4,5},{5,4},{6,7},{7,6},{8,9},{9,8},{10,11... | collective-permute-start | bytes 3145736 | tf_op jit(solution)/shard_map/ppermute | solution.py:531
  49.2 3.8 %collective-permute-start.11 = (f32[16,128,128]{2,1,0:T(8,128)S(1)}, f32[16,128,128]{2,1,0:T(8,128)S(1)}, u32[]{:S(2)}, u32[]{:S(2)}) collective-permute-start(f32[16,128,128]{2,1,0:T(8,128)S(1)} %get-tuple-element.47.refs_2_), channel_id=1, source_target_pairs={{0,1},{1,0},{2,3},{3,2},{4,5},{5,4},{6,7},{7,6},{8,9},{9,8},{10,11... | collective-permute-start | bytes 3145736 | tf_op jit(solution)/shard_map/ppermute | solution.py:531
  49.2 5.2 %collective-permute-start.10 = (f32[16,128,128]{2,1,0:T(8,128)S(1)}, f32[16,128,128]{2,1,0:T(8,128)S(1)}, u32[]{:S(2)}, u32[]{:S(2)}) collective-permute-start(f32[16,128,128]{2,1,0:T(8,128)S(1)} %get-tuple-element.42.refs_0_), channel_id=1, source_target_pairs={{0,1},{1,0},{2,3},{3,2},{4,5},{5,4},{6,7},{7,6},{8,9},{9,8},{10,11... | collective-permute-start | bytes 3145736 | tf_op jit(solution)/shard_map/ppermute | solution.py:531
  51.0 6.1 %collective-permute-start.9 = (f32[8,128,128]{2,1,0:T(8,128)S(1)}, f32[8,128,128]{2,1,0:T(8,128)S(1)}, u32[]{:S(2)}, u32[]{:S(2)}) collective-permute-start(f32[8,128,128]{2,1,0:T(8,128)S(1)} %get-tuple-element.46), channel_id=1, source_target_pairs={{0,1},{1,0},{2,3},{3,2},{4,5},{5,4},{6,7},{7,6},{8,9},{9,8},{10,11... | collective-permute-start | bytes 1572872 | tf_op jit(solution)/shard_map/ppermute | solution.py:531

commit v5 on v4

--- a/solution.py
+++ b/solution.py
@@ -55,7 +55,7 @@
 
 
 def pack_x_kernel(*refs):
-    fields, out, stage, small, sems, out_sems = refs[:8], *refs[8:]
+    fields, small, stage, sems = refs[:8], *refs[8:]
     core = lax.axis_index("mem")
     width, rows, _ = fields[0].shape
     pairs = []
@@ -63,17 +63,9 @@
         begin = jnp.where(core == 0, width - d, 0)
         pairs.append((f.at[pl.ds(begin, d)], stage.at[pl.ds(s, d)]))
     copies = copy_all(pairs, sems)
-    sent = []
-
-    def send(i, begin, size):
-        part = pl.ds(begin, size)
-        sent.append(pltpu.make_async_copy(small.at[part], out.at[part], out_sems.at[i]))
-        sent[-1].start()
-
     for i in range(8):
         copies[i].wait()
         small[SENT_AT[i] : SENT_AT[i] + SENT[i]] = stage[pl.ds(STARTS[i] + 1 - core, SENT[i])].astype(BF16)
-        send(i, SENT_AT[i], SENT[i])
     at = [s + (1 + core if i < 2 else 2 * core) for i, s in enumerate(STARTS)]
     p, q, old_p, old_q, horiz, vert, ratio, tilt = [stage[j] for j in at]
     row = lax.broadcasted_iota(jnp.int32, p.shape, 0)
@@ -89,32 +81,28 @@
     ends = jnp.where(row == 0, horiz[:1], jnp.where(row == 1, horiz[rows - 1 :], 0.0))
     ends = jnp.where(row == 2, both[:1], jnp.where(row == 3, both[rows - 1 :], ends))
     small[AHEAD + 2] = ends.astype(BF16)
-    send(8, AHEAD, 3)
-    wait_all(sent)
 
 
 def pack_x(fields):
     shape = fields[0].shape[1:]
     return pl.pallas_call(
         pack_x_kernel,
-        out_shape=jax.ShapeDtypeStruct((LAYERS,) + shape, BF16),
+        out_shape=pltpu.VMEM((LAYERS,) + shape, BF16),
         in_specs=[HBM] * 8,
-        out_specs=HBM,
+        out_specs=VMEM,
         scratch_shapes=[
             pltpu.VMEM((sum(DEPTHS),) + shape, F32),
-            pltpu.VMEM((LAYERS,) + shape, BF16),
             pltpu.SemaphoreType.DMA((8,)),
-            pltpu.SemaphoreType.DMA((9,)),
         ],
-        compiler_params=params(),
+        compiler_params=params(16),
         name="pack_x",
     )(*pin(fields))
 
 
 def pack_rest_kernel(*refs):
-    fields, own, other, _ = refs[:8], *refs[8:11]
-    ys, same, cross, xs = refs[11:15]
-    stage, snaps, edges, stage_c, snaps_c, mixed, s_ys, s_same, s_cross, sems, out_sems = refs[15:]
+    fields, own, other = refs[:8], *refs[8:10]
+    s_ys, s_same, s_cross, edges = refs[10:14]
+    stage, snaps, stage_c, snaps_c, mixed, sems = refs[14:]
     core = lax.axis_index("mem")
     width, rows, _ = fields[0].shape
     near, far = width - DEEP, width - HMAX
@@ -134,12 +122,6 @@
         pairs.append((rim, snaps_c.at[half]))
         pairs.append((ref.at[:, pl.ds(x_far, HMAX)], edges.at[pl.ds(2 * half, 2)]))
     copies = copy_all(pairs, sems)
-    sent = []
-
-    def send(a, b):
-        sent.append(pltpu.make_async_copy(a, b, out_sems.at[len(sent)]))
-        sent[-1].start()
-
     wait_all(copies[:16])
     skip, skip_c = jnp.where(to_low, 0, 4), jnp.where(to_low, 4, 0)
     for slab in range(2):
@@ -160,47 +142,37 @@
         s_ys[2 + pair] = mixed[:width].astype(BF16)
         begin = 2 * DEEP + pair * HMAX
         s_cross[begin : begin + HMAX] = mixed[width : width + HMAX].astype(BF16)
-    send(s_ys, ys)
-    send(s_cross, cross)
-    send(edges, xs)
     for slab in range(2):
         begin = slab * DEEP
         s_same[begin : begin + DEEP] = s_ys[slab, pl.ds(x_near, DEEP)]
         begin = 2 * DEEP + slab * HMAX
         s_same[begin : begin + HMAX] = s_ys[2 + slab, pl.ds(x_far, HMAX)]
-    send(s_same, same)
-    wait_all(sent)
-
-
-def pack_rest(fields, own, other, earlier):
+
+
+def pack_rest(fields, own, other):
     width, rows, depth = fields[0].shape
     corner = (2 * DEEP + 2 * HMAX, 16, depth)
     return pl.pallas_call(
         pack_rest_kernel,
         out_shape=(
-            jax.ShapeDtypeStruct((4, width, 16, depth), BF16),
-            jax.ShapeDtypeStruct(corner, BF16),
-            jax.ShapeDtypeStruct(corner, BF16),
-            jax.ShapeDtypeStruct((NT, HMAX, rows, depth), BF16),
+            pltpu.VMEM((4, width, 16, depth), BF16),
+            pltpu.VMEM(corner, BF16),
+            pltpu.VMEM(corner, BF16),
+            pltpu.VMEM((NT, HMAX, rows, depth), BF16),
         ),
-        in_specs=[HBM] * 11,
-        out_specs=(HBM,) * 4,
+        in_specs=[HBM] * 9 + [pl.BlockSpec(memory_space=pl.ANY)],
+        out_specs=(VMEM,) * 4,
         scratch_shapes=[
             pltpu.VMEM((8, width, 8, depth), F32),
             pltpu.VMEM((2, 2, width, 16, depth), BF16),
-            pltpu.VMEM((NT, HMAX, rows, depth), BF16),
             pltpu.VMEM((8, DEEP, 8, depth), F32),
             pltpu.VMEM((2, 2, HMAX, 16, depth), BF16),
             pltpu.VMEM((width + HMAX, 16, depth), F32),
-            pltpu.VMEM((4, width, 16, depth), BF16),
-            pltpu.VMEM(corner, BF16),
-            pltpu.VMEM(corner, BF16),
             pltpu.SemaphoreType.DMA((22,)),
-            pltpu.SemaphoreType.DMA((4,)),
         ],
-        compiler_params=params(),
+        compiler_params=params(16),
         name="pack_rest",
-    )(*pin((*fields, own, other, earlier)))
+    )(*pin((*fields, own)), other)
 
 
 def load_kernel(target, *refs):
@@ -236,7 +208,7 @@
     wait_all(copies + [save])
 
 
-def load(fields, earlier, target):
+def load(fields, target):
     width, rows, depth = fields[0].shape
     any_space = pl.BlockSpec(memory_space=pl.ANY)
     n = target.shape[0] - 4
@@ -245,7 +217,7 @@
     return pl.pallas_call(
         load_kernel,
         out_shape=(pltpu.VMEM(shape, F32),) * 8 + (jax.ShapeDtypeStruct(listed, jnp.int32),),
-        in_specs=[any_space] + [HBM] * 8 + [any_space],
+        in_specs=[any_space] + [HBM] * 8,
         out_specs=(VMEM,) * 8 + (any_space,),
         scratch_shapes=[
             pltpu.SMEM(listed, jnp.int32),
@@ -256,7 +228,7 @@
         ],
         compiler_params=params(8),
         name="load",
-    )(target, *pin(fields), earlier)
+    )(target, *pin(fields))
 
 
 def wave_kernel(ints, amounts, *refs):
@@ -299,7 +271,7 @@
     def step(k, p, q, old_p, old_q):
         low, high = 1 + k, half + 2 * DEEP - 1 - k
         begin, end = (ROW0 - 8, ROW0 + rows + 8) if k < NT - 1 else (ROW0, ROW0 + rows)
-        size = 24 if (end - begin) % 24 == 0 else 32 if (end - begin) % 32 == 0 else 8
+        size = 48 if (end - begin) % 48 == 0 else 64 if (end - begin) % 64 == 0 else 8
 
         def strip(i, _):
             r = pl.multiple_of(begin + i * size, 8)
@@ -352,7 +324,7 @@
 
         def layer(i, _):
             at = jnp.clip(core * HMAX + i - off_x, 0, half + HMAX - 1)
-            slot = i % 4
+            slot = i % 8
             mine, others = y_own[2 + pair, core * HMAX + at], y_other[2 + pair, core * HMAX + at]
             rim = jnp.where(from_own, mine.astype(F32), others.astype(F32))
             rim = rim[8 * part : 8 * part + 8]
@@ -363,7 +335,7 @@
             totals[lag][i] = term if k == 0 else totals[lag][i] + term
             return 0
 
-        lax.fori_loop(0, half, layer, 0, unroll=4)
+        lax.fori_loop(0, half, layer, 0, unroll=8)
 
     p_now, q_now, p_old, q_old = bufs[:4]
     main = slice(ROW0, ROW0 + rows)
@@ -403,7 +375,7 @@
             pltpu.VMEM((NT, HMAX, rows, depth), F32),
         )
         + tuple(pltpu.VMEM(b.shape, F32) for b in bufs),
-        in_specs=[any_space] * 2 + [VMEM] * 5 + [HBM] * 2 + [any_space] + [VMEM] * 8,
+        in_specs=[any_space] * 2 + [VMEM] * 5 + [HBM] + [any_space] * 2 + [VMEM] * 8,
         out_specs=(VMEM,) * 13,
         input_output_aliases={10 + i: 5 + i for i in range(8)},
         scratch_shapes=[
@@ -411,13 +383,13 @@
             pltpu.SMEM(data.shape, F32),
             pltpu.VMEM((half + 2 * DEEP, 16, depth), F32),
             pltpu.VMEM((NT, half + HMAX, rows, depth), BF16),
-            pltpu.VMEM((4, rows + 2 * HMAX, depth), F32),
+            pltpu.VMEM((8, rows + 2 * HMAX, depth), F32),
             pltpu.VMEM((2, rows, depth), F32),
             pltpu.SemaphoreType.DMA((4,)),
         ],
         compiler_params=params(8),
         name="wave",
-    )(ints, data, *pin(halos, pltpu.VMEM), *pin((own, other)), earlier, *pin(bufs, pltpu.VMEM))[:5]
+    )(ints, data, *pin(halos, pltpu.VMEM), *pin((own,)), other, earlier, *pin(bufs, pltpu.VMEM))[:5]
 
 
 def merge_kernel(*refs):
@@ -559,9 +531,9 @@
     other = swap(src_hist)
     packed = pack_x(fields)
     xw = outward(packed, 1, 0)
-    ys, same, cross, xs = pack_rest(fields, src_hist, other, packed)
+    ys, same, cross, xs = pack_rest(fields, src_hist, after(other, packed))
     ys, same, cross = outward(ys, 0, 1), outward(same, 1, 1), outward(cross, 1, -1)
-    *bufs, ints = load(fields, packed, target)
+    *bufs, ints = load(fields, after(target, packed))
     xs = outward(after(xs, (same, cross)), 1, 0)
     halos = (xw, ys, swap(ys), same, cross)
     token = swap(xw[0, :16])

time: 58.6 us -> 57.5 us (0.981)
  no operation moved by 1% of the time
where the time goes in v5:
time: 57.5 us; the launch traced here: 56.8 us
  Pallas kernels  26.6 us (46%)
  starting transfers between devices  21.8 us (38%)
  waiting for transfers between devices  6.84 us (12%)
  between operations  0.8 us (1%)
  local copies, waits for them, and re-layouts  0.77 us (1%)
    ppermute x5, starting transfers between devices, outward(): return lax.ppermute(v, ('gx', 'gy', 'mem'), pairs)  19.7 us
    pallas_call x1, Pallas kernels, wave(): pl.pallas_call(wave_kernel, out_shape=(*(pltpu.VMEM((half, rows, depth),...  12.1 us
    pallas_call x1, Pallas kernels, load(): pl.pallas_call(load_kernel, out_shape=(pltpu.VMEM(shape, F32),) * 8 + (ja...  4.4 us
    ppermute x5, waiting for transfers between devices, outward(): return lax.ppermute(v, ('gx', 'gy', 'mem'), pairs)  3.49 us
    ppermute x8, waiting for transfers between devices, swap(): return lax.ppermute(v, 'mem', [(0, 1), (1, 0)])  3.35 us
    pallas_call x1, Pallas kernels, pack_rest(): pl.pallas_call(pack_rest_kernel, out_shape=(pltpu.VMEM((4, width, 16, dep...  2.84 us
    pallas_call x1, Pallas kernels, merge(): pl.pallas_call(merge_kernel, out_shape=(block,) * 3, in_specs=[VMEM] * 6,...  2.72 us
    pallas_call x1, Pallas kernels, pack_x(): pl.pallas_call(pack_x_kernel, out_shape=pltpu.VMEM((LAYERS,) + shape, BF1...  2.48 us
  transfers between devices with their start and end apart: 13, of which 5 were waited for; matrix products, arithmetic and copies ran while one was open for 1% of the time, Pallas kernels for 46%

profile of v5, /device:TPU:0, one launch (start us, length us, event | category | flops | bytes accessed | tf_op | source)
XLA Modules:
  0.0 56.8 jit_solution(1195708275161114459)
XLA Ops:
  0.6 0.5 collective-permute-start.1
  1.1 2.5 %pack_x.1 = bf16[21,128,128]{2,1,0:T(8,128)(2,1)} custom-call(f32[32,128,128]{2,1,0:T(8,128)} %refs_0_.5, f32[32,128,128]{2,1,0:T(8,128)} %refs_1_.5, f32[32,128,128]{2,1,0:T(8,128)} %refs_2_.5, f32[32,128,128]{2,1,0:T(8,128)} %refs_3_.5, f32[32,128,128]{2,1,0:T(8,128)} %refs_4_.5, f32[32,128,128]{2,1,0:T(8,128)} %refs_5_.6, f32[32,128,128]{2,1,0:T(8,128)} %refs_6_.5, ...), custom_call_target="tpu_custom_call" | custom-call | tf_op jit(solution)/shard_map/pack_x/pallas_call | solution.py:88
  3.6 0.0 copy-start.1
  3.6 0.0 copy-start.2
  3.7 5.3 %collective-permute-start.5 = (bf16[21,128,128]{2,1,0:T(8,128)(2,1)}, bf16[21,128,128]{2,1,0:T(8,128)(2,1)}, u32[]{:S(2)}, u32[]{:S(2)}) collective-permute-start(bf16[21,128,128]{2,1,0:T(8,128)(2,1)} %pack_x.1), channel_id=1, source_target_pairs={{0,8},{2,10},{4,12},{6,14},{8,16},{9,1},{10,18},{11,3},{12,20},{13... | collective-permute-start | bytes 2064392 | tf_op jit(solution)/shard_map/ppermute | solution.py:517
  9.0 0.0 collective-permute-done.1.refs_9_.refs_6_
  9.0 2.8 %pack_rest.1 = (bf16[4,32,16,128]{3,2,1,0:T(8,128)(2,1)S(1)}, bf16[24,16,128]{2,1,0:T(8,128)(2,1)S(1)}, bf16[24,16,128]{2,1,0:T(8,128)(2,1)S(1)}, bf16[4,8,128,128]{3,2,1,0:T(8,128)(2,1)}) custom-call(f32[32,128,128]{2,1,0:T(8,128)} %refs_0_.5, f32[32,128,128]{2,1,0:T(8,128)} %refs_1_.5, f32[32,128,128]{2,1,0:T(8,128)} %refs_2_.5, f32[32,128,128]{2,1,0:T(8,128)} %refs_3_.5, ...), custom_call_target="tpu_custom_call" | custom-call | tf_op jit(solution)/shard_map/pack_rest/pallas_call | solution.py:155
  11.8 4.3 %collective-permute-start.6 = (bf16[4,32,16,128]{3,2,1,0:T(8,128)(2,1)S(1)}, bf16[4,32,16,128]{3,2,1,0:T(8,128)(2,1)}, u32[]{:S(2)}, u32[]{:S(2)}) collective-permute-start(bf16[4,32,16,128]{3,2,1,0:T(8,128)(2,1)S(1)} %get-tuple-element.37), channel_id=1, source_target_pairs={{0,2},{2,4},{3,1},{4,6},{5,3},{7,5},{8,10},{10,12},{11,9},{12,14},... | collective-permute-start | bytes 1572872 | tf_op jit(solution)/shard_map/ppermute | solution.py:517
  16.1 2.8 %collective-permute-start.2 = (bf16[24,16,128]{2,1,0:T(8,128)(2,1)S(1)}, bf16[24,16,128]{2,1,0:T(8,128)(2,1)S(1)}, u32[]{:S(2)}, u32[]{:S(2)}) collective-permute-start(bf16[24,16,128]{2,1,0:T(8,128)(2,1)S(1)} %get-tuple-element.32), channel_id=1, source_target_pairs={{0,10},{2,12},{4,14},{8,18},{10,20},{11,1},{12,22},{13,3},{15,5},{... | collective-permute-start | bytes 294920 | tf_op jit(solution)/shard_map/ppermute | solution.py:517
  18.9 0.7 %collective-permute-start.3 = (bf16[24,16,128]{2,1,0:T(8,128)(2,1)S(1)}, bf16[24,16,128]{2,1,0:T(8,128)(2,1)S(1)}, u32[]{:S(2)}, u32[]{:S(2)}) collective-permute-start(bf16[24,16,128]{2,1,0:T(8,128)(2,1)S(1)} %get-tuple-element.33), channel_id=1, source_target_pairs={{2,8},{4,10},{6,12},{9,3},{10,16},{11,5},{12,18},{13,7},{14,20},{1... | collective-permute-start | bytes 294920 | tf_op jit(solution)/shard_map/ppermute | solution.py:517
  19.6 2.4 %collective-permute-done.6.refs_1_ = bf16[4,32,16,128]{3,2,1,0:T(8,128)(2,1)} collective-permute-done((bf16[4,32,16,128]{3,2,1,0:T(8,128)(2,1)S(1)}, bf16[4,32,16,128]{3,2,1,0:T(8,128)(2,1)}, u32[]{:S(2)}, u32[]{:S(2)}) %collective-permute-start.6) | collective-permute-done | bytes 524320 | tf_op jit(solution)/shard_map/ppermute | solution.py:517
  22.0 1.0 %collective-permute-done.2.refs_3_.same = bf16[24,16,128]{2,1,0:T(8,128)(2,1)S(1)} collective-permute-done((bf16[24,16,128]{2,1,0:T(8,128)(2,1)S(1)}, bf16[24,16,128]{2,1,0:T(8,128)(2,1)S(1)}, u32[]{:S(2)}, u32[]{:S(2)}) %collective-permute-start.2) | collective-permute-done | bytes 98336 | tf_op jit(solution)/shard_map/ppermute | solution.py:517
  23.1 6.7 %collective-permute-start.4 = (bf16[4,8,128,128]{3,2,1,0:T(8,128)(2,1)}, bf16[4,8,128,128]{3,2,1,0:T(8,128)(2,1)S(1)}, u32[]{:S(2)}, u32[]{:S(2)}) collective-permute-start(bf16[4,8,128,128]{3,2,1,0:T(8,128)(2,1)} %get-tuple-element.34), channel_id=1, source_target_pairs={{0,8},{2,10},{4,12},{6,14},{8,16},{9,1},{10,18},{11,3},{12,20},{13... | collective-permute-start | bytes 3145736 | tf_op jit(solution)/shard_map/ppermute | solution.py:517
  29.8 0.1 collective-permute-start
  29.9 0.0 collective-permute-done.5.refs_0_
  29.9 0.7 %slice_bitcast_fusion = bf16[16,128]{1,0:T(8,128)(2,1)S(1)} fusion(bf16[21,128,128]{2,1,0:T(8,128)(2,1)} %collective-permute-done.5.refs_0_), kind=kLoop, calls=%fused_computation.17 | loop fusion | bytes 8192 | tf_op jit(solution)/shard_map/squeeze | solution.py:539
  30.5 0.5 collective-permute-start.8
  31.1 0.0 collective-permute-done.offs_other
  31.1 0.1 concatenate.3.target
  31.1 4.4 %load.1 = (f32[24,160,128]{2,1,0:T(8,128)S(1)}, f32[24,160,128]{2,1,0:T(8,128)S(1)}, f32[24,160,128]{2,1,0:T(8,128)S(1)}, f32[24,160,128]{2,1,0:T(8,128)S(1)}, f...) custom-call(s32[1028]{0:T(1024)S(1)} %concatenate.3.target, ...), custom_call_target="tpu_custom_call" | custom-call | tf_op jit(solution)/shard_map/load/pallas_call | solution.py:217
  35.6 0.0 collective-permute-done.7.refs_2_
  35.6 12.1 %wave.1 = (f32[16,128,128]{2,1,0:T(8,128)S(1)}, f32[16,128,128]{2,1,0:T(8,128)S(1)}, f32[16,128,128]{2,1,0:T(8,128)S(1)}, f32[16,128,128]{2,1,0:T(8,128)S(1)}, f...) custom-call(s32[2064]{0:T(1024)S(1)} %get-tuple-element.36.ints, ...), custom_call_target="tpu_custom_call", output_to_operand_aliasing={{5}: (10, {}), {6}: (11, {}), {7}: (12, {}), {8}: (13, {}),... | custom-call | tf_op jit(solution)/shard_map/wave/pallas_call | solution.py:371
  47.7 0.4 collective-permute-start.12
  48.1 0.2 collective-permute-start.11
  48.3 0.3 collective-permute-start.10
  48.6 1.4 %rim_image.1 = (f32[16,128,128]{2,1,0:T(8,128)S(1)}, f32[8,128,128]{2,1,0:T(8,128)S(1)}) custom-call(s32[1,2]{1,0:T(1,128)S(1)} %copy-done.1, s32[1,2]{1,0:T(1,128)S(1)} %collective-permute-done.offs_other, bf16[4,8,128,128]{3,2,1,0:T(8,128)(2,1)S(1)} %collective-permute-done.4.xs, ...), custom_call_target="tpu_custom_call", output_to_operand_aliasing={{0}: (6, {})} | custom-call | tf_op jit(solution)/shard_map/rim_image/pallas_call | solution.py:453
  50.0 0.1 collective-permute-start.9
  50.1 0.3 collective-permute-done.12.refs_5_
  50.4 1.5 %collective-permute-done.11.refs_3_ = f32[16,128,128]{2,1,0:T(8,128)S(1)} collective-permute-done((f32[16,128,128]{2,1,0:T(8,128)S(1)}, f32[16,128,128]{2,1,0:T(8,128)S(1)}, u32[]{:S(2)}, u32[]{:S(2)}) %collective-permute-start.11) | collective-permute-done | bytes 1048608 | tf_op jit(solution)/shard_map/ppermute | solution.py:503
  51.9 1.5 %collective-permute-done.10.refs_1_ = f32[16,128,128]{2,1,0:T(8,128)S(1)} collective-permute-done((f32[16,128,128]{2,1,0:T(8,128)S(1)}, f32[16,128,128]{2,1,0:T(8,128)S(1)}, u32[]{:S(2)}, u32[]{:S(2)}) %collective-permute-start.10) | collective-permute-done | bytes 1048608 | tf_op jit(solution)/shard_map/ppermute | solution.py:503
  53.4 2.7 %merge.1 = (f32[32,128,128]{2,1,0:T(8,128)}, f32[32,128,128]{2,1,0:T(8,128)}, f32[32,128,128]{2,1,0:T(8,128)}) custom-call(f32[16,128,128]{2,1,0:T(8,128)S(1)} %get-tuple-element.46.refs_0_, f32[16,128,128]{2,1,0:T(8,128)S(1)} %collective-permute-done.10.refs_1_, f32[16,128,128]{2,1,0:T(8,128)S(1)} %get-tuple-element.51.refs_2_, ...), custom_call_target="tpu_custom_call" | custom-call | tf_op jit(solution)/shard_map/merge/pallas_call | solution.py:408
  56.2 0.6 %place_rim.1 = f32[32,128,128]{2,1,0:T(8,128)} custom-call(s32[1,2]{1,0:T(1,128)S(1)} %copy-done.1, f32[8,128,128]{2,1,0:T(8,128)S(1)} %collective-permute-done.9.given, f32[32,128,128]{2,1,0:T(8,128)} %get-tuple-element.54._), custom_call_target="tpu_custom_call", output_to_operand_aliasing={{}: (2, {})} | custom-call | tf_op jit(solution)/shard_map/place_rim/pallas_call | solution.py:484
  (10 shorter events, 0.0 us)
Async XLA Ops:
  0.6 8.3 %collective-permute-start.1 = (bf16[2,32,128,128]{3,2,1,0:T(8,128)(2,1)}, bf16[2,32,128,128]{3,2,1,0:T(8,128)(2,1)S(1)}, u32[]{:S(2)}, u32[]{:S(2)}) collective-permute-start(bf16[2,32,128,128]{3,2,1,0:T(8,128)(2,1)} %refs_5_.7), channel_id=1, source_target_pairs={{0,1},{1,0},{2,3},{3,2},{4,5},{5,4},{6,7},{7,6},{8,9},{9,8},{10,11... | collective-permute-start | bytes 6291464 | tf_op jit(solution)/shard_map/ppermute | solution.py:503
  3.6 26.1 %copy-start.1 = (s32[1,2]{1,0:T(1,128)S(1)}, s32[1,2]{1,0:T(1,128)}, u32[]{:S(2)}) copy-start(s32[1,2]{1,0:T(1,128)} %offs.3) | copy-start | bytes 28
  3.6 27.4 %copy-start.2 = (s32[1024]{0:T(1024)S(1)}, s32[1024]{0:T(1024)}, u32[]{:S(2)}) copy-start(s32[1024]{0:T(1024)} %param.21) | copy-start | bytes 12292
  3.7 26.2 %collective-permute-start.5 = (bf16[21,128,128]{2,1,0:T(8,128)(2,1)}, bf16[21,128,128]{2,1,0:T(8,128)(2,1)}, u32[]{:S(2)}, u32[]{:S(2)}) collective-permute-start(bf16[21,128,128]{2,1,0:T(8,128)(2,1)} %pack_x.1), channel_id=1, source_target_pairs={{0,8},{2,10},{4,12},{6,14},{8,16},{9,1},{10,18},{11,3},{12,20},{13... | collective-permute-start | bytes 2064392 | tf_op jit(solution)/shard_map/ppermute | solution.py:517
  11.8 10.2 %collective-permute-start.6 = (bf16[4,32,16,128]{3,2,1,0:T(8,128)(2,1)S(1)}, bf16[4,32,16,128]{3,2,1,0:T(8,128)(2,1)}, u32[]{:S(2)}, u32[]{:S(2)}) collective-permute-start(bf16[4,32,16,128]{3,2,1,0:T(8,128)(2,1)S(1)} %get-tuple-element.37), channel_id=1, source_target_pairs={{0,2},{2,4},{3,1},{4,6},{5,3},{7,5},{8,10},{10,12},{11,9},{12,14},... | collective-permute-start | bytes 1572872 | tf_op jit(solution)/shard_map/ppermute | solution.py:517
  16.1 6.9 %collective-permute-start.2 = (bf16[24,16,128]{2,1,0:T(8,128)(2,1)S(1)}, bf16[24,16,128]{2,1,0:T(8,128)(2,1)S(1)}, u32[]{:S(2)}, u32[]{:S(2)}) collective-permute-start(bf16[24,16,128]{2,1,0:T(8,128)(2,1)S(1)} %get-tuple-element.32), channel_id=1, source_target_pairs={{0,10},{2,12},{4,14},{8,18},{10,20},{11,1},{12,22},{13,3},{15,5},{... | collective-permute-start | bytes 294920 | tf_op jit(solution)/shard_map/ppermute | solution.py:517
  18.9 4.2 %collective-permute-start.3 = (bf16[24,16,128]{2,1,0:T(8,128)(2,1)S(1)}, bf16[24,16,128]{2,1,0:T(8,128)(2,1)S(1)}, u32[]{:S(2)}, u32[]{:S(2)}) collective-permute-start(bf16[24,16,128]{2,1,0:T(8,128)(2,1)S(1)} %get-tuple-element.33), channel_id=1, source_target_pairs={{2,8},{4,10},{6,12},{9,3},{10,16},{11,5},{12,18},{13,7},{14,20},{1... | collective-permute-start | bytes 294920 | tf_op jit(solution)/shard_map/ppermute | solution.py:517
  22.0 13.6 %collective-permute-start.7 = (bf16[4,32,16,128]{3,2,1,0:T(8,128)(2,1)}, bf16[4,32,16,128]{3,2,1,0:T(8,128)(2,1)}, u32[]{:S(2)}, u32[]{:S(2)}) collective-permute-start(bf16[4,32,16,128]{3,2,1,0:T(8,128)(2,1)} %collective-permute-done.6.refs_1_), channel_id=1, source_target_pairs={{0,1},{1,0},{2,3},{3,2},{4,5},{5,4},{6,7},{7,6},{8,9},{9,8},{10,11... | collective-permute-start | bytes 1572872 | tf_op jit(solution)/shard_map/ppermute | solution.py:503
  23.1 25.5 %collective-permute-start.4 = (bf16[4,8,128,128]{3,2,1,0:T(8,128)(2,1)}, bf16[4,8,128,128]{3,2,1,0:T(8,128)(2,1)S(1)}, u32[]{:S(2)}, u32[]{:S(2)}) collective-permute-start(bf16[4,8,128,128]{3,2,1,0:T(8,128)(2,1)} %get-tuple-element.34), channel_id=1, source_target_pairs={{0,8},{2,10},{4,12},{6,14},{8,16},{9,1},{10,18},{11,3},{12,20},{13... | collective-permute-start | bytes 3145736 | tf_op jit(solution)/shard_map/ppermute | solution.py:517
  29.8 1.3 %collective-permute-start = (s32[1,2]{1,0:T(1,128)S(1)}, s32[1,2]{1,0:T(1,128)S(1)}, u32[]{:S(2)}, u32[]{:S(2)}) collective-permute-start(s32[1,2]{1,0:T(1,128)S(1)} %copy-done.1), channel_id=1, source_target_pairs={{0,1},{1,0},{2,3},{3,2},{4,5},{5,4},{6,7},{7,6},{8,9},{9,8},{10,11... | collective-permute-start | bytes 32 | tf_op jit(solution)/shard_map/ppermute | solution.py:503
  30.5 5.0 %collective-permute-start.8 = (bf16[16,128]{1,0:T(8,128)(2,1)S(1)}, bf16[16,128]{1,0:T(8,128)(2,1)S(1)}, u32[]{:S(2)}, u32[]{:S(2)}) collective-permute-start(bf16[16,128]{1,0:T(8,128)(2,1)S(1)} %slice_bitcast_fusion), channel_id=1, source_target_pairs={{0,1},{1,0},{2,3},{3,2},{4,5},{5,4},{6,7},{7,6},{8,9},{9,8},{10,11... | collective-permute-start | bytes 12296 | tf_op jit(solution)/shard_map/ppermute | solution.py:503
  31.1 4.4 %copy-start = (f32[4,1024]{1,0:T(4,128)S(1)}, f32[4,1024]{1,0:T(4,128)}, u32[]{:S(2)}) copy-start(f32[4,1024]{1,0:T(4,128)} %amounts.1) | copy-start | bytes 49156
  47.7 2.7 %collective-permute-start.12 = (f32[16,128,128]{2,1,0:T(8,128)S(1)}, f32[16,128,128]{2,1,0:T(8,128)S(1)}, u32[]{:S(2)}, u32[]{:S(2)}) collective-permute-start(f32[16,128,128]{2,1,0:T(8,128)S(1)} %get-tuple-element.53), channel_id=1, source_target_pairs={{0,1},{1,0},{2,3},{3,2},{4,5},{5,4},{6,7},{7,6},{8,9},{9,8},{10,11... | collective-permute-start | bytes 3145736 | tf_op jit(solution)/shard_map/ppermute | solution.py:503
  48.1 3.9 %collective-permute-start.11 = (f32[16,128,128]{2,1,0:T(8,128)S(1)}, f32[16,128,128]{2,1,0:T(8,128)S(1)}, u32[]{:S(2)}, u32[]{:S(2)}) collective-permute-start(f32[16,128,128]{2,1,0:T(8,128)S(1)} %get-tuple-element.51.refs_2_), channel_id=1, source_target_pairs={{0,1},{1,0},{2,3},{3,2},{4,5},{5,4},{6,7},{7,6},{8,9},{9,8},{10,11... | collective-permute-start | bytes 3145736 | tf_op jit(solution)/shard_map/ppermute | solution.py:503
  48.3 5.1 %collective-permute-start.10 = (f32[16,128,128]{2,1,0:T(8,128)S(1)}, f32[16,128,128]{2,1,0:T(8,128)S(1)}, u32[]{:S(2)}, u32[]{:S(2)}) collective-permute-start(f32[16,128,128]{2,1,0:T(8,128)S(1)} %get-tuple-element.46.refs_0_), channel_id=1, source_target_pairs={{0,1},{1,0},{2,3},{3,2},{4,5},{5,4},{6,7},{7,6},{8,9},{9,8},{10,11... | collective-permute-start | bytes 3145736 | tf_op jit(solution)/shard_map/ppermute | solution.py:503
  50.0 6.1 %collective-permute-start.9 = (f32[8,128,128]{2,1,0:T(8,128)S(1)}, f32[8,128,128]{2,1,0:T(8,128)S(1)}, u32[]{:S(2)}, u32[]{:S(2)}) collective-permute-start(f32[8,128,128]{2,1,0:T(8,128)S(1)} %get-tuple-element.50), channel_id=1, source_target_pairs={{0,1},{1,0},{2,3},{3,2},{4,5},{5,4},{6,7},{7,6},{8,9},{9,8},{10,11... | collective-permute-start | bytes 1572872 | tf_op jit(solution)/shard_map/ppermute | solution.py:503

commit v6 on v5

--- a/solution.py
+++ b/solution.py
@@ -392,10 +392,10 @@
     )(ints, data, *pin(halos, pltpu.VMEM), *pin((own,)), other, earlier, *pin(bufs, pltpu.VMEM))[:5]
 
 
-def merge_kernel(*refs):
-    halves, outs, sems = refs[:6], refs[6:9], refs[9]
-    core = lax.axis_index("mem")
-    half = outs[0].shape[0] // 2
+def merge_kernel(n, *refs):
+    halves, outs, sems = refs[: 2 * n], refs[-n - 1 : -1], refs[-1]
+    core = lax.axis_index("mem")
+    half = halves[0].shape[0]
     pairs = []
     for i, out in enumerate(outs):
         pairs.append((halves[2 * i], out.at[pl.ds(half * core, half)]))
@@ -403,17 +403,18 @@
     wait_all(copy_all(pairs, sems))
 
 
-def merge(p, p_other, q, q_other, total, image_other):
-    block = jax.ShapeDtypeStruct((2 * p.shape[0],) + p.shape[1:], F32)
-    return pl.pallas_call(
-        merge_kernel,
-        out_shape=(block,) * 3,
-        in_specs=[VMEM] * 6,
-        out_specs=(HBM,) * 3,
-        scratch_shapes=[pltpu.SemaphoreType.DMA((6,))],
+def merge(halves, earlier, name):
+    n = len(halves) // 2
+    block = jax.ShapeDtypeStruct((2 * halves[0].shape[0],) + halves[0].shape[1:], F32)
+    return pl.pallas_call(
+        functools.partial(merge_kernel, n),
+        out_shape=(block,) * n,
+        in_specs=[VMEM] * 2 * n + [pl.BlockSpec(memory_space=pl.ANY)] * len(earlier),
+        out_specs=(HBM,) * n,
+        scratch_shapes=[pltpu.SemaphoreType.DMA((2 * n,))],
         compiler_params=params(8),
-        name="merge",
-    )(*pin((p, p_other, q, q_other, total, image_other), pltpu.VMEM))
+        name=name,
+    )(*pin(halves, pltpu.VMEM), *earlier)
 
 
 def rim_kernel(offs, offs_other, xs, same, cross, p_rims, _, total, given, wide):
@@ -540,7 +541,8 @@
     p, q, total, total_other, p_rims = wave(ints, rec_data, halos, src_hist, other, token, bufs)
     parts = (swap(p), swap(q), swap(total_other))
     total, given = rim_image(lag_offs, offs_other, (after(xs, p), same, cross), p_rims, total)
-    p, q, image = merge(p, parts[0], q, parts[1], total, parts[2])
+    p, q = merge((p, parts[0], q, parts[1]), (given,), "merge_fields")
+    (image,) = merge((total, parts[2]), pin((p,)), "merge_image")
     image = place_rim(lag_offs, swap(given), image)
     return image[None], p, q
 

time: 57.5 us -> 56.8 us (0.988)
  waiting for transfers between devices: 6.84 us -> 5.34 us
  Pallas kernels: 26.6 us -> 27.3 us
    ppermute x8, waiting for transfers between devices: 3.35 us -> 1.85 us  [swap(): return lax.ppermute(v, 'mem', [(0, 1), (1, 0)])]
    pallas_call x1 -> x2, Pallas kernels: 2.72 us -> 3.38 us  [merge(): pl.pallas_call(functools.partial(merge_kernel, n), out_shape=(block,) * n...]
  transfers between devices with their start and end apart: 13 -> 13, of which waited for: 5 -> 4; matrix products, arithmetic and copies ran while one was open for 1% -> 1% of each run, Pallas kernels for 46% -> 48%
where the time goes in v6:
time: 56.8 us; the launch traced here: 56 us
  Pallas kernels  27.3 us (48%)
  starting transfers between devices  21.8 us (38%)
  waiting for transfers between devices  5.34 us (9%)
  between operations  0.82 us (1%)
  local copies, waits for them, and re-layouts  0.77 us (1%)
    ppermute x5, starting transfers between devices, outward(): return lax.ppermute(v, ('gx', 'gy', 'mem'), pairs)  19.7 us
    pallas_call x1, Pallas kernels, wave(): pl.pallas_call(wave_kernel, out_shape=(*(pltpu.VMEM((half, rows, depth),...  12.1 us
    pallas_call x1, Pallas kernels, load(): pl.pallas_call(load_kernel, out_shape=(pltpu.VMEM(shape, F32),) * 8 + (ja...  4.4 us
    ppermute x5, waiting for transfers between devices, outward(): return lax.ppermute(v, ('gx', 'gy', 'mem'), pairs)  3.49 us
    pallas_call x2, Pallas kernels, merge(): pl.pallas_call(functools.partial(merge_kernel, n), out_shape=(block,) * n...  3.38 us
    pallas_call x1, Pallas kernels, pack_rest(): pl.pallas_call(pack_rest_kernel, out_shape=(pltpu.VMEM((4, width, 16, dep...  2.84 us
    pallas_call x1, Pallas kernels, pack_x(): pl.pallas_call(pack_x_kernel, out_shape=pltpu.VMEM((LAYERS,) + shape, BF1...  2.48 us
    ppermute x8, starting transfers between devices, swap(): return lax.ppermute(v, 'mem', [(0, 1), (1, 0)])  2.04 us
  transfers between devices with their start and end apart: 13, of which 4 were waited for; matrix products, arithmetic and copies ran while one was open for 1% of the time, Pallas kernels for 48%

profile of v6, /device:TPU:0, one launch (start us, length us, event | category | flops | bytes accessed | tf_op | source)
XLA Modules:
  0.0 56.0 jit_solution(5135443766343388938)
XLA Ops:
  0.6 0.5 collective-permute-start.1
  1.1 2.5 %pack_x.1 = bf16[21,128,128]{2,1,0:T(8,128)(2,1)} custom-call(f32[32,128,128]{2,1,0:T(8,128)} %refs_0_.5, f32[32,128,128]{2,1,0:T(8,128)} %refs_1_.5, f32[32,128,128]{2,1,0:T(8,128)} %refs_2_.5, f32[32,128,128]{2,1,0:T(8,128)} %refs_3_.5, f32[32,128,128]{2,1,0:T(8,128)} %refs_4_.5, f32[32,128,128]{2,1,0:T(8,128)} %refs_5_.6, f32[32,128,128]{2,1,0:T(8,128)} %refs_6_.5, ...), custom_call_target="tpu_custom_call" | custom-call | tf_op jit(solution)/shard_map/pack_x/pallas_call | solution.py:88
  3.6 0.0 copy-start.1
  3.6 0.0 copy-start.2
  3.7 5.3 %collective-permute-start.5 = (bf16[21,128,128]{2,1,0:T(8,128)(2,1)}, bf16[21,128,128]{2,1,0:T(8,128)(2,1)}, u32[]{:S(2)}, u32[]{:S(2)}) collective-permute-start(bf16[21,128,128]{2,1,0:T(8,128)(2,1)} %pack_x.1), channel_id=1, source_target_pairs={{0,8},{2,10},{4,12},{6,14},{8,16},{9,1},{10,18},{11,3},{12,20},{13... | collective-permute-start | bytes 2064392 | tf_op jit(solution)/shard_map/ppermute | solution.py:518
  9.0 0.0 collective-permute-done.1.refs_9_.refs_6_
  9.0 2.8 %pack_rest.1 = (bf16[4,32,16,128]{3,2,1,0:T(8,128)(2,1)S(1)}, bf16[24,16,128]{2,1,0:T(8,128)(2,1)S(1)}, bf16[24,16,128]{2,1,0:T(8,128)(2,1)S(1)}, bf16[4,8,128,128]{3,2,1,0:T(8,128)(2,1)}) custom-call(f32[32,128,128]{2,1,0:T(8,128)} %refs_0_.5, f32[32,128,128]{2,1,0:T(8,128)} %refs_1_.5, f32[32,128,128]{2,1,0:T(8,128)} %refs_2_.5, f32[32,128,128]{2,1,0:T(8,128)} %refs_3_.5, ...), custom_call_target="tpu_custom_call" | custom-call | tf_op jit(solution)/shard_map/pack_rest/pallas_call | solution.py:155
  11.8 4.3 %collective-permute-start.6 = (bf16[4,32,16,128]{3,2,1,0:T(8,128)(2,1)S(1)}, bf16[4,32,16,128]{3,2,1,0:T(8,128)(2,1)}, u32[]{:S(2)}, u32[]{:S(2)}) collective-permute-start(bf16[4,32,16,128]{3,2,1,0:T(8,128)(2,1)S(1)} %get-tuple-element.36), channel_id=1, source_target_pairs={{0,2},{2,4},{3,1},{4,6},{5,3},{7,5},{8,10},{10,12},{11,9},{12,14},... | collective-permute-start | bytes 1572872 | tf_op jit(solution)/shard_map/ppermute | solution.py:518
  16.1 2.8 %collective-permute-start.2 = (bf16[24,16,128]{2,1,0:T(8,128)(2,1)S(1)}, bf16[24,16,128]{2,1,0:T(8,128)(2,1)S(1)}, u32[]{:S(2)}, u32[]{:S(2)}) collective-permute-start(bf16[24,16,128]{2,1,0:T(8,128)(2,1)S(1)} %get-tuple-element.31), channel_id=1, source_target_pairs={{0,10},{2,12},{4,14},{8,18},{10,20},{11,1},{12,22},{13,3},{15,5},{... | collective-permute-start | bytes 294920 | tf_op jit(solution)/shard_map/ppermute | solution.py:518
  18.9 0.7 %collective-permute-start.3 = (bf16[24,16,128]{2,1,0:T(8,128)(2,1)S(1)}, bf16[24,16,128]{2,1,0:T(8,128)(2,1)S(1)}, u32[]{:S(2)}, u32[]{:S(2)}) collective-permute-start(bf16[24,16,128]{2,1,0:T(8,128)(2,1)S(1)} %get-tuple-element.32), channel_id=1, source_target_pairs={{2,8},{4,10},{6,12},{9,3},{10,16},{11,5},{12,18},{13,7},{14,20},{1... | collective-permute-start | bytes 294920 | tf_op jit(solution)/shard_map/ppermute | solution.py:518
  19.6 2.4 %collective-permute-done.6.refs_1_ = bf16[4,32,16,128]{3,2,1,0:T(8,128)(2,1)} collective-permute-done((bf16[4,32,16,128]{3,2,1,0:T(8,128)(2,1)S(1)}, bf16[4,32,16,128]{3,2,1,0:T(8,128)(2,1)}, u32[]{:S(2)}, u32[]{:S(2)}) %collective-permute-start.6) | collective-permute-done | bytes 524320 | tf_op jit(solution)/shard_map/ppermute | solution.py:518
  22.0 0.0 collective-permute-start.7
  22.0 1.0 %collective-permute-done.2.refs_3_.same = bf16[24,16,128]{2,1,0:T(8,128)(2,1)S(1)} collective-permute-done((bf16[24,16,128]{2,1,0:T(8,128)(2,1)S(1)}, bf16[24,16,128]{2,1,0:T(8,128)(2,1)S(1)}, u32[]{:S(2)}, u32[]{:S(2)}) %collective-permute-start.2) | collective-permute-done | bytes 98336 | tf_op jit(solution)/shard_map/ppermute | solution.py:518
  23.1 6.7 %collective-permute-start.4 = (bf16[4,8,128,128]{3,2,1,0:T(8,128)(2,1)}, bf16[4,8,128,128]{3,2,1,0:T(8,128)(2,1)S(1)}, u32[]{:S(2)}, u32[]{:S(2)}) collective-permute-start(bf16[4,8,128,128]{3,2,1,0:T(8,128)(2,1)} %get-tuple-element.33), channel_id=1, source_target_pairs={{0,8},{2,10},{4,12},{6,14},{8,16},{9,1},{10,18},{11,3},{12,20},{13... | collective-permute-start | bytes 3145736 | tf_op jit(solution)/shard_map/ppermute | solution.py:518
  29.8 0.1 collective-permute-start
  29.9 0.0 collective-permute-done.5.refs_0_
  29.9 0.7 %slice_bitcast_fusion = bf16[16,128]{1,0:T(8,128)(2,1)S(1)} fusion(bf16[21,128,128]{2,1,0:T(8,128)(2,1)} %collective-permute-done.5.refs_0_), kind=kLoop, calls=%fused_computation.17 | loop fusion | bytes 8192 | tf_op jit(solution)/shard_map/squeeze | solution.py:540
  30.5 0.5 collective-permute-start.8
  31.1 0.0 collective-permute-done.offs_other
  31.1 0.1 concatenate.3.target
  31.1 4.4 %load.1 = (f32[24,160,128]{2,1,0:T(8,128)S(1)}, f32[24,160,128]{2,1,0:T(8,128)S(1)}, f32[24,160,128]{2,1,0:T(8,128)S(1)}, f32[24,160,128]{2,1,0:T(8,128)S(1)}, f...) custom-call(s32[1028]{0:T(1024)S(1)} %concatenate.3.target, ...), custom_call_target="tpu_custom_call" | custom-call | tf_op jit(solution)/shard_map/load/pallas_call | solution.py:217
  35.6 12.1 %wave.1 = (f32[16,128,128]{2,1,0:T(8,128)S(1)}, f32[16,128,128]{2,1,0:T(8,128)S(1)}, f32[16,128,128]{2,1,0:T(8,128)S(1)}, f32[16,128,128]{2,1,0:T(8,128)S(1)}, f...) custom-call(s32[2064]{0:T(1024)S(1)} %get-tuple-element.35.ints, ...), custom_call_target="tpu_custom_call", output_to_operand_aliasing={{5}: (10, {}), {6}: (11, {}), {7}: (12, {}), {8}: (13, {}),... | custom-call | tf_op jit(solution)/shard_map/wave/pallas_call | solution.py:371
  47.7 0.4 collective-permute-start.12
  48.1 0.2 collective-permute-start.11
  48.3 0.3 collective-permute-start.10
  48.6 1.4 %rim_image.1 = (f32[16,128,128]{2,1,0:T(8,128)S(1)}, f32[8,128,128]{2,1,0:T(8,128)S(1)}) custom-call(s32[1,2]{1,0:T(1,128)S(1)} %copy-done.1, s32[1,2]{1,0:T(1,128)S(1)} %collective-permute-done.offs_other, bf16[4,8,128,128]{3,2,1,0:T(8,128)(2,1)S(1)} %collective-permute-done.4.xs, ...), custom_call_target="tpu_custom_call", output_to_operand_aliasing={{0}: (6, {})} | custom-call | tf_op jit(solution)/shard_map/rim_image/pallas_call | solution.py:454
  50.0 0.1 collective-permute-start.9
  50.1 0.3 collective-permute-done.12.refs_3_
  50.4 1.5 %collective-permute-done.11.refs_1_ = f32[16,128,128]{2,1,0:T(8,128)S(1)} collective-permute-done((f32[16,128,128]{2,1,0:T(8,128)S(1)}, f32[16,128,128]{2,1,0:T(8,128)S(1)}, u32[]{:S(2)}, u32[]{:S(2)}) %collective-permute-start.11) | collective-permute-done | bytes 1048608 | tf_op jit(solution)/shard_map/ppermute | solution.py:504
  51.9 2.0 %merge_fields.1 = (f32[32,128,128]{2,1,0:T(8,128)}, f32[32,128,128]{2,1,0:T(8,128)}) custom-call(f32[16,128,128]{2,1,0:T(8,128)S(1)} %get-tuple-element.45.refs_0_, f32[16,128,128]{2,1,0:T(8,128)S(1)} %collective-permute-done.11.refs_1_, f32[16,128,128]{2,1,0:T(8,128)S(1)} %get-tuple-element.52.refs_2_, f32[16,128,128]{2,1,0:T(8,128)S(1)} %collective-permute-done.12.refs_3_, ...), custom_call_target="tpu_custom_call" | custom-call | tf_op jit(solution)/shard_map/merge_fields/pallas_call | solution.py:409
  54.0 1.3 %merge_image.1._ = f32[32,128,128]{2,1,0:T(8,128)} custom-call(f32[16,128,128]{2,1,0:T(8,128)S(1)} %get-tuple-element.50.refs_0_, f32[16,128,128]{2,1,0:T(8,128)S(1)} %collective-permute-done.10.refs_1_, f32[32,128,128]{2,1,0:T(8,128)} %get-tuple-element.27.refs_2_), custom_call_target="tpu_custom_call" | custom-call | tf_op jit(solution)/shard_map/merge_image/pallas_call | solution.py:409
  55.3 0.6 %place_rim.1 = f32[32,128,128]{2,1,0:T(8,128)} custom-call(s32[1,2]{1,0:T(1,128)S(1)} %copy-done.1, f32[8,128,128]{2,1,0:T(8,128)S(1)} %collective-permute-done.9.given, f32[32,128,128]{2,1,0:T(8,128)} %merge_image.1._), custom_call_target="tpu_custom_call", output_to_operand_aliasing={{}: (2, {})} | custom-call | tf_op jit(solution)/shard_map/place_rim/pallas_call | solution.py:485
  (11 shorter events, 0.0 us)
Async XLA Ops:
  0.6 8.3 %collective-permute-start.1 = (bf16[2,32,128,128]{3,2,1,0:T(8,128)(2,1)}, bf16[2,32,128,128]{3,2,1,0:T(8,128)(2,1)S(1)}, u32[]{:S(2)}, u32[]{:S(2)}) collective-permute-start(bf16[2,32,128,128]{3,2,1,0:T(8,128)(2,1)} %refs_5_.7), channel_id=1, source_target_pairs={{0,1},{1,0},{2,3},{3,2},{4,5},{5,4},{6,7},{7,6},{8,9},{9,8},{10,11... | collective-permute-start | bytes 6291464 | tf_op jit(solution)/shard_map/ppermute | solution.py:504
  3.6 26.1 %copy-start.1 = (s32[1,2]{1,0:T(1,128)S(1)}, s32[1,2]{1,0:T(1,128)}, u32[]{:S(2)}) copy-start(s32[1,2]{1,0:T(1,128)} %offs.3) | copy-start | bytes 28
  3.6 27.4 %copy-start.2 = (s32[1024]{0:T(1024)S(1)}, s32[1024]{0:T(1024)}, u32[]{:S(2)}) copy-start(s32[1024]{0:T(1024)} %param.21) | copy-start | bytes 12292
  3.7 26.2 %collective-permute-start.5 = (bf16[21,128,128]{2,1,0:T(8,128)(2,1)}, bf16[21,128,128]{2,1,0:T(8,128)(2,1)}, u32[]{:S(2)}, u32[]{:S(2)}) collective-permute-start(bf16[21,128,128]{2,1,0:T(8,128)(2,1)} %pack_x.1), channel_id=1, source_target_pairs={{0,8},{2,10},{4,12},{6,14},{8,16},{9,1},{10,18},{11,3},{12,20},{13... | collective-permute-start | bytes 2064392 | tf_op jit(solution)/shard_map/ppermute | solution.py:518
  11.8 10.2 %collective-permute-start.6 = (bf16[4,32,16,128]{3,2,1,0:T(8,128)(2,1)S(1)}, bf16[4,32,16,128]{3,2,1,0:T(8,128)(2,1)}, u32[]{:S(2)}, u32[]{:S(2)}) collective-permute-start(bf16[4,32,16,128]{3,2,1,0:T(8,128)(2,1)S(1)} %get-tuple-element.36), channel_id=1, source_target_pairs={{0,2},{2,4},{3,1},{4,6},{5,3},{7,5},{8,10},{10,12},{11,9},{12,14},... | collective-permute-start | bytes 1572872 | tf_op jit(solution)/shard_map/ppermute | solution.py:518
  16.1 6.9 %collective-permute-start.2 = (bf16[24,16,128]{2,1,0:T(8,128)(2,1)S(1)}, bf16[24,16,128]{2,1,0:T(8,128)(2,1)S(1)}, u32[]{:S(2)}, u32[]{:S(2)}) collective-permute-start(bf16[24,16,128]{2,1,0:T(8,128)(2,1)S(1)} %get-tuple-element.31), channel_id=1, source_target_pairs={{0,10},{2,12},{4,14},{8,18},{10,20},{11,1},{12,22},{13,3},{15,5},{... | collective-permute-start | bytes 294920 | tf_op jit(solution)/shard_map/ppermute | solution.py:518
  18.9 4.2 %collective-permute-start.3 = (bf16[24,16,128]{2,1,0:T(8,128)(2,1)S(1)}, bf16[24,16,128]{2,1,0:T(8,128)(2,1)S(1)}, u32[]{:S(2)}, u32[]{:S(2)}) collective-permute-start(bf16[24,16,128]{2,1,0:T(8,128)(2,1)S(1)} %get-tuple-element.32), channel_id=1, source_target_pairs={{2,8},{4,10},{6,12},{9,3},{10,16},{11,5},{12,18},{13,7},{14,20},{1... | collective-permute-start | bytes 294920 | tf_op jit(solution)/shard_map/ppermute | solution.py:518
  22.0 13.6 %collective-permute-start.7 = (bf16[4,32,16,128]{3,2,1,0:T(8,128)(2,1)}, bf16[4,32,16,128]{3,2,1,0:T(8,128)(2,1)}, u32[]{:S(2)}, u32[]{:S(2)}) collective-permute-start(bf16[4,32,16,128]{3,2,1,0:T(8,128)(2,1)} %collective-permute-done.6.refs_1_), channel_id=1, source_target_pairs={{0,1},{1,0},{2,3},{3,2},{4,5},{5,4},{6,7},{7,6},{8,9},{9,8},{10,11... | collective-permute-start | bytes 1572872 | tf_op jit(solution)/shard_map/ppermute | solution.py:504
  23.1 25.5 %collective-permute-start.4 = (bf16[4,8,128,128]{3,2,1,0:T(8,128)(2,1)}, bf16[4,8,128,128]{3,2,1,0:T(8,128)(2,1)S(1)}, u32[]{:S(2)}, u32[]{:S(2)}) collective-permute-start(bf16[4,8,128,128]{3,2,1,0:T(8,128)(2,1)} %get-tuple-element.33), channel_id=1, source_target_pairs={{0,8},{2,10},{4,12},{6,14},{8,16},{9,1},{10,18},{11,3},{12,20},{13... | collective-permute-start | bytes 3145736 | tf_op jit(solution)/shard_map/ppermute | solution.py:518
  29.8 1.3 %collective-permute-start = (s32[1,2]{1,0:T(1,128)S(1)}, s32[1,2]{1,0:T(1,128)S(1)}, u32[]{:S(2)}, u32[]{:S(2)}) collective-permute-start(s32[1,2]{1,0:T(1,128)S(1)} %copy-done.1), channel_id=1, source_target_pairs={{0,1},{1,0},{2,3},{3,2},{4,5},{5,4},{6,7},{7,6},{8,9},{9,8},{10,11... | collective-permute-start | bytes 32 | tf_op jit(solution)/shard_map/ppermute | solution.py:504
  30.5 5.0 %collective-permute-start.8 = (bf16[16,128]{1,0:T(8,128)(2,1)S(1)}, bf16[16,128]{1,0:T(8,128)(2,1)S(1)}, u32[]{:S(2)}, u32[]{:S(2)}) collective-permute-start(bf16[16,128]{1,0:T(8,128)(2,1)S(1)} %slice_bitcast_fusion), channel_id=1, source_target_pairs={{0,1},{1,0},{2,3},{3,2},{4,5},{5,4},{6,7},{7,6},{8,9},{9,8},{10,11... | collective-permute-start | bytes 12296 | tf_op jit(solution)/shard_map/ppermute | solution.py:504
  31.1 4.4 %copy-start = (f32[4,1024]{1,0:T(4,128)S(1)}, f32[4,1024]{1,0:T(4,128)}, u32[]{:S(2)}) copy-start(f32[4,1024]{1,0:T(4,128)} %amounts.1) | copy-start | bytes 49156
  47.7 2.7 %collective-permute-start.12 = (f32[16,128,128]{2,1,0:T(8,128)S(1)}, f32[16,128,128]{2,1,0:T(8,128)S(1)}, u32[]{:S(2)}, u32[]{:S(2)}) collective-permute-start(f32[16,128,128]{2,1,0:T(8,128)S(1)} %get-tuple-element.52.refs_2_), channel_id=1, source_target_pairs={{0,1},{1,0},{2,3},{3,2},{4,5},{5,4},{6,7},{7,6},{8,9},{9,8},{10,11... | collective-permute-start | bytes 3145736 | tf_op jit(solution)/shard_map/ppermute | solution.py:504
  48.1 3.8 %collective-permute-start.11 = (f32[16,128,128]{2,1,0:T(8,128)S(1)}, f32[16,128,128]{2,1,0:T(8,128)S(1)}, u32[]{:S(2)}, u32[]{:S(2)}) collective-permute-start(f32[16,128,128]{2,1,0:T(8,128)S(1)} %get-tuple-element.45.refs_0_), channel_id=1, source_target_pairs={{0,1},{1,0},{2,3},{3,2},{4,5},{5,4},{6,7},{7,6},{8,9},{9,8},{10,11... | collective-permute-start | bytes 3145736 | tf_op jit(solution)/shard_map/ppermute | solution.py:504
  48.3 5.7 %collective-permute-start.10 = (f32[16,128,128]{2,1,0:T(8,128)S(1)}, f32[16,128,128]{2,1,0:T(8,128)S(1)}, u32[]{:S(2)}, u32[]{:S(2)}) collective-permute-start(f32[16,128,128]{2,1,0:T(8,128)S(1)} %get-tuple-element.51), channel_id=1, source_target_pairs={{0,1},{1,0},{2,3},{3,2},{4,5},{5,4},{6,7},{7,6},{8,9},{9,8},{10,11... | collective-permute-start | bytes 3145736 | tf_op jit(solution)/shard_map/ppermute | solution.py:504
  50.0 5.3 %collective-permute-start.9 = (f32[8,128,128]{2,1,0:T(8,128)S(1)}, f32[8,128,128]{2,1,0:T(8,128)S(1)}, u32[]{:S(2)}, u32[]{:S(2)}) collective-permute-start(f32[8,128,128]{2,1,0:T(8,128)S(1)} %get-tuple-element.49.refs_4_), channel_id=1, source_target_pairs={{0,1},{1,0},{2,3},{3,2},{4,5},{5,4},{6,7},{7,6},{8,9},{9,8},{10,11... | collective-permute-start | bytes 1572872 | tf_op jit(solution)/shard_map/ppermute | solution.py:504

commit v7 on v5

--- a/solution.py
+++ b/solution.py
@@ -12,6 +12,7 @@
 DEEP = NT
 ROW0 = 16
 GROUP = 4
+CORNER = (DEEP - 1, DEEP - 2)
 HEAD = 8
 F32 = jnp.float32
 BF16 = jnp.bfloat16
@@ -130,7 +131,9 @@
             mixed[:width, at, :] = stage[4 * slab + i, :, pl.ds(skip, 4), :]
             mixed[width : width + DEEP, at, :] = stage_c[4 * slab + i, :, pl.ds(skip_c, 4), :]
         s_ys[slab] = mixed[:width].astype(BF16)
-        s_cross[slab * DEEP : (slab + 1) * DEEP] = mixed[width : width + DEEP].astype(BF16)
+        d, begin = CORNER[slab], slab * CORNER[0]
+        part = mixed[pl.ds(width + (DEEP - d) * (1 - core), d)]
+        s_cross[begin : begin + d] = part.astype(BF16)
     wait_all(copies[16:])
     for pair in range(2):
         for i in range(2):
@@ -140,18 +143,18 @@
             both = snaps_c[pair, i].astype(F32)
             mixed[width : width + HMAX, at, :] = jnp.where(to_low, both[:, 8:], both[:, :8])
         s_ys[2 + pair] = mixed[:width].astype(BF16)
-        begin = 2 * DEEP + pair * HMAX
+        begin = sum(CORNER) + pair * HMAX
         s_cross[begin : begin + HMAX] = mixed[width : width + HMAX].astype(BF16)
     for slab in range(2):
-        begin = slab * DEEP
-        s_same[begin : begin + DEEP] = s_ys[slab, pl.ds(x_near, DEEP)]
-        begin = 2 * DEEP + slab * HMAX
+        d, begin = CORNER[slab], slab * CORNER[0]
+        s_same[begin : begin + d] = s_ys[slab, pl.ds(jnp.where(to_low, 0, width - d), d)]
+        begin = sum(CORNER) + slab * HMAX
         s_same[begin : begin + HMAX] = s_ys[2 + slab, pl.ds(x_far, HMAX)]
 
 
 def pack_rest(fields, own, other):
     width, rows, depth = fields[0].shape
-    corner = (2 * DEEP + 2 * HMAX, 16, depth)
+    corner = (sum(CORNER) + 2 * HMAX, 16, depth)
     return pl.pallas_call(
         pack_rest_kernel,
         out_shape=(
@@ -247,7 +250,6 @@
         ],
         sem_in.at[pl.ds(2, 2)],
     )
-    face = core * (half + DEEP)
     inner = half + DEEP
     for f in range(8):
         d = SENT[f]
@@ -259,8 +261,9 @@
         for slab in range(2):
             part = ys[slab, pl.ds(core * (half - DEEP), inner)]
             stage[pl.ds(DEEP * (1 - core), inner)] = part.astype(F32)
-            part = corner[slab * DEEP : slab * DEEP + DEEP]
-            stage[pl.ds(face, DEEP)] = part.astype(F32)
+            d, begin = CORNER[slab], slab * CORNER[0]
+            to_x = jnp.where(core == 0, DEEP - d, half + DEEP)
+            stage[pl.ds(to_x, d)] = corner[begin : begin + d].astype(F32)
             for i in range(4):
                 bufs[4 * slab + i][:, pl.ds(to, DEEP), :] = stage[:, 4 * i : 4 * i + 4, :]
 
@@ -392,28 +395,25 @@
     )(ints, data, *pin(halos, pltpu.VMEM), *pin((own,)), other, earlier, *pin(bufs, pltpu.VMEM))[:5]
 
 
-def merge_kernel(*refs):
-    halves, outs, sems = refs[:6], refs[6:9], refs[9]
-    core = lax.axis_index("mem")
-    half = outs[0].shape[0] // 2
-    pairs = []
-    for i, out in enumerate(outs):
-        pairs.append((halves[2 * i], out.at[pl.ds(half * core, half)]))
-        pairs.append((halves[2 * i + 1], out.at[pl.ds(half - half * core, half)]))
-    wait_all(copy_all(pairs, sems))
-
-
-def merge(p, p_other, q, q_other, total, image_other):
-    block = jax.ShapeDtypeStruct((2 * p.shape[0],) + p.shape[1:], F32)
+def merge_kernel(p_own, p_other, q_own, q_other, total, _, p, q, image, sems):
+    core = lax.axis_index("mem")
+    half = total.shape[0]
+    here, there = pl.ds(half * core, half), pl.ds(half - half * core, half)
+    pairs = [(p_own, p.at[here]), (p_other, p.at[there]), (q_own, q.at[here]), (q_other, q.at[there])]
+    wait_all(copy_all(pairs + [(total, image.at[here])], sems))
+
+
+def merge(halves, earlier):
+    half, rows, depth = halves[0].shape
     return pl.pallas_call(
         merge_kernel,
-        out_shape=(block,) * 3,
-        in_specs=[VMEM] * 6,
+        out_shape=(jax.ShapeDtypeStruct((2 * half, rows, depth), F32),) * 3,
+        in_specs=[VMEM] * 5 + [pl.BlockSpec(memory_space=pl.ANY)],
         out_specs=(HBM,) * 3,
-        scratch_shapes=[pltpu.SemaphoreType.DMA((6,))],
+        scratch_shapes=[pltpu.SemaphoreType.DMA((5,))],
         compiler_params=params(8),
         name="merge",
-    )(*pin((p, p_other, q, q_other, total, image_other), pltpu.VMEM))
+    )(*pin(halves, pltpu.VMEM), earlier)
 
 
 def rim_kernel(offs, offs_other, xs, same, cross, p_rims, _, total, given, wide):
@@ -429,7 +429,7 @@
             mine = jnp.where(core == 0, i, HMAX - layers + i)
             result = None
             for pair in range(2):
-                place = 2 * DEEP + pair * HMAX + at
+                place = sum(CORNER) + pair * HMAX + at
                 strip = jnp.where(from_same, same[place].astype(F32), cross[place].astype(F32))
                 for part in range(2):
                     t = 2 * pair + part
@@ -465,32 +465,40 @@
     )(offs, offs_other, *pin((*halos, p_rims, total), pltpu.VMEM))
 
 
-def place_kernel(offs, given, _, image, sem_out):
-    core = lax.axis_index("mem")
-    width = image.shape[0]
+def place_kernel(offs, _, given, __, image, others, sems):
+    core = lax.axis_index("mem")
+    half = others.shape[0]
+    there = half - half * core
+    rim, inner = (half - HMAX) * (1 - core), HMAX * core
+    rest = pltpu.make_async_copy(
+        others.at[pl.ds(inner, half - HMAX)], image.at[pl.ds(there + inner, half - HMAX)], sems.at[0]
+    )
+    rest.start()
     layers = jnp.maximum(jnp.where(core == 0, -offs[0, 0], offs[0, 0]), 0)
 
-    def out_copy(i):
-        x = jnp.where(core == 0, width - layers + i, i)
-        return pltpu.make_async_copy(given.at[i], image.at[x], sem_out.at[i])
+    def put(i):
+        others[jnp.where(core == 0, half - layers + i, i)] = given[i]
 
     for i in range(HMAX):
-        pl.when(i < layers)(lambda i=i: out_copy(i).start())
-    for i in range(HMAX):
-        pl.when(i < layers)(lambda i=i: out_copy(i).wait())
-
-
-def place_rim(offs, given, image):
+        pl.when(i < layers)(lambda i=i: put(i))
+    last = pltpu.make_async_copy(
+        others.at[pl.ds(rim, HMAX)], image.at[pl.ds(there + rim, HMAX)], sems.at[1]
+    )
+    last.start()
+    wait_all([rest, last])
+
+
+def place_image(offs, others, given, image):
     return pl.pallas_call(
         place_kernel,
-        out_shape=jax.ShapeDtypeStruct(image.shape, F32),
-        in_specs=[SMEM, VMEM, HBM],
-        out_specs=HBM,
-        input_output_aliases={2: 0},
-        scratch_shapes=[pltpu.SemaphoreType.DMA((HMAX,))],
+        out_shape=(jax.ShapeDtypeStruct(image.shape, F32), pltpu.VMEM(others.shape, F32)),
+        in_specs=[SMEM] + [VMEM] * 2 + [HBM],
+        out_specs=(HBM, VMEM),
+        input_output_aliases={1: 1, 3: 0},
+        scratch_shapes=[pltpu.SemaphoreType.DMA((2,))],
         compiler_params=params(8),
-        name="place_rim",
-    )(offs, *pin((given,), pltpu.VMEM), *pin((image,)))
+        name="place_image",
+    )(offs, *pin((others, given), pltpu.VMEM), *pin((image,)))[0]
 
 
 def body(
@@ -540,8 +548,8 @@
     p, q, total, total_other, p_rims = wave(ints, rec_data, halos, src_hist, other, token, bufs)
     parts = (swap(p), swap(q), swap(total_other))
     total, given = rim_image(lag_offs, offs_other, (after(xs, p), same, cross), p_rims, total)
-    p, q, image = merge(p, parts[0], q, parts[1], total, parts[2])
-    image = place_rim(lag_offs, swap(given), image)
+    p, q, image = merge((p, parts[0], q, parts[1], total), given)
+    image = place_image(lag_offs, parts[2], swap(given), image)
     return image[None], p, q
 
 

time: 57.5 us -> 55.9 us (0.972)
  waiting for transfers between devices: 6.84 us -> 5.37 us
    ppermute x8, waiting for transfers between devices: 3.35 us -> 2.01 us  [swap(): return lax.ppermute(v, 'mem', [(0, 1), (1, 0)])]
  transfers between devices with their start and end apart: 13 -> 13, of which waited for: 5 -> 4; matrix products, arithmetic and copies ran while one was open for 1% -> 1% of each run, Pallas kernels for 46% -> 45%
where the time goes in v7:
time: 55.9 us; the launch traced here: 55.4 us
  Pallas kernels  26.7 us (48%)
  starting transfers between devices  21.8 us (39%)
  waiting for transfers between devices  5.37 us (10%)
  between operations  0.81 us (1%)
  local copies, waits for them, and re-layouts  0.77 us (1%)
    ppermute x5, starting transfers between devices, outward(): return lax.ppermute(v, ('gx', 'gy', 'mem'), pairs)  19.7 us
    pallas_call x1, Pallas kernels, wave(): pl.pallas_call(wave_kernel, out_shape=(*(pltpu.VMEM((half, rows, depth),...  11.8 us
    pallas_call x1, Pallas kernels, load(): pl.pallas_call(load_kernel, out_shape=(pltpu.VMEM(shape, F32),) * 8 + (ja...  4.4 us
    ppermute x5, waiting for transfers between devices, outward(): return lax.ppermute(v, ('gx', 'gy', 'mem'), pairs)  3.36 us
    pallas_call x1, Pallas kernels, pack_rest(): pl.pallas_call(pack_rest_kernel, out_shape=(pltpu.VMEM((4, width, 16, dep...  2.84 us
    pallas_call x1, Pallas kernels, pack_x(): pl.pallas_call(pack_x_kernel, out_shape=pltpu.VMEM((LAYERS,) + shape, BF1...  2.48 us
    pallas_call x1, Pallas kernels, merge(): pl.pallas_call(merge_kernel, out_shape=(jax.ShapeDtypeStruct((2 * half, r...  2.39 us
    ppermute x8, starting transfers between devices, swap(): return lax.ppermute(v, 'mem', [(0, 1), (1, 0)])  2.02 us
  transfers between devices with their start and end apart: 13, of which 4 were waited for; matrix products, arithmetic and copies ran while one was open for 1% of the time, Pallas kernels for 45%

profile of v7, /device:TPU:0, one launch (start us, length us, event | category | flops | bytes accessed | tf_op | source)
XLA Modules:
  0.0 55.4 jit_solution(12820261692215365266)
XLA Ops:
  0.6 0.5 collective-permute-start.2
  1.1 2.5 %pack_x.1 = bf16[21,128,128]{2,1,0:T(8,128)(2,1)} custom-call(f32[32,128,128]{2,1,0:T(8,128)} %refs_0_.5, f32[32,128,128]{2,1,0:T(8,128)} %refs_1_.5, f32[32,128,128]{2,1,0:T(8,128)} %refs_2_.5, f32[32,128,128]{2,1,0:T(8,128)} %refs_3_.5, f32[32,128,128]{2,1,0:T(8,128)} %refs_4_.5, f32[32,128,128]{2,1,0:T(8,128)} %refs_5_.6, f32[32,128,128]{2,1,0:T(8,128)} %refs_6_.5, ...), custom_call_target="tpu_custom_call" | custom-call | tf_op jit(solution)/shard_map/pack_x/pallas_call | solution.py:89
  3.6 0.0 copy-start.1
  3.6 0.0 copy-start.2
  3.7 5.3 %collective-permute-start.1 = (bf16[21,128,128]{2,1,0:T(8,128)(2,1)}, bf16[21,128,128]{2,1,0:T(8,128)(2,1)}, u32[]{:S(2)}, u32[]{:S(2)}) collective-permute-start(bf16[21,128,128]{2,1,0:T(8,128)(2,1)} %pack_x.1), channel_id=1, source_target_pairs={{0,8},{2,10},{4,12},{6,14},{8,16},{9,1},{10,18},{11,3},{12,20},{13... | collective-permute-start | bytes 2064392 | tf_op jit(solution)/shard_map/ppermute | solution.py:525
  9.0 0.0 collective-permute-done.2.refs_9_.refs_6_
  9.0 2.8 %pack_rest.1 = (bf16[4,32,16,128]{3,2,1,0:T(8,128)(2,1)S(1)}, bf16[21,16,128]{2,1,0:T(8,128)(2,1)S(1)}, bf16[21,16,128]{2,1,0:T(8,128)(2,1)S(1)}, bf16[4,8,128,128]{3,2,1,0:T(8,128)(2,1)}) custom-call(f32[32,128,128]{2,1,0:T(8,128)} %refs_0_.5, f32[32,128,128]{2,1,0:T(8,128)} %refs_1_.5, f32[32,128,128]{2,1,0:T(8,128)} %refs_2_.5, f32[32,128,128]{2,1,0:T(8,128)} %refs_3_.5, ...), custom_call_target="tpu_custom_call" | custom-call | tf_op jit(solution)/shard_map/pack_rest/pallas_call | solution.py:158
  11.8 4.3 %collective-permute-start.3 = (bf16[4,32,16,128]{3,2,1,0:T(8,128)(2,1)S(1)}, bf16[4,32,16,128]{3,2,1,0:T(8,128)(2,1)}, u32[]{:S(2)}, u32[]{:S(2)}) collective-permute-start(bf16[4,32,16,128]{3,2,1,0:T(8,128)(2,1)S(1)} %get-tuple-element.34), channel_id=1, source_target_pairs={{0,2},{2,4},{3,1},{4,6},{5,3},{7,5},{8,10},{10,12},{11,9},{12,14},... | collective-permute-start | bytes 1572872 | tf_op jit(solution)/shard_map/ppermute | solution.py:525
  16.1 2.8 %collective-permute-start.5 = (bf16[21,16,128]{2,1,0:T(8,128)(2,1)S(1)}, bf16[21,16,128]{2,1,0:T(8,128)(2,1)S(1)}, u32[]{:S(2)}, u32[]{:S(2)}) collective-permute-start(bf16[21,16,128]{2,1,0:T(8,128)(2,1)S(1)} %get-tuple-element.35), channel_id=1, source_target_pairs={{0,10},{2,12},{4,14},{8,18},{10,20},{11,1},{12,22},{13,3},{15,5},{... | collective-permute-start | bytes 258056 | tf_op jit(solution)/shard_map/ppermute | solution.py:525
  18.9 0.7 %collective-permute-start.6 = (bf16[21,16,128]{2,1,0:T(8,128)(2,1)S(1)}, bf16[21,16,128]{2,1,0:T(8,128)(2,1)S(1)}, u32[]{:S(2)}, u32[]{:S(2)}) collective-permute-start(bf16[21,16,128]{2,1,0:T(8,128)(2,1)S(1)} %get-tuple-element.36), channel_id=1, source_target_pairs={{2,8},{4,10},{6,12},{9,3},{10,16},{11,5},{12,18},{13,7},{14,20},{1... | collective-permute-start | bytes 258056 | tf_op jit(solution)/shard_map/ppermute | solution.py:525
  19.6 2.4 %collective-permute-done.3.refs_1_ = bf16[4,32,16,128]{3,2,1,0:T(8,128)(2,1)} collective-permute-done((bf16[4,32,16,128]{3,2,1,0:T(8,128)(2,1)S(1)}, bf16[4,32,16,128]{3,2,1,0:T(8,128)(2,1)}, u32[]{:S(2)}, u32[]{:S(2)}) %collective-permute-start.3) | collective-permute-done | bytes 524320 | tf_op jit(solution)/shard_map/ppermute | solution.py:525
  22.0 0.0 collective-permute-start.4
  22.0 0.9 %collective-permute-done.5.refs_3_.same = bf16[21,16,128]{2,1,0:T(8,128)(2,1)S(1)} collective-permute-done((bf16[21,16,128]{2,1,0:T(8,128)(2,1)S(1)}, bf16[21,16,128]{2,1,0:T(8,128)(2,1)S(1)}, u32[]{:S(2)}, u32[]{:S(2)}) %collective-permute-start.5) | collective-permute-done | bytes 86048 | tf_op jit(solution)/shard_map/ppermute | solution.py:525
  22.9 0.0 collective-permute-done.6.refs_4_.cross
  22.9 6.7 %collective-permute-start.9 = (bf16[4,8,128,128]{3,2,1,0:T(8,128)(2,1)}, bf16[4,8,128,128]{3,2,1,0:T(8,128)(2,1)S(1)}, u32[]{:S(2)}, u32[]{:S(2)}) collective-permute-start(bf16[4,8,128,128]{3,2,1,0:T(8,128)(2,1)} %get-tuple-element.47), channel_id=1, source_target_pairs={{0,8},{2,10},{4,12},{6,14},{8,16},{9,1},{10,18},{11,3},{12,20},{13... | collective-permute-start | bytes 3145736 | tf_op jit(solution)/shard_map/ppermute | solution.py:525
  29.6 0.1 collective-permute-start
  29.7 0.7 %slice_bitcast_fusion = bf16[16,128]{1,0:T(8,128)(2,1)S(1)} fusion(bf16[21,128,128]{2,1,0:T(8,128)(2,1)} %collective-permute-done.1.refs_0_), kind=kLoop, calls=%fused_computation.17 | loop fusion | bytes 8192 | tf_op jit(solution)/shard_map/squeeze | solution.py:547
  30.4 0.5 collective-permute-start.7
  30.9 0.1 concatenate.3.target
  31.0 4.4 %load.1 = (f32[24,160,128]{2,1,0:T(8,128)S(1)}, f32[24,160,128]{2,1,0:T(8,128)S(1)}, f32[24,160,128]{2,1,0:T(8,128)S(1)}, f32[24,160,128]{2,1,0:T(8,128)S(1)}, f...) custom-call(s32[1028]{0:T(1024)S(1)} %concatenate.3.target, ...), custom_call_target="tpu_custom_call" | custom-call | tf_op jit(solution)/shard_map/load/pallas_call | solution.py:220
  35.4 0.0 collective-permute-done.7.refs_7_
  35.4 11.8 %wave.1 = (f32[16,128,128]{2,1,0:T(8,128)S(1)}, f32[16,128,128]{2,1,0:T(8,128)S(1)}, f32[16,128,128]{2,1,0:T(8,128)S(1)}, f32[16,128,128]{2,1,0:T(8,128)S(1)}, f...) custom-call(s32[2064]{0:T(1024)S(1)} %get-tuple-element.32.ints, ...), custom_call_target="tpu_custom_call", output_to_operand_aliasing={{5}: (10, {}), {6}: (11, {}), {7}: (12, {}), {8}: (13, {}),... | custom-call | tf_op jit(solution)/shard_map/wave/pallas_call | solution.py:374
  47.3 0.4 collective-permute-start.12
  47.6 0.2 collective-permute-start.11
  47.8 0.3 collective-permute-start.8
  48.1 1.3 %rim_image.1 = (f32[16,128,128]{2,1,0:T(8,128)S(1)}, f32[8,128,128]{2,1,0:T(8,128)S(1)}) custom-call(s32[1,2]{1,0:T(1,128)S(1)} %copy-done.1, s32[1,2]{1,0:T(1,128)S(1)} %collective-permute-done.offs_other, bf16[4,8,128,128]{3,2,1,0:T(8,128)(2,1)S(1)} %collective-permute-done.9.xs, ...), custom_call_target="tpu_custom_call", output_to_operand_aliasing={{0}: (6, {})} | custom-call | tf_op jit(solution)/shard_map/rim_image/pallas_call | solution.py:453
  49.4 0.1 collective-permute-start.10
  49.5 0.5 collective-permute-done.12.q_other
  50.0 1.5 %collective-permute-done.11.p_other = f32[16,128,128]{2,1,0:T(8,128)S(1)} collective-permute-done((f32[16,128,128]{2,1,0:T(8,128)S(1)}, f32[16,128,128]{2,1,0:T(8,128)S(1)}, u32[]{:S(2)}, u32[]{:S(2)}) %collective-permute-start.11) | collective-permute-done | bytes 1048608 | tf_op jit(solution)/shard_map/ppermute | solution.py:511
  51.5 2.4 %merge.1 = (f32[32,128,128]{2,1,0:T(8,128)}, f32[32,128,128]{2,1,0:T(8,128)}, f32[32,128,128]{2,1,0:T(8,128)}) custom-call(f32[16,128,128]{2,1,0:T(8,128)S(1)} %get-tuple-element.48.p_own, f32[16,128,128]{2,1,0:T(8,128)S(1)} %collective-permute-done.11.p_other, f32[16,128,128]{2,1,0:T(8,128)S(1)} %get-tuple-element.53.q_own, ...), custom_call_target="tpu_custom_call" | custom-call | tf_op jit(solution)/shard_map/merge/pallas_call | solution.py:408
  53.9 0.0 collective-permute-done.10.given
  53.9 1.5 %place_image.1 = (f32[32,128,128]{2,1,0:T(8,128)}, f32[16,128,128]{2,1,0:T(8,128)S(1)}) custom-call(s32[1,2]{1,0:T(1,128)S(1)} %copy-done.1, f32[16,128,128]{2,1,0:T(8,128)S(1)} %collective-permute-done.8._, f32[8,128,128]{2,1,0:T(8,128)S(1)} %collective-permute-done.10.given, ...), custom_call_target="tpu_custom_call", output_to_operand_aliasing={{1}: (1, {}), {0}: (3, {})} | custom-call | tf_op jit(solution)/shard_map/place_image/pallas_call | solution.py:492
  (10 shorter events, 0.0 us)
Async XLA Ops:
  0.6 8.3 %collective-permute-start.2 = (bf16[2,32,128,128]{3,2,1,0:T(8,128)(2,1)}, bf16[2,32,128,128]{3,2,1,0:T(8,128)(2,1)S(1)}, u32[]{:S(2)}, u32[]{:S(2)}) collective-permute-start(bf16[2,32,128,128]{3,2,1,0:T(8,128)(2,1)} %refs_5_.7), channel_id=1, source_target_pairs={{0,1},{1,0},{2,3},{3,2},{4,5},{5,4},{6,7},{7,6},{8,9},{9,8},{10,11... | collective-permute-start | bytes 6291464 | tf_op jit(solution)/shard_map/ppermute | solution.py:511
  3.6 26.0 %copy-start.1 = (s32[1,2]{1,0:T(1,128)S(1)}, s32[1,2]{1,0:T(1,128)}, u32[]{:S(2)}) copy-start(s32[1,2]{1,0:T(1,128)} %offs.3) | copy-start | bytes 28
  3.6 27.2 %copy-start.2 = (s32[1024]{0:T(1024)S(1)}, s32[1024]{0:T(1024)}, u32[]{:S(2)}) copy-start(s32[1024]{0:T(1024)} %param.21) | copy-start | bytes 12292
  3.7 26.1 %collective-permute-start.1 = (bf16[21,128,128]{2,1,0:T(8,128)(2,1)}, bf16[21,128,128]{2,1,0:T(8,128)(2,1)}, u32[]{:S(2)}, u32[]{:S(2)}) collective-permute-start(bf16[21,128,128]{2,1,0:T(8,128)(2,1)} %pack_x.1), channel_id=1, source_target_pairs={{0,8},{2,10},{4,12},{6,14},{8,16},{9,1},{10,18},{11,3},{12,20},{13... | collective-permute-start | bytes 2064392 | tf_op jit(solution)/shard_map/ppermute | solution.py:525
  11.8 10.2 %collective-permute-start.3 = (bf16[4,32,16,128]{3,2,1,0:T(8,128)(2,1)S(1)}, bf16[4,32,16,128]{3,2,1,0:T(8,128)(2,1)}, u32[]{:S(2)}, u32[]{:S(2)}) collective-permute-start(bf16[4,32,16,128]{3,2,1,0:T(8,128)(2,1)S(1)} %get-tuple-element.34), channel_id=1, source_target_pairs={{0,2},{2,4},{3,1},{4,6},{5,3},{7,5},{8,10},{10,12},{11,9},{12,14},... | collective-permute-start | bytes 1572872 | tf_op jit(solution)/shard_map/ppermute | solution.py:525
  16.1 6.8 %collective-permute-start.5 = (bf16[21,16,128]{2,1,0:T(8,128)(2,1)S(1)}, bf16[21,16,128]{2,1,0:T(8,128)(2,1)S(1)}, u32[]{:S(2)}, u32[]{:S(2)}) collective-permute-start(bf16[21,16,128]{2,1,0:T(8,128)(2,1)S(1)} %get-tuple-element.35), channel_id=1, source_target_pairs={{0,10},{2,12},{4,14},{8,18},{10,20},{11,1},{12,22},{13,3},{15,5},{... | collective-permute-start | bytes 258056 | tf_op jit(solution)/shard_map/ppermute | solution.py:525
  18.9 4.0 %collective-permute-start.6 = (bf16[21,16,128]{2,1,0:T(8,128)(2,1)S(1)}, bf16[21,16,128]{2,1,0:T(8,128)(2,1)S(1)}, u32[]{:S(2)}, u32[]{:S(2)}) collective-permute-start(bf16[21,16,128]{2,1,0:T(8,128)(2,1)S(1)} %get-tuple-element.36), channel_id=1, source_target_pairs={{2,8},{4,10},{6,12},{9,3},{10,16},{11,5},{12,18},{13,7},{14,20},{1... | collective-permute-start | bytes 258056 | tf_op jit(solution)/shard_map/ppermute | solution.py:525
  22.0 13.4 %collective-permute-start.4 = (bf16[4,32,16,128]{3,2,1,0:T(8,128)(2,1)}, bf16[4,32,16,128]{3,2,1,0:T(8,128)(2,1)}, u32[]{:S(2)}, u32[]{:S(2)}) collective-permute-start(bf16[4,32,16,128]{3,2,1,0:T(8,128)(2,1)} %collective-permute-done.3.refs_1_), channel_id=1, source_target_pairs={{0,1},{1,0},{2,3},{3,2},{4,5},{5,4},{6,7},{7,6},{8,9},{9,8},{10,11... | collective-permute-start | bytes 1572872 | tf_op jit(solution)/shard_map/ppermute | solution.py:511
  22.9 25.2 %collective-permute-start.9 = (bf16[4,8,128,128]{3,2,1,0:T(8,128)(2,1)}, bf16[4,8,128,128]{3,2,1,0:T(8,128)(2,1)S(1)}, u32[]{:S(2)}, u32[]{:S(2)}) collective-permute-start(bf16[4,8,128,128]{3,2,1,0:T(8,128)(2,1)} %get-tuple-element.47), channel_id=1, source_target_pairs={{0,8},{2,10},{4,12},{6,14},{8,16},{9,1},{10,18},{11,3},{12,20},{13... | collective-permute-start | bytes 3145736 | tf_op jit(solution)/shard_map/ppermute | solution.py:525
  29.6 1.3 %collective-permute-start = (s32[1,2]{1,0:T(1,128)S(1)}, s32[1,2]{1,0:T(1,128)S(1)}, u32[]{:S(2)}, u32[]{:S(2)}) collective-permute-start(s32[1,2]{1,0:T(1,128)S(1)} %copy-done.1), channel_id=1, source_target_pairs={{0,1},{1,0},{2,3},{3,2},{4,5},{5,4},{6,7},{7,6},{8,9},{9,8},{10,11... | collective-permute-start | bytes 32 | tf_op jit(solution)/shard_map/ppermute | solution.py:511
  30.4 5.0 %collective-permute-start.7 = (bf16[16,128]{1,0:T(8,128)(2,1)S(1)}, bf16[16,128]{1,0:T(8,128)(2,1)S(1)}, u32[]{:S(2)}, u32[]{:S(2)}) collective-permute-start(bf16[16,128]{1,0:T(8,128)(2,1)S(1)} %slice_bitcast_fusion), channel_id=1, source_target_pairs={{0,1},{1,0},{2,3},{3,2},{4,5},{5,4},{6,7},{7,6},{8,9},{9,8},{10,11... | collective-permute-start | bytes 12296 | tf_op jit(solution)/shard_map/ppermute | solution.py:511
  31.0 4.4 %copy-start = (f32[4,1024]{1,0:T(4,128)S(1)}, f32[4,1024]{1,0:T(4,128)}, u32[]{:S(2)}) copy-start(f32[4,1024]{1,0:T(4,128)} %amounts.1) | copy-start | bytes 49156
  47.3 2.7 %collective-permute-start.12 = (f32[16,128,128]{2,1,0:T(8,128)S(1)}, f32[16,128,128]{2,1,0:T(8,128)S(1)}, u32[]{:S(2)}, u32[]{:S(2)}) collective-permute-start(f32[16,128,128]{2,1,0:T(8,128)S(1)} %get-tuple-element.53.q_own), channel_id=1, source_target_pairs={{0,1},{1,0},{2,3},{3,2},{4,5},{5,4},{6,7},{7,6},{8,9},{9,8},{10,11... | collective-permute-start | bytes 3145736 | tf_op jit(solution)/shard_map/ppermute | solution.py:511
  47.6 3.9 %collective-permute-start.11 = (f32[16,128,128]{2,1,0:T(8,128)S(1)}, f32[16,128,128]{2,1,0:T(8,128)S(1)}, u32[]{:S(2)}, u32[]{:S(2)}) collective-permute-start(f32[16,128,128]{2,1,0:T(8,128)S(1)} %get-tuple-element.48.p_own), channel_id=1, source_target_pairs={{0,1},{1,0},{2,3},{3,2},{4,5},{5,4},{6,7},{7,6},{8,9},{9,8},{10,11... | collective-permute-start | bytes 3145736 | tf_op jit(solution)/shard_map/ppermute | solution.py:511
  47.8 6.1 %collective-permute-start.8 = (f32[16,128,128]{2,1,0:T(8,128)S(1)}, f32[16,128,128]{2,1,0:T(8,128)S(1)}, u32[]{:S(2)}, u32[]{:S(2)}) collective-permute-start(f32[16,128,128]{2,1,0:T(8,128)S(1)} %get-tuple-element.45), channel_id=1, source_target_pairs={{0,1},{1,0},{2,3},{3,2},{4,5},{5,4},{6,7},{7,6},{8,9},{9,8},{10,11... | collective-permute-start | bytes 3145736 | tf_op jit(solution)/shard_map/ppermute | solution.py:511
  49.4 4.5 %collective-permute-start.10 = (f32[8,128,128]{2,1,0:T(8,128)S(1)}, f32[8,128,128]{2,1,0:T(8,128)S(1)}, u32[]{:S(2)}, u32[]{:S(2)}) collective-permute-start(f32[8,128,128]{2,1,0:T(8,128)S(1)} %get-tuple-element.52._), channel_id=1, source_target_pairs={{0,1},{1,0},{2,3},{3,2},{4,5},{5,4},{6,7},{7,6},{8,9},{9,8},{10,11... | collective-permute-start | bytes 1572872 | tf_op jit(solution)/shard_map/ppermute | solution.py:511

commit v8 on v7

--- a/solution.py
+++ b/solution.py
@@ -11,7 +11,7 @@
 HMAX = 8
 DEEP = NT
 ROW0 = 16
-GROUP = 4
+GROUP = 8
 CORNER = (DEEP - 1, DEEP - 2)
 HEAD = 8
 F32 = jnp.float32
@@ -199,7 +199,7 @@
         listed[at + n + GROUP] = place
         return at + jnp.where(place >= 0, 1, 0)
 
-    end = lax.fori_loop(0, n, one, jnp.int32(HEAD), unroll=16)
+    end = lax.fori_loop(0, n, one, jnp.int32(HEAD), unroll=32)
     for i in range(GROUP):
         listed[end + i] = 0
         listed[end + i + n + GROUP] = 0

time: 55.9 us -> 55.7 us (level)
  no operation moved by 1% of the time
where the time goes in v8:
time: 55.7 us; the launch traced here: 55.4 us
  Pallas kernels  26.5 us (48%)
  starting transfers between devices  21.8 us (39%)
  waiting for transfers between devices  5.57 us (10%)
  between operations  0.81 us (1%)
  local copies, waits for them, and re-layouts  0.77 us (1%)
    ppermute x5, starting transfers between devices, outward(): return lax.ppermute(v, ('gx', 'gy', 'mem'), pairs)  19.7 us
    pallas_call x1, Pallas kernels, wave(): pl.pallas_call(wave_kernel, out_shape=(*(pltpu.VMEM((half, rows, depth),...  12 us
    pallas_call x1, Pallas kernels, load(): pl.pallas_call(load_kernel, out_shape=(pltpu.VMEM(shape, F32),) * 8 + (ja...  4.22 us
    ppermute x5, waiting for transfers between devices, outward(): return lax.ppermute(v, ('gx', 'gy', 'mem'), pairs)  3.36 us
    pallas_call x1, Pallas kernels, pack_rest(): pl.pallas_call(pack_rest_kernel, out_shape=(pltpu.VMEM((4, width, 16, dep...  2.84 us
    pallas_call x1, Pallas kernels, pack_x(): pl.pallas_call(pack_x_kernel, out_shape=pltpu.VMEM((LAYERS,) + shape, BF1...  2.48 us
    pallas_call x1, Pallas kernels, merge(): pl.pallas_call(merge_kernel, out_shape=(jax.ShapeDtypeStruct((2 * half, r...  2.39 us
    ppermute x8, waiting for transfers between devices, swap(): return lax.ppermute(v, 'mem', [(0, 1), (1, 0)])  2.22 us
  transfers between devices with their start and end apart: 13, of which 4 were waited for; matrix products, arithmetic and copies ran while one was open for 1% of the time, Pallas kernels for 45%

profile of v8, /device:TPU:0, one launch (start us, length us, event | category | flops | bytes accessed | tf_op | source)
XLA Modules:
  0.0 55.4 jit_solution(12456133309781284652)
XLA Ops:
  0.6 0.5 collective-permute-start.2
  1.1 2.5 %pack_x.1 = bf16[21,128,128]{2,1,0:T(8,128)(2,1)} custom-call(f32[32,128,128]{2,1,0:T(8,128)} %refs_0_.5, f32[32,128,128]{2,1,0:T(8,128)} %refs_1_.5, f32[32,128,128]{2,1,0:T(8,128)} %refs_2_.5, f32[32,128,128]{2,1,0:T(8,128)} %refs_3_.5, f32[32,128,128]{2,1,0:T(8,128)} %refs_4_.5, f32[32,128,128]{2,1,0:T(8,128)} %refs_5_.6, f32[32,128,128]{2,1,0:T(8,128)} %refs_6_.5, ...), custom_call_target="tpu_custom_call" | custom-call | tf_op jit(solution)/shard_map/pack_x/pallas_call | solution.py:89
  3.6 0.0 copy-start.1
  3.6 0.0 copy-start.2
  3.7 5.3 %collective-permute-start.1 = (bf16[21,128,128]{2,1,0:T(8,128)(2,1)}, bf16[21,128,128]{2,1,0:T(8,128)(2,1)}, u32[]{:S(2)}, u32[]{:S(2)}) collective-permute-start(bf16[21,128,128]{2,1,0:T(8,128)(2,1)} %pack_x.1), channel_id=1, source_target_pairs={{0,8},{2,10},{4,12},{6,14},{8,16},{9,1},{10,18},{11,3},{12,20},{13... | collective-permute-start | bytes 2064392 | tf_op jit(solution)/shard_map/ppermute | solution.py:525
  9.0 0.0 collective-permute-done.2.refs_9_.refs_6_
  9.0 2.8 %pack_rest.1 = (bf16[4,32,16,128]{3,2,1,0:T(8,128)(2,1)S(1)}, bf16[21,16,128]{2,1,0:T(8,128)(2,1)S(1)}, bf16[21,16,128]{2,1,0:T(8,128)(2,1)S(1)}, bf16[4,8,128,128]{3,2,1,0:T(8,128)(2,1)}) custom-call(f32[32,128,128]{2,1,0:T(8,128)} %refs_0_.5, f32[32,128,128]{2,1,0:T(8,128)} %refs_1_.5, f32[32,128,128]{2,1,0:T(8,128)} %refs_2_.5, f32[32,128,128]{2,1,0:T(8,128)} %refs_3_.5, ...), custom_call_target="tpu_custom_call" | custom-call | tf_op jit(solution)/shard_map/pack_rest/pallas_call | solution.py:158
  11.8 4.3 %collective-permute-start.3 = (bf16[4,32,16,128]{3,2,1,0:T(8,128)(2,1)S(1)}, bf16[4,32,16,128]{3,2,1,0:T(8,128)(2,1)}, u32[]{:S(2)}, u32[]{:S(2)}) collective-permute-start(bf16[4,32,16,128]{3,2,1,0:T(8,128)(2,1)S(1)} %get-tuple-element.34), channel_id=1, source_target_pairs={{0,2},{2,4},{3,1},{4,6},{5,3},{7,5},{8,10},{10,12},{11,9},{12,14},... | collective-permute-start | bytes 1572872 | tf_op jit(solution)/shard_map/ppermute | solution.py:525
  16.1 2.8 %collective-permute-start.5 = (bf16[21,16,128]{2,1,0:T(8,128)(2,1)S(1)}, bf16[21,16,128]{2,1,0:T(8,128)(2,1)S(1)}, u32[]{:S(2)}, u32[]{:S(2)}) collective-permute-start(bf16[21,16,128]{2,1,0:T(8,128)(2,1)S(1)} %get-tuple-element.35), channel_id=1, source_target_pairs={{0,10},{2,12},{4,14},{8,18},{10,20},{11,1},{12,22},{13,3},{15,5},{... | collective-permute-start | bytes 258056 | tf_op jit(solution)/shard_map/ppermute | solution.py:525
  18.9 0.7 %collective-permute-start.6 = (bf16[21,16,128]{2,1,0:T(8,128)(2,1)S(1)}, bf16[21,16,128]{2,1,0:T(8,128)(2,1)S(1)}, u32[]{:S(2)}, u32[]{:S(2)}) collective-permute-start(bf16[21,16,128]{2,1,0:T(8,128)(2,1)S(1)} %get-tuple-element.36), channel_id=1, source_target_pairs={{2,8},{4,10},{6,12},{9,3},{10,16},{11,5},{12,18},{13,7},{14,20},{1... | collective-permute-start | bytes 258056 | tf_op jit(solution)/shard_map/ppermute | solution.py:525
  19.6 2.4 %collective-permute-done.3.refs_1_ = bf16[4,32,16,128]{3,2,1,0:T(8,128)(2,1)} collective-permute-done((bf16[4,32,16,128]{3,2,1,0:T(8,128)(2,1)S(1)}, bf16[4,32,16,128]{3,2,1,0:T(8,128)(2,1)}, u32[]{:S(2)}, u32[]{:S(2)}) %collective-permute-start.3) | collective-permute-done | bytes 524320 | tf_op jit(solution)/shard_map/ppermute | solution.py:525
  22.0 0.0 collective-permute-start.4
  22.0 0.9 %collective-permute-done.5.refs_3_.same = bf16[21,16,128]{2,1,0:T(8,128)(2,1)S(1)} collective-permute-done((bf16[21,16,128]{2,1,0:T(8,128)(2,1)S(1)}, bf16[21,16,128]{2,1,0:T(8,128)(2,1)S(1)}, u32[]{:S(2)}, u32[]{:S(2)}) %collective-permute-start.5) | collective-permute-done | bytes 86048 | tf_op jit(solution)/shard_map/ppermute | solution.py:525
  22.9 0.0 collective-permute-done.6.refs_4_.cross
  22.9 6.7 %collective-permute-start.9 = (bf16[4,8,128,128]{3,2,1,0:T(8,128)(2,1)}, bf16[4,8,128,128]{3,2,1,0:T(8,128)(2,1)S(1)}, u32[]{:S(2)}, u32[]{:S(2)}) collective-permute-start(bf16[4,8,128,128]{3,2,1,0:T(8,128)(2,1)} %get-tuple-element.47), channel_id=1, source_target_pairs={{0,8},{2,10},{4,12},{6,14},{8,16},{9,1},{10,18},{11,3},{12,20},{13... | collective-permute-start | bytes 3145736 | tf_op jit(solution)/shard_map/ppermute | solution.py:525
  29.6 0.1 collective-permute-start
  29.7 0.0 collective-permute-done.1.refs_0_
  29.7 0.7 %slice_bitcast_fusion = bf16[16,128]{1,0:T(8,128)(2,1)S(1)} fusion(bf16[21,128,128]{2,1,0:T(8,128)(2,1)} %collective-permute-done.1.refs_0_), kind=kLoop, calls=%fused_computation.17 | loop fusion | bytes 8192 | tf_op jit(solution)/shard_map/squeeze | solution.py:547
  30.4 0.5 collective-permute-start.7
  30.9 0.0 collective-permute-done.offs_other
  30.9 0.1 concatenate.3.target
  31.0 4.2 %load.1 = (f32[24,160,128]{2,1,0:T(8,128)S(1)}, f32[24,160,128]{2,1,0:T(8,128)S(1)}, f32[24,160,128]{2,1,0:T(8,128)S(1)}, f32[24,160,128]{2,1,0:T(8,128)S(1)}, f...) custom-call(s32[1028]{0:T(1024)S(1)} %concatenate.3.target, ...), custom_call_target="tpu_custom_call" | custom-call | tf_op jit(solution)/shard_map/load/pallas_call | solution.py:220
  35.3 12.0 %wave.1 = (f32[16,128,128]{2,1,0:T(8,128)S(1)}, f32[16,128,128]{2,1,0:T(8,128)S(1)}, f32[16,128,128]{2,1,0:T(8,128)S(1)}, f32[16,128,128]{2,1,0:T(8,128)S(1)}, f...) custom-call(s32[2072]{0:T(1024)S(1)} %get-tuple-element.32.ints, ...), custom_call_target="tpu_custom_call", output_to_operand_aliasing={{5}: (10, {}), {6}: (11, {}), {7}: (12, {}), {8}: (13, {}),... | custom-call | tf_op jit(solution)/shard_map/wave/pallas_call | solution.py:374
  47.2 0.1 collective-permute-start.12
  47.3 0.5 collective-permute-start.11
  47.8 0.1 collective-permute-start.8
  47.9 1.0 %rim_image.1 = (f32[16,128,128]{2,1,0:T(8,128)S(1)}, f32[8,128,128]{2,1,0:T(8,128)S(1)}) custom-call(s32[1,2]{1,0:T(1,128)S(1)} %copy-done.1, s32[1,2]{1,0:T(1,128)S(1)} %collective-permute-done.offs_other, bf16[4,8,128,128]{3,2,1,0:T(8,128)(2,1)S(1)} %collective-permute-done.9.xs, ...), custom_call_target="tpu_custom_call", output_to_operand_aliasing={{0}: (6, {})} | custom-call | tf_op jit(solution)/shard_map/rim_image/pallas_call | solution.py:453
  48.9 0.3 collective-permute-start.10
  49.3 0.7 %collective-permute-done.12.q_other = f32[16,128,128]{2,1,0:T(8,128)S(1)} collective-permute-done((f32[16,128,128]{2,1,0:T(8,128)S(1)}, f32[16,128,128]{2,1,0:T(8,128)S(1)}, u32[]{:S(2)}, u32[]{:S(2)}) %collective-permute-start.12) | collective-permute-done | bytes 1048608 | tf_op jit(solution)/shard_map/ppermute | solution.py:511
  50.0 1.5 %collective-permute-done.11.p_other = f32[16,128,128]{2,1,0:T(8,128)S(1)} collective-permute-done((f32[16,128,128]{2,1,0:T(8,128)S(1)}, f32[16,128,128]{2,1,0:T(8,128)S(1)}, u32[]{:S(2)}, u32[]{:S(2)}) %collective-permute-start.11) | collective-permute-done | bytes 1048608 | tf_op jit(solution)/shard_map/ppermute | solution.py:511
  51.5 2.4 %merge.1 = (f32[32,128,128]{2,1,0:T(8,128)}, f32[32,128,128]{2,1,0:T(8,128)}, f32[32,128,128]{2,1,0:T(8,128)}) custom-call(f32[16,128,128]{2,1,0:T(8,128)S(1)} %get-tuple-element.48.p_own, f32[16,128,128]{2,1,0:T(8,128)S(1)} %collective-permute-done.11.p_other, f32[16,128,128]{2,1,0:T(8,128)S(1)} %get-tuple-element.53.q_own, ...), custom_call_target="tpu_custom_call" | custom-call | tf_op jit(solution)/shard_map/merge/pallas_call | solution.py:408
  53.9 1.5 %place_image.1 = (f32[32,128,128]{2,1,0:T(8,128)}, f32[16,128,128]{2,1,0:T(8,128)S(1)}) custom-call(s32[1,2]{1,0:T(1,128)S(1)} %copy-done.1, f32[16,128,128]{2,1,0:T(8,128)S(1)} %collective-permute-done.8._, f32[8,128,128]{2,1,0:T(8,128)S(1)} %collective-permute-done.10.given, ...), custom_call_target="tpu_custom_call", output_to_operand_aliasing={{1}: (1, {}), {0}: (3, {})} | custom-call | tf_op jit(solution)/shard_map/place_image/pallas_call | solution.py:492
  (10 shorter events, 0.0 us)
Async XLA Ops:
  0.6 8.3 %collective-permute-start.2 = (bf16[2,32,128,128]{3,2,1,0:T(8,128)(2,1)}, bf16[2,32,128,128]{3,2,1,0:T(8,128)(2,1)S(1)}, u32[]{:S(2)}, u32[]{:S(2)}) collective-permute-start(bf16[2,32,128,128]{3,2,1,0:T(8,128)(2,1)} %refs_5_.7), channel_id=1, source_target_pairs={{0,1},{1,0},{2,3},{3,2},{4,5},{5,4},{6,7},{7,6},{8,9},{9,8},{10,11... | collective-permute-start | bytes 6291464 | tf_op jit(solution)/shard_map/ppermute | solution.py:511
  3.6 26.0 %copy-start.1 = (s32[1,2]{1,0:T(1,128)S(1)}, s32[1,2]{1,0:T(1,128)}, u32[]{:S(2)}) copy-start(s32[1,2]{1,0:T(1,128)} %offs.3) | copy-start | bytes 28
  3.6 27.2 %copy-start.2 = (s32[1024]{0:T(1024)S(1)}, s32[1024]{0:T(1024)}, u32[]{:S(2)}) copy-start(s32[1024]{0:T(1024)} %param.21) | copy-start | bytes 12292
  3.7 26.1 %collective-permute-start.1 = (bf16[21,128,128]{2,1,0:T(8,128)(2,1)}, bf16[21,128,128]{2,1,0:T(8,128)(2,1)}, u32[]{:S(2)}, u32[]{:S(2)}) collective-permute-start(bf16[21,128,128]{2,1,0:T(8,128)(2,1)} %pack_x.1), channel_id=1, source_target_pairs={{0,8},{2,10},{4,12},{6,14},{8,16},{9,1},{10,18},{11,3},{12,20},{13... | collective-permute-start | bytes 2064392 | tf_op jit(solution)/shard_map/ppermute | solution.py:525
  11.8 10.2 %collective-permute-start.3 = (bf16[4,32,16,128]{3,2,1,0:T(8,128)(2,1)S(1)}, bf16[4,32,16,128]{3,2,1,0:T(8,128)(2,1)}, u32[]{:S(2)}, u32[]{:S(2)}) collective-permute-start(bf16[4,32,16,128]{3,2,1,0:T(8,128)(2,1)S(1)} %get-tuple-element.34), channel_id=1, source_target_pairs={{0,2},{2,4},{3,1},{4,6},{5,3},{7,5},{8,10},{10,12},{11,9},{12,14},... | collective-permute-start | bytes 1572872 | tf_op jit(solution)/shard_map/ppermute | solution.py:525
  16.1 6.8 %collective-permute-start.5 = (bf16[21,16,128]{2,1,0:T(8,128)(2,1)S(1)}, bf16[21,16,128]{2,1,0:T(8,128)(2,1)S(1)}, u32[]{:S(2)}, u32[]{:S(2)}) collective-permute-start(bf16[21,16,128]{2,1,0:T(8,128)(2,1)S(1)} %get-tuple-element.35), channel_id=1, source_target_pairs={{0,10},{2,12},{4,14},{8,18},{10,20},{11,1},{12,22},{13,3},{15,5},{... | collective-permute-start | bytes 258056 | tf_op jit(solution)/shard_map/ppermute | solution.py:525
  18.9 4.0 %collective-permute-start.6 = (bf16[21,16,128]{2,1,0:T(8,128)(2,1)S(1)}, bf16[21,16,128]{2,1,0:T(8,128)(2,1)S(1)}, u32[]{:S(2)}, u32[]{:S(2)}) collective-permute-start(bf16[21,16,128]{2,1,0:T(8,128)(2,1)S(1)} %get-tuple-element.36), channel_id=1, source_target_pairs={{2,8},{4,10},{6,12},{9,3},{10,16},{11,5},{12,18},{13,7},{14,20},{1... | collective-permute-start | bytes 258056 | tf_op jit(solution)/shard_map/ppermute | solution.py:525
  22.0 13.3 %collective-permute-start.4 = (bf16[4,32,16,128]{3,2,1,0:T(8,128)(2,1)}, bf16[4,32,16,128]{3,2,1,0:T(8,128)(2,1)}, u32[]{:S(2)}, u32[]{:S(2)}) collective-permute-start(bf16[4,32,16,128]{3,2,1,0:T(8,128)(2,1)} %collective-permute-done.3.refs_1_), channel_id=1, source_target_pairs={{0,1},{1,0},{2,3},{3,2},{4,5},{5,4},{6,7},{7,6},{8,9},{9,8},{10,11... | collective-permute-start | bytes 1572872 | tf_op jit(solution)/shard_map/ppermute | solution.py:511
  22.9 25.0 %collective-permute-start.9 = (bf16[4,8,128,128]{3,2,1,0:T(8,128)(2,1)}, bf16[4,8,128,128]{3,2,1,0:T(8,128)(2,1)S(1)}, u32[]{:S(2)}, u32[]{:S(2)}) collective-permute-start(bf16[4,8,128,128]{3,2,1,0:T(8,128)(2,1)} %get-tuple-element.47), channel_id=1, source_target_pairs={{0,8},{2,10},{4,12},{6,14},{8,16},{9,1},{10,18},{11,3},{12,20},{13... | collective-permute-start | bytes 3145736 | tf_op jit(solution)/shard_map/ppermute | solution.py:525
  29.6 1.3 %collective-permute-start = (s32[1,2]{1,0:T(1,128)S(1)}, s32[1,2]{1,0:T(1,128)S(1)}, u32[]{:S(2)}, u32[]{:S(2)}) collective-permute-start(s32[1,2]{1,0:T(1,128)S(1)} %copy-done.1), channel_id=1, source_target_pairs={{0,1},{1,0},{2,3},{3,2},{4,5},{5,4},{6,7},{7,6},{8,9},{9,8},{10,11... | collective-permute-start | bytes 32 | tf_op jit(solution)/shard_map/ppermute | solution.py:511
  30.4 4.8 %collective-permute-start.7 = (bf16[16,128]{1,0:T(8,128)(2,1)S(1)}, bf16[16,128]{1,0:T(8,128)(2,1)S(1)}, u32[]{:S(2)}, u32[]{:S(2)}) collective-permute-start(bf16[16,128]{1,0:T(8,128)(2,1)S(1)} %slice_bitcast_fusion), channel_id=1, source_target_pairs={{0,1},{1,0},{2,3},{3,2},{4,5},{5,4},{6,7},{7,6},{8,9},{9,8},{10,11... | collective-permute-start | bytes 12296 | tf_op jit(solution)/shard_map/ppermute | solution.py:511
  31.0 4.3 %copy-start = (f32[4,1024]{1,0:T(4,128)S(1)}, f32[4,1024]{1,0:T(4,128)}, u32[]{:S(2)}) copy-start(f32[4,1024]{1,0:T(4,128)} %amounts.1) | copy-start | bytes 49156
  47.2 2.7 %collective-permute-start.12 = (f32[16,128,128]{2,1,0:T(8,128)S(1)}, f32[16,128,128]{2,1,0:T(8,128)S(1)}, u32[]{:S(2)}, u32[]{:S(2)}) collective-permute-start(f32[16,128,128]{2,1,0:T(8,128)S(1)} %get-tuple-element.53.q_own), channel_id=1, source_target_pairs={{0,1},{1,0},{2,3},{3,2},{4,5},{5,4},{6,7},{7,6},{8,9},{9,8},{10,11... | collective-permute-start | bytes 3145736 | tf_op jit(solution)/shard_map/ppermute | solution.py:511
  47.3 4.1 %collective-permute-start.11 = (f32[16,128,128]{2,1,0:T(8,128)S(1)}, f32[16,128,128]{2,1,0:T(8,128)S(1)}, u32[]{:S(2)}, u32[]{:S(2)}) collective-permute-start(f32[16,128,128]{2,1,0:T(8,128)S(1)} %get-tuple-element.48.p_own), channel_id=1, source_target_pairs={{0,1},{1,0},{2,3},{3,2},{4,5},{5,4},{6,7},{7,6},{8,9},{9,8},{10,11... | collective-permute-start | bytes 3145736 | tf_op jit(solution)/shard_map/ppermute | solution.py:511
  47.8 6.1 %collective-permute-start.8 = (f32[16,128,128]{2,1,0:T(8,128)S(1)}, f32[16,128,128]{2,1,0:T(8,128)S(1)}, u32[]{:S(2)}, u32[]{:S(2)}) collective-permute-start(f32[16,128,128]{2,1,0:T(8,128)S(1)} %get-tuple-element.45), channel_id=1, source_target_pairs={{0,1},{1,0},{2,3},{3,2},{4,5},{5,4},{6,7},{7,6},{8,9},{9,8},{10,11... | collective-permute-start | bytes 3145736 | tf_op jit(solution)/shard_map/ppermute | solution.py:511
  48.9 4.9 %collective-permute-start.10 = (f32[8,128,128]{2,1,0:T(8,128)S(1)}, f32[8,128,128]{2,1,0:T(8,128)S(1)}, u32[]{:S(2)}, u32[]{:S(2)}) collective-permute-start(f32[8,128,128]{2,1,0:T(8,128)S(1)} %get-tuple-element.52._), channel_id=1, source_target_pairs={{0,1},{1,0},{2,3},{3,2},{4,5},{5,4},{6,7},{7,6},{8,9},{9,8},{10,11... | collective-permute-start | bytes 1572872 | tf_op jit(solution)/shard_map/ppermute | solution.py:511
